TPU v7x, 128 devices: a whole 4x4x4 slice. The times are simulated.
128 devices in a mesh: shard: 4 (over y), context: 16 (over x, z), tensor: 2 (over core).
Axes of the slice: x: 4, y: 4, z: 4, core: 2. Of those that a mesh axis runs over, the one named last changes fastest.
Arguments:
- tokens: bfloat16 [4, 2560, 2560], P('shard', 'context'), may hold values from -6 to 6
- lengths: int32 [4], P('shard'), may hold values from 1024 to 2560, as said below
- attn_gain: bfloat16 [2560], P(('shard', 'context')), may hold values from 0.5 to 1.5
- w_query: bfloat16 [2560, 2560], P(('shard', 'context'), 'tensor'), may hold values from -0.25 to 0.25
- w_keyval: bfloat16 [2560, 512], P(('shard', 'context')), may hold values from -0.125 to 0.125
- w_output: bfloat16 [2560, 2560], P(('shard', 'context'), 'tensor'), may hold values from -0.625 to 0.625
- mlp_gain: bfloat16 [2560], P(('shard', 'context')), may hold values from 0.5 to 1.5
- w_gate: bfloat16 [2560, 7680], P(('shard', 'context'), 'tensor'), may hold values from -0.125 to 0.125
- w_up: bfloat16 [2560, 7680], P(('shard', 'context'), 'tensor'), may hold values from -0.125 to 0.125
- w_down: bfloat16 [2560, 7680], P(('shard', 'context'), 'tensor'), may hold values from -0.0625 to 0.0625
- cotangent: bfloat16 [4, 2560, 2560], P('shard', 'context'), may hold values from -6 to 6
Outputs:
- block_out: bfloat16 [4, 2560, 2560], P('shard', 'context')
- tokens_grad: bfloat16 [4, 2560, 2560], P('shard', 'context')
- attn_gain_grad: float32 [2560], P(('shard', 'context'))
- query_grad: float32 [2560, 2560], P(('shard', 'context'), 'tensor')
- keyval_grad: float32 [2560, 512], P(('shard', 'context'))
- output_grad: float32 [2560, 2560], P(('shard', 'context'), 'tensor')
- mlp_gain_grad: float32 [2560], P(('shard', 'context'))
- gate_grad: float32 [2560, 7680], P(('shard', 'context'), 'tensor')
- up_grad: float32 [2560, 7680], P(('shard', 'context'), 'tensor')
- down_grad: float32 [2560, 7680], P(('shard', 'context'), 'tensor')
Inputs may be any that keep to these rules, and one draw needn't show every extreme that they name: `lengths`: valid tokens fill the end of each slot; at least one of the 4 slots holds 2560 valid tokens.
All inputs are finite; a program needn't handle non-finite values.
Results may differ from a plain program's by a relative error of at most 0.02.
Values may be sent and summed in bfloat16 or wider, within the bound.
No kernel may reach another device: no remote copies, remote signals or barrier semaphores. Data moves between devices by JAX's collectives and lax.ppermute only.
A program may use at most 448 MiB of HBM per device.

v0:
```python
import jax
import jax.numpy as jnp
from jax import lax
from jax.sharding import Mesh
from jax.sharding import PartitionSpec as P

WINDOW = 2048
SHARD_CONTEXT = ("shard", "context_0", "context_1")
CONTEXT = ("context_0", "context_1")


EPSILON = 1e-06
NEGATIVE_FILL = -1e30


def in_one_piece(arrays, axis, dim, along):
    columns = [a.reshape(*a.shape[:along], -1) for a in arrays]
    both = jnp.concatenate(columns, axis=along)
    result, at, gathered = (lax.all_gather(both, axis, axis=dim, tiled=True), 0, [])
    for a, column in zip(arrays, columns):
        share = result[..., at : at + column.shape[along]]
        gathered.append(share.reshape(*share.shape[:along], *a.shape[along:]))
        at += column.shape[along]
    return tuple(gathered)


def copy_for_each(x, axis):
    peers = lax.axis_size(axis)
    return lax.all_to_all(jnp.broadcast_to(x[None], (peers, *x.shape)), axis, 0, 0, tiled=True)


def joined_along(blocks, dim):
    shape = list(blocks.shape[1:])
    shape[dim] *= blocks.shape[0]
    return jnp.moveaxis(blocks, 0, dim).reshape(shape)


def gather_directly(x, axis, dim):
    blocks = copy_for_each(x, axis)
    return joined_along(blocks, dim)


def over_copies(x, axis):
    return copy_for_each(x, axis).sum(axis=0)


def taken_together(x, axis):
    return copy_for_each(x, axis).astype(jnp.float32).sum(axis=0)


def summed_rows(x, axes, dim):
    if not axes:
        return x
    nearer = lax.psum_scatter(x, axes[0], scatter_dimension=dim, tiled=True)
    return summed_rows(nearer, axes[1:], dim)


def packed_total(arrays, axis):
    vector, at, gathered = (jnp.concatenate([a.reshape(-1) for a in arrays]), 0, [])
    subtotal = over_copies(vector, axis)
    for a in arrays:
        gathered.append(subtotal[at : at + a.size].reshape(a.shape))
        at += a.size
    return tuple(gathered)


def side_by_side(arrays, axis, dim, along):
    columns = [a.reshape(*a.shape[:along], -1) for a in arrays]
    both = jnp.concatenate(columns, axis=along)
    result, at, gathered = (lax.psum_scatter(both, axis, scatter_dimension=dim, tiled=True), 0, [])
    for a, column in zip(arrays, columns):
        share = result[..., at : at + column.shape[along]]
        gathered.append(share.reshape(*share.shape[:along], *a.shape[along:]))
        at += column.shape[along]
    return tuple(gathered)


def scaled_norm(values, gain_vec):
    inverse = lax.rsqrt(jnp.mean(values * values, axis=-1, keepdims=True) + EPSILON)
    return values * inverse * gain_vec


def angles(position, head_dim):
    quarter = head_dim // 4
    frequency = 10000.0 ** (-jnp.arange(quarter, dtype=jnp.float32) / quarter)
    phase_angle = position[:, None].astype(jnp.float32) * frequency[None, :]
    return (jnp.cos(phase_angle), jnp.sin(phase_angle))


def rotate(values, cosine, sine_part):
    quarter = cosine.shape[-1]
    first_half = values[..., :quarter]
    second = values[..., quarter : 2 * quarter]
    cos_rows = cosine[:, None, :]
    sin_rows = sine_part[:, None, :]
    return jnp.concatenate(
        [
            first_half * cos_rows - second * sin_rows,
            second * cos_rows + first_half * sin_rows,
            values[..., 2 * quarter :],
        ],
        axis=-1,
    )


def softmax_rows(queries, key_rows, allowed, live):
    scores = jnp.einsum("qhd,kd->hqk", queries, key_rows, preferred_element_type=jnp.float32)
    row_top = jnp.max(jnp.where(allowed, scores, NEGATIVE_FILL), axis=-1, keepdims=True)
    row_top = jnp.where(live, row_top, 0.0)
    weights_exp = jnp.where(allowed, jnp.exp(scores - row_top), 0.0)
    row_total = jnp.where(live, jnp.sum(weights_exp, axis=-1, keepdims=True), 1.0)
    return weights_exp / row_total


def shards(
    tokens,
    lengths,
    attn_gain,
    w_query,
    w_keyval,
    w_output,
    mlp_gain,
    w_gate,
    w_up,
    w_down,
    cotangent,
):
    gathered = in_one_piece(
        (attn_gain, w_query, w_keyval, w_output, mlp_gain, w_gate, w_up, w_down),
        SHARD_CONTEXT,
        0,
        1,
    )
    gain_one, query_w, keyval_w, output_w, gain_two, gate_w, up_w, down_w = gathered
    inputs = tokens[0].astype(jnp.float32)
    row_count = inputs.shape[0]
    seq_count = row_count * lax.axis_size(CONTEXT)
    head_dim = keyval_w.shape[1] // 2
    row_start = lax.axis_index(CONTEXT) * row_count
    padding = seq_count - lengths[0]
    token_index = row_start + jnp.arange(row_count, dtype=jnp.int32)
    position = token_index - padding
    live_rows = position >= 0
    key_index = jnp.arange(seq_count, dtype=jnp.int32)
    offset = token_index[:, None] - key_index[None, :]
    allowed = ((offset >= 0) & (offset < WINDOW) & (key_index >= padding)[None, :])[None]
    live = live_rows[None, :, None]
    cosine, sine_part = angles(position, head_dim)
    query_scale = head_dim ** (-0.5)
    normed = scaled_norm(inputs, gain_one.astype(jnp.float32)).astype(jnp.bfloat16)
    query_pre = jnp.dot(normed, query_w, preferred_element_type=jnp.float32)
    head_count = query_pre.shape[1] // head_dim
    queries = (
        rotate(query_pre.reshape(row_count, head_count, head_dim), cosine, sine_part) * query_scale
    ).astype(jnp.bfloat16)
    keyval = jnp.dot(normed, keyval_w, preferred_element_type=jnp.float32)
    keys_turned = rotate(keyval[:, None, :head_dim], cosine, sine_part)[:, 0, :]
    keyval_local = jnp.concatenate([keys_turned, keyval[:, head_dim:]], axis=1).astype(jnp.bfloat16)
    keyval_all = gather_directly(keyval_local, CONTEXT, 0)
    prob = softmax_rows(queries, keyval_all[:, :head_dim], allowed, live)
    attended = jnp.einsum(
        "hqk,kd->qhd",
        prob.astype(jnp.bfloat16),
        keyval_all[:, head_dim:],
        preferred_element_type=jnp.float32,
    )
    attended = attended.reshape(row_count, head_count * head_dim).astype(jnp.bfloat16)
    branch = over_copies(
        jnp.einsum("qc,dc->qd", attended, output_w, preferred_element_type=jnp.float32), "tensor"
    )
    hidden_in = inputs + branch
    normed_two = scaled_norm(hidden_in, gain_two.astype(jnp.float32)).astype(jnp.bfloat16)
    gate_pre = jnp.dot(normed_two, gate_w, preferred_element_type=jnp.float32)
    up_pre = jnp.dot(normed_two, up_w, preferred_element_type=jnp.float32)
    activated = jax.nn.gelu(gate_pre)
    hidden = (activated * up_pre).astype(jnp.bfloat16)
    mlp_branch = taken_together(
        jnp.einsum("qf,df->qd", hidden, down_w, preferred_element_type=jnp.float32).astype(
            jnp.bfloat16
        ),
        "tensor",
    ).astype(jnp.float32)
    block_out = jnp.where(live_rows[:, None], hidden_in + mlp_branch, 0.0).astype(jnp.bfloat16)
    grad_out = jnp.where(live_rows[:, None], cotangent[0].astype(jnp.float32), 0.0)
    grad_low = grad_out.astype(jnp.bfloat16)
    weights_back = in_one_piece(
        (attn_gain, w_query, w_keyval, w_output, mlp_gain, w_gate, w_up, w_down),
        SHARD_CONTEXT,
        0,
        1,
    )
    keyval_back = gather_directly(keyval_local, CONTEXT, 0)
    (
        gain_one_back,
        query_back,
        keyval_w_back,
        output_back,
        gain_two_back,
        gate_back,
        up_back,
        down_back,
    ) = weights_back
    down_part = jnp.einsum("qd,qf->df", grad_low, hidden, preferred_element_type=jnp.float32)
    grad_hidden = jnp.einsum("qd,df->qf", grad_low, down_back, preferred_element_type=jnp.float32)
    _, gelu_pull = jax.vjp(jax.nn.gelu, gate_pre)
    grad_gate = gelu_pull(grad_hidden * up_pre)[0].astype(jnp.bfloat16)
    grad_up = (grad_hidden * activated).astype(jnp.bfloat16)
    gate_part = jnp.einsum("qd,qf->df", normed_two, grad_gate, preferred_element_type=jnp.float32)
    up_part = jnp.einsum("qd,qf->df", normed_two, grad_up, preferred_element_type=jnp.float32)
    normed_two_part = jnp.einsum(
        "qf,df->qd", grad_gate, gate_back, preferred_element_type=jnp.float32
    ) + jnp.einsum("qf,df->qd", grad_up, up_back, preferred_element_type=jnp.float32)
    grad_normed_two = over_copies(normed_two_part, "tensor")
    _, second_pull = jax.vjp(scaled_norm, hidden_in, gain_two_back.astype(jnp.float32))
    grad_hidden_in, gain_two_part = second_pull(grad_normed_two)
    grad_hidden_in = grad_hidden_in + grad_out
    branch_low = grad_hidden_in.astype(jnp.bfloat16)
    output_part = jnp.einsum("qd,qc->dc", branch_low, attended, preferred_element_type=jnp.float32)
    grad_attended = jnp.einsum(
        "qd,dc->qc", branch_low, output_back, preferred_element_type=jnp.float32
    )
    grad_attended = grad_attended.astype(jnp.bfloat16).reshape(row_count, head_count, head_dim)
    keys_back = keyval_back[:, :head_dim]
    values_back = keyval_back[:, head_dim:]
    prob_back = softmax_rows(queries, keys_back, allowed, live)
    grad_prob = jnp.einsum(
        "qhd,kd->hqk", grad_attended, values_back, preferred_element_type=jnp.float32
    )
    spread = jnp.sum(prob_back * grad_prob, axis=-1, keepdims=True)
    grad_scores = (prob_back * (grad_prob - spread)).astype(jnp.bfloat16)
    grad_queries = jnp.einsum(
        "hqk,kd->qhd", grad_scores, keys_back, preferred_element_type=jnp.float32
    )
    grad_query_pre = (
        rotate(grad_queries * query_scale, cosine, -sine_part)
        .reshape(row_count, head_count * head_dim)
        .astype(jnp.bfloat16)
    )
    grad_keys = jnp.einsum("hqk,qhd->kd", grad_scores, queries, preferred_element_type=jnp.float32)
    grad_values = jnp.einsum(
        "hqk,qhd->kd",
        prob_back.astype(jnp.bfloat16),
        grad_attended,
        preferred_element_type=jnp.float32,
    )
    keyval_part = summed_rows(jnp.concatenate([grad_keys, grad_values], axis=1), CONTEXT, 0)
    normed_part = jnp.einsum(
        "qc,dc->qd", grad_query_pre, query_back, preferred_element_type=jnp.float32
    )
    grad_normed, keyval_sum = packed_total((normed_part, keyval_part), "tensor")
    grad_keys_pre = rotate(keyval_sum[:, None, :head_dim], cosine, -sine_part)[:, 0, :]
    grad_keyval = jnp.concatenate([grad_keys_pre, keyval_sum[:, head_dim:]], axis=1).astype(
        jnp.bfloat16
    )
    grad_normed = grad_normed + jnp.einsum(
        "qe,de->qd", grad_keyval, keyval_w_back, preferred_element_type=jnp.float32
    )
    query_part = jnp.einsum("qd,qc->dc", normed, grad_query_pre, preferred_element_type=jnp.float32)
    keyval_w_part = jnp.einsum("qd,qe->de", normed, grad_keyval, preferred_element_type=jnp.float32)
    _, first_pull = jax.vjp(scaled_norm, inputs, gain_one_back.astype(jnp.float32))
    grad_inputs, gain_one_part = first_pull(grad_normed)
    tokens_grad = (grad_inputs + grad_hidden_in).astype(jnp.bfloat16)
    partial_sums = tuple(
        (
            part.astype(jnp.float32)
            for part in side_by_side(
                (
                    gain_one_part.astype(jnp.bfloat16),
                    query_part.astype(jnp.bfloat16),
                    keyval_w_part.astype(jnp.bfloat16),
                    output_part.astype(jnp.bfloat16),
                    gain_two_part.astype(jnp.bfloat16),
                    gate_part.astype(jnp.bfloat16),
                    up_part.astype(jnp.bfloat16),
                    down_part.astype(jnp.bfloat16),
                ),
                "shard",
                0,
                1,
            )
        )
    )
    owner_sums = tuple(
        (
            part.astype(jnp.float32)
            for part in side_by_side(
                (
                    partial_sums[0].astype(jnp.bfloat16),
                    partial_sums[1].astype(jnp.bfloat16),
                    partial_sums[2].astype(jnp.bfloat16),
                    partial_sums[3].astype(jnp.bfloat16),
                    partial_sums[4].astype(jnp.bfloat16),
                    partial_sums[5].astype(jnp.bfloat16),
                    partial_sums[6].astype(jnp.bfloat16),
                    partial_sums[7].astype(jnp.bfloat16),
                ),
                CONTEXT,
                0,
                1,
            )
        )
    )
    attn_sums = owner_sums[:4]
    mlp_sums = owner_sums[4:]
    return (
        block_out[None],
        tokens_grad[None],
        attn_sums[0],
        attn_sums[1],
        attn_sums[2],
        attn_sums[3],
        mlp_sums[0],
        mlp_sums[1],
        mlp_sums[2],
        mlp_sums[3],
    )


def solution(mesh):
    torus = Mesh(
        mesh.devices.reshape(mesh.shape["shard"], 4, 4, mesh.shape["tensor"]),
        ("shard", "context_0", "context_1", "tensor"),
    )
    in_specs = (
        P("shard", CONTEXT, None),
        P("shard"),
        P(SHARD_CONTEXT),
        P(SHARD_CONTEXT, "tensor"),
        P(SHARD_CONTEXT, None),
        P(SHARD_CONTEXT, "tensor"),
        P(SHARD_CONTEXT),
        P(SHARD_CONTEXT, "tensor"),
        P(SHARD_CONTEXT, "tensor"),
        P(SHARD_CONTEXT, "tensor"),
        P("shard", CONTEXT, None),
    )
    out_specs = (
        P("shard", CONTEXT, None),
        P("shard", CONTEXT, None),
        P(SHARD_CONTEXT),
        P(SHARD_CONTEXT, "tensor"),
        P(SHARD_CONTEXT, None),
        P(SHARD_CONTEXT, "tensor"),
        P(SHARD_CONTEXT),
        P(SHARD_CONTEXT, "tensor"),
        P(SHARD_CONTEXT, "tensor"),
        P(SHARD_CONTEXT, "tensor"),
    )
    return jax.shard_map(
        shards, mesh=torus, in_specs=in_specs, out_specs=out_specs, check_vma=False
    )
```

profile of v0, /device:TPU:1, one launch (start us, length us, event | category | flops | bytes accessed | tf_op | source)
XLA Modules:
  0.0 1658.8 jit_solution(12722582827987578419)
XLA Ops:
  15.0 305.9 %all-gather.2.cloned.1.call-done = bf16[2560,14594]{1,0:T(8,128)(2,1)} async-done(((bf16[40,14594]{1,0:T(8,128)(2,1)}), bf16[2560,14594]{1,0:T(8,128)(2,1)}) %all-gather.2.cloned.1.call-update) | async-done | bytes 74721296 | tf_op jit(solution)/shard_map/all_gather | solution.py:19
  328.4 6.0 all-to-all-start
  334.5 9.7 slice_bitcast_fusion
  344.2 10.0 copy.70
  354.2 5.1 fusion.88
  360.7 15.0 fusion
  385.3 5.7 fusion.22
  391.4 8.0 all_to_all.27
  402.3 11.1 fusion.6
  413.5 13.6 fusion.38
  427.0 12.1 fusion.4
  439.2 11.7 fusion.26
  451.4 7.8 all_to_all.28
  464.9 6.1 fusion.44
  490.8 6.7 fusion.24
  500.1 5.9 convolution_convert_fusion.4
  506.0 9.6 copy.78
  515.5 11.0 convolution_convert_fusion.2
  526.5 15.0 reduce-scatter.8.cloned.1.call-done
  544.6 6.4 convolution_convert_fusion.3
  551.0 9.6 copy.80
  561.8 11.0 convolution_convert_fusion.1
  572.8 9.5 convolution_convert_fusion
  584.9 9.3 broadcast_in_dim.170
  594.2 8.4 all_to_all.29
  602.6 20.8 %reduce_sum.152 = f32[491520]{0:T(1024)} reduce(f32[2,1,491520]{2,1,0:T(1,128)} %all_to_all.29, f32[]{:T(128)} %constant.15.clone.1), dimensions={0,1}, to_apply=%region_11.12 | reduce | flops 491520 | bytes 5898244 | tf_op jit(solution)/shard_map/reduce_sum | solution.py:44
  637.1 4.6 fusion.56
  647.4 132.6 %concatenate.54 = bf16[2560,14594]{1,0:T(8,128)(2,1)} concatenate(bf16[2560,1]{1,0:T(8,128)(2,1)} %convert_element_type.290, bf16[2560,1280]{1,0:T(8,128)(2,1)} %copy.78, bf16[2560,512]{1,0:T(8,128)(2,1)} %copy.79, bf16[2560,1280]{1,0:T(8,128)(2,1)} %copy.80, bf16[2560,1]{1,0:T(8,128)(2,1)} %convert_element_type.291, bf16[2560,3840]{1,0:T(8,128)(2,1)} %convolution_convert_fusion.2, ...), dimensions={1} | concatenate | bytes 149442560 | tf_op jit(solution)/shard_map/concatenate | solution.py:69
  780.0 619.8 %reduce-scatter.12.cloned.1.call-done = bf16[640,14594]{1,0:T(8,128)(2,1)} async-done(((bf16[2560,14594]{1,0:T(8,128)(2,1)}), bf16[640,14594]{1,0:T(8,128)(2,1)}) %reduce-scatter.12.cloned.1.call-update) | async-done | bytes 18680336
  1401.7 11.6 fusion.29
  1413.4 5.5 all_to_all.30
  1423.6 220.7 %all-reduce.4.cloned.1.call-done = bf16[640,14594]{1,0:T(8,128)(2,1)} async-done(((bf16[640,14594]{1,0:T(8,128)(2,1)}), bf16[640,14594]{1,0:T(8,128)(2,1)}) %all-reduce.4.cloned.1.call-update) | async-done | bytes 18680336
  (166 shorter events, 96.8 us)
Async XLA Ops:
  7.2 6.0 copy-start
  7.2 313.8 %all-gather.2.cloned.1.call-start = ((), (), s32[]{:S(2)}) async-start(), calls=%async_computation.8 | async-start | bytes 76544000 | tf_op jit(solution)/shard_map/all_gather | solution.py:19
  13.1 313.0 %copy-start.33 = (f32[64]{0:T(128)}, f32[64]{0:T(128)S(1)}, u32[]{:S(2)}) copy-start(f32[64]{0:T(128)S(1)} %multiply_power_fusion) | copy-start | bytes 772
  13.2 312.9 %copy-start.29 = (f32[160]{0:T(256)}, f32[160]{0:T(256)S(1)}, u32[]{:S(2)}) copy-start(f32[160]{0:T(256)S(1)} %subtract_convert_fusion) | copy-start | bytes 1924
  13.5 312.6 %copy-start.31 = (f32[160]{0:T(256)}, f32[160]{0:T(256)S(1)}, u32[]{:S(2)}) copy-start(f32[160]{0:T(256)S(1)} %fusion.62) | copy-start | bytes 1924
  13.5 340.7 %copy-start.27 = (f32[160]{0:T(256)}, f32[160]{0:T(256)S(1)}, u32[]{:S(2)}) copy-start(f32[160]{0:T(256)S(1)} %fusion.126) | copy-start | bytes 1924
  14.5 344.9 %copy-start.22 = (f32[160,64]{1,0:T(8,128)}, f32[160,64]{1,0:T(8,128)S(1)}, u32[]{:S(2)}) copy-start(f32[160,64]{1,0:T(8,128)S(1)} %get-tuple-element.36) | copy-start | bytes 122884
  15.0 365.5 %copy-start.7 = (pred[160,2560]{1,0:T(8,128)(4,1)}, pred[160,2560]{1,0:T(8,128)(4,1)S(1)}, u32[]{:S(2)}) copy-start(pred[160,2560]{1,0:T(8,128)(4,1)S(1)} %fusion.74) | copy-start | bytes 1228804
  322.9 31.3 %copy-start.24 = (f32[2560]{0:T(1024)}, f32[2560]{0:T(1024)S(1)}, u32[]{:S(2)}) copy-start(f32[2560]{0:T(1024)S(1)} %get-tuple-element.10) | copy-start | bytes 30724
  328.4 47.2 %all-to-all-start = ((bf16[16,160,512]{2,1,0:T(8,128)(2,1)}), bf16[16,160,512]{2,1,0:T(8,128)(2,1)}, u32[]{:S(2)}, u32[]{:S(2)}) async-start(bf16[16,160,512]{2,1,0:T(8,128)(2,1)} %broadcast_in_dim.156), calls=%async_computation | async-start | bytes 5242880 | tf_op jit(solution)/shard_map/all_to_all | solution.py:29
  334.4 207.0 %reduce-scatter.8.cloned.1.call-start = ((), (), s32[]{:S(2)}) async-start(), calls=%async_computation.9 | async-start | bytes 6553600 | tf_op jit(solution)/shard_map/reduce_scatter | solution.py:54
  359.4 16.2 copy-start.17
  360.7 15.0 copy-start.13
  360.7 15.0 copy-start.15
  378.5 3.2 copy-start.3
  385.3 5.7 copy-start.11
  402.3 11.1 copy-start.6
  402.3 11.1 copy-start.36
  427.0 12.1 copy-start.20
  427.0 12.1 copy-start.21
  462.6 8.3 slice-start
  464.9 6.1 slice-start.1
  464.9 6.1 copy-start.8
  478.1 3.0 copy-start.14
  485.7 3.9 copy-start.23
  485.7 3.9 copy-start.26
  485.7 96.5 %reduce-scatter.10.cloned.1.call-start = ((), (), s32[]{:S(2)}) async-start(), calls=%async_computation.10 | async-start | bytes 1638400 | tf_op jit(solution)/shard_map/reduce_scatter | solution.py:54
  544.4 855.5 %reduce-scatter.12.cloned.1.call-start = ((), (), s32[]{:S(2)}) async-start(), calls=%async_computation.12 | async-start | bytes 94208000
  561.8 11.0 copy-start.19
  623.4 8.1 copy-start.30
  623.4 8.1 copy-start.34
  780.0 864.2 %all-reduce.4.cloned.1.call-start = ((), (), s32[]{:S(2)}) async-start(), calls=%async_computation.11 | async-start | bytes 37683200
  (13 other events, 25.8 us)
Sparse Core Ops, SparseCore 0:
  12.6 308.3 all-gather.1
  485.8 55.6 reduce-scatter.7
  544.5 23.1 reduce-scatter.9
  780.1 619.6 reduce-scatter.11
  1403.3 240.8 all-reduce.3
where the time goes:
time: 1670 us; the launch traced here: 1660 us
  waiting for transfers between devices  1160 us (69%)
  local copies, waits for them, and re-layouts  218 us (13%)
  matrix products  172 us (10%)
  other arithmetic  54.8 us (3%)
  blocking collectives  29.7 us (2%)
    unnamed x7, waiting for transfers between devices  841 us
    all_gather x1, waiting for transfers between devices, in_one_piece(): lax.all_gather(both, axis, axis=dim, tiled=True)  306 us
    concatenate x1, local copies, waits for them, and re-layouts, side_by_side(): both = jnp.concatenate(columns, axis=along)  133 us
  transfers between devices with their start and end apart: 6, of which 4 were waited for; matrix products, arithmetic and copies ran while one was open for 8% of the time, Pallas kernels for 0%

commit v1 on v0

v1 whole, which is shorter than its diff:
```python
import jax
import jax.numpy as jnp
from jax import lax
from jax.sharding import Mesh
from jax.sharding import PartitionSpec as P

WINDOW = 2048
SHARD_CONTEXT = ("shard", "context_0", "context_1")
CONTEXT = ("context_0", "context_1")
Y, X, Z, T = "shard", "context_0", "context_1", "tensor"

EPSILON = 1e-06
NEGATIVE_FILL = -1e30
BF = jnp.bfloat16
F32 = jnp.float32


def shift(x, axis, by):
    n = lax.axis_size(axis)
    return lax.ppermute(x, axis, [(i, (i + by) % n) for i in range(n)])


def ring_blocks(x, axis):
    after = shift(x, axis, -1)
    before = shift(x, axis, 1)
    return [x, after, shift(x, axis, 2), before]


def placed(blocks, axis, out, dim, rest):
    me = lax.axis_index(axis)
    for r, block in enumerate(blocks):
        start = list(rest)
        start[dim] = (me + r) % 4
        out = lax.dynamic_update_slice(out, jnp.expand_dims(block, dim), start)
    return out


def gather_context(block):
    rows, cols = block.shape
    half = rows // 2
    out = jnp.zeros((4, 4, rows, cols), block.dtype)
    lead = jnp.zeros((4, half, cols), block.dtype)
    tail = jnp.zeros((4, rows - half, cols), block.dtype)
    first = placed(ring_blocks(block[:half], X), X, lead, 0, (0, 0, 0))
    second = placed(ring_blocks(block[half:], Z), Z, tail, 0, (0, 0, 0))
    out = placed(ring_blocks(first, Z), Z, out, 1, (0, 0, 0, 0))
    out = placed(ring_blocks(second, X), X, out, 0, (0, 0, half, 0))
    return out.reshape(16 * rows, cols)


def summed_over(parts, axis, dim):
    me = lax.axis_index(axis)
    total = lax.dynamic_index_in_dim(parts, me, dim, keepdims=False).astype(F32)
    for r in (1, 3, 2):
        block = lax.dynamic_index_in_dim(parts, (me + r) % 4, dim, keepdims=False)
        total = total + shift(block, axis, r).astype(F32)
    return total


def scatter_context(parts, kind):
    rows, cols = parts.shape[0] // 16, parts.shape[1]
    half = rows // 2
    grid = parts.astype(kind).reshape(4, 4, rows, cols)
    one = summed_over(grid[:, :, :half], X, 0).astype(kind)
    two = summed_over(grid[:, :, half:], Z, 1).astype(kind)
    return jnp.concatenate([summed_over(one, Z, 0), summed_over(two, X, 0)], axis=0)


def gather_rows(mine):
    own = jnp.concatenate(ring_blocks(mine, Y), axis=0)
    return jnp.concatenate([own, shift(own, T, 1)], axis=0)


def scatter_rows(parts):
    half = parts.shape[0] // 2
    own = parts[:half] + shift(parts[half:].astype(BF), T, 1).astype(F32)
    blocks = own.reshape(4, half // 4, -1)
    low = blocks.astype(BF)
    total = blocks[0]
    for r in (1, 3, 2):
        total = total + shift(low[r], Y, r).astype(F32)
    return total


def rows_home(parts):
    me = lax.axis_index(Y)
    cols = parts.shape[1]
    blocks = parts.reshape(2, 4, 80, cols).swapaxes(0, 1).reshape(4, 160, cols)
    out = jnp.zeros((4, 160, cols), parts.dtype)
    for r in range(4):
        block = shift(blocks[r], Y, r) if r else blocks[0]
        out = lax.dynamic_update_slice(out, block[None], ((me - r) % 4, 0, 0))
    return out


def columns_out(blocks):
    me = lax.axis_index(Y)
    cols = blocks.shape[2]
    got = [None] * 4
    for r in range(4):
        block = lax.dynamic_index_in_dim(blocks, (me + r) % 4, 0, keepdims=False)
        got[(4 - r) % 4] = shift(block, Y, r) if r else block
    return jnp.stack(got).reshape(4, 2, 80, cols).swapaxes(0, 1).reshape(640, cols)


def quarters(x):
    rows = x.shape[0]
    return x.reshape(rows, 4, -1).swapaxes(0, 1)


def joined(blocks):
    return blocks.swapaxes(0, 1).reshape(blocks.shape[1], -1)


def to_piece_order(x):
    rows = x.shape[0]
    return x.reshape(rows, 4, 16, 40).swapaxes(1, 2).reshape(rows, 2560)


def from_piece_order(x):
    rows = x.shape[0]
    return x.reshape(rows, 16, 4, 40).swapaxes(1, 2).reshape(rows, 2560)


def halves_home(mine, t):
    other = shift(mine, T, 1)
    return jnp.where(t == 0, jnp.concatenate([mine, other]), jnp.concatenate([other, mine]))


def inverse_root(values):
    return lax.rsqrt(jnp.mean(values * values, axis=-1, keepdims=True) + EPSILON)


def norm_back(grad, values, inverse, gain):
    scaled = gain * grad
    return inverse * scaled - values * inverse**3 * jnp.mean(
        scaled * values, axis=-1, keepdims=True
    )


def angles(position, head_dim):
    quarter = head_dim // 4
    frequency = 10000.0 ** (-jnp.arange(quarter, dtype=F32) / quarter)
    phase_angle = position[:, None].astype(F32) * frequency[None, :]
    return (jnp.cos(phase_angle), jnp.sin(phase_angle))


def rotate(values, cosine, sine_part):
    quarter = cosine.shape[-1]
    first_half = values[..., :quarter]
    second = values[..., quarter : 2 * quarter]
    cos_rows = cosine[:, None, :]
    sin_rows = sine_part[:, None, :]
    return jnp.concatenate(
        [
            first_half * cos_rows - second * sin_rows,
            second * cos_rows + first_half * sin_rows,
            values[..., 2 * quarter :],
        ],
        axis=-1,
    )


def dot(a, b, da, db):
    return lax.dot_general(a, b, (((da,), (db,)), ((), ())), preferred_element_type=F32)


def shards(
    tokens,
    lengths,
    attn_gain,
    w_query,
    w_keyval,
    w_output,
    mlp_gain,
    w_gate,
    w_up,
    w_down,
    cotangent,
):
    t = lax.axis_index(T)
    piece = lax.axis_index(CONTEXT)
    head_dim = 256
    query_scale = head_dim ** (-0.5)
    seq_count = 2560
    padding = seq_count - lengths[0]
    row_start = piece * 160
    natural = row_start + jnp.arange(160, dtype=jnp.int32)
    turned = row_start + (jnp.arange(160, dtype=jnp.int32) + t * 80) % 160
    live_turned = turned >= padding
    live_mine = live_turned[:80, None]

    x_mine = to_piece_order(lax.dynamic_slice_in_dim(tokens[0], t * 80, 80, 0)).astype(F32)
    cot_mine = to_piece_order(lax.dynamic_slice_in_dim(cotangent[0], t * 80, 80, 0))
    grad_mine = jnp.where(live_mine, cot_mine, jnp.zeros_like(cot_mine))

    keyval_half = lax.dynamic_slice_in_dim(w_keyval, t * 256, 256, 1)
    gains = jnp.concatenate([attn_gain, mlp_gain])[None, :]
    gains = jnp.broadcast_to(jnp.pad(gains, ((0, 7), (0, 304)))[None], (4, 8, 384))
    attn_out = jnp.concatenate(
        [jnp.concatenate([quarters(w_query), quarters(keyval_half)], axis=2), gains], axis=1
    )
    attn_in = lax.all_to_all(attn_out, Y, 0, 0, tiled=True)
    gain_rows = attn_in[:, 40, :80].reshape(4, 2, 40).swapaxes(0, 1).reshape(1, 320)
    gain_block = jnp.pad(gain_rows, ((0, 15), (0, 64)))
    attn_block = jnp.concatenate([attn_in[:, :40].reshape(160, 384), gain_block], axis=0)
    attn_all = gather_context(attn_block).reshape(16, 176, 384)
    w_qkv = attn_all[:, :160].reshape(2560, 384)
    gain_one = attn_all[:, 160, :160].reshape(1, 2560).astype(F32)
    gain_two = attn_all[:, 160, 160:320].reshape(1, 2560).astype(F32)

    mlp_out_blocks = jnp.concatenate([quarters(w_gate), quarters(w_up), quarters(w_down)], axis=2)
    mlp_block = lax.all_to_all(mlp_out_blocks, Y, 0, 0, tiled=True).reshape(160, 2880)
    w_mlp = lax.all_gather(mlp_block, CONTEXT, axis=0, tiled=True)
    w_gate_up = w_mlp[:, :1920]
    w_down_all = w_mlp[:, 1920:]

    out_piece = gather_context(w_output).reshape(16, 40, 1280)
    w_out = placed(
        ring_blocks(out_piece, Y), Y, jnp.zeros((16, 4, 40, 1280), BF), 1, (0, 0, 0, 0)
    ).reshape(2560, 1280)

    inverse_one = inverse_root(x_mine)
    normed = gather_rows((x_mine * inverse_one * gain_one).astype(BF))
    projected = dot(normed, w_qkv, 1, 0).astype(BF)
    home = rows_home(projected)
    query_pre = joined(home[:, :, :320]).reshape(160, 5, head_dim).astype(F32)
    cosine, sine_part = angles(turned - padding, head_dim)
    queries = (rotate(query_pre, cosine, sine_part) * query_scale).astype(BF)
    keyval_turned = joined(home[:, :, 320:])
    keyval_own = jnp.where(
        t == 0, keyval_turned, jnp.concatenate([keyval_turned[80:], keyval_turned[:80]])
    )
    cosine_nat, sine_nat = angles(natural - padding, head_dim)
    keys_own = rotate(keyval_own[:, None].astype(F32), cosine_nat, sine_nat)[:, 0].astype(BF)
    kv_own = jnp.where(t == 0, keys_own, keyval_own)
    kv_mine = gather_context(kv_own)
    kv_other = shift(kv_mine, T, 1)
    keys = jnp.where(t == 0, kv_mine, kv_other)
    values = jnp.where(t == 0, kv_other, kv_mine)

    key_index = jnp.arange(seq_count, dtype=jnp.int32)
    offset = turned[:, None] - key_index[None, :]
    allowed = ((offset >= 0) & (offset < WINDOW) & (key_index >= padding)[None, :])[None]
    live = live_turned[None, :, None]
    scores = jnp.einsum("qhd,kd->hqk", queries, keys, preferred_element_type=F32)
    row_top = jnp.max(jnp.where(allowed, scores, NEGATIVE_FILL), axis=-1, keepdims=True)
    row_top = jnp.where(live, row_top, 0.0)
    weights_exp = jnp.where(allowed, jnp.exp(scores - row_top), 0.0)
    row_total = jnp.where(live, jnp.sum(weights_exp, axis=-1, keepdims=True), 1.0)
    prob = weights_exp / row_total
    prob_low = prob.astype(BF)
    attended = jnp.einsum("hqk,kd->qhd", prob_low, values, preferred_element_type=F32)
    attended = attended.reshape(160, 1280).astype(BF)
    attended_group = columns_out(quarters(attended))

    branch = dot(attended, w_out, 1, 1)
    hidden_mine = x_mine + branch[:80] + shift(branch[80:], T, 1)

    inverse_two = inverse_root(hidden_mine)
    normed_two = gather_rows((hidden_mine * inverse_two * gain_two).astype(BF))
    grad_group = gather_rows(grad_mine)
    gate_up = dot(normed_two, w_gate_up, 1, 0)
    gate_pre, up_pre = gate_up[:, :960], gate_up[:, 960:]
    activated, gelu_pull = jax.vjp(jax.nn.gelu, gate_pre)
    hidden = (activated * up_pre).astype(BF)
    grad_hidden = dot(grad_group, w_down_all, 1, 0)
    grad_gate = gelu_pull(grad_hidden * up_pre)[0].astype(BF)
    grad_up = (grad_hidden * activated).astype(BF)
    grad_gate_up = jnp.concatenate([grad_gate, grad_up], axis=1)
    grad_normed_two = scatter_rows(dot(grad_gate_up, w_gate_up, 1, 1))

    gate_up_part = dot(normed_two, grad_gate_up, 0, 0).astype(BF)
    down_part = dot(grad_group, hidden, 0, 0).astype(BF)
    mlp_part = jnp.concatenate([gate_up_part, down_part], axis=1)
    mlp_sum = lax.psum_scatter(mlp_part, CONTEXT, scatter_dimension=0, tiled=True)

    mlp_mine = scatter_rows(dot(hidden, w_down_all, 1, 1))
    block_mine = jnp.where(live_mine, hidden_mine + mlp_mine, 0.0).astype(BF)
    block_out = halves_home(from_piece_order(block_mine), t)

    grad_h_mine = grad_mine.astype(F32) + norm_back(
        grad_normed_two, hidden_mine, inverse_two, gain_two
    )
    branch_mine = grad_h_mine.astype(BF)
    branch_low = jnp.concatenate([branch_mine, shift(branch_mine, T, 1)])
    grad_attended = dot(branch_low, w_out, 1, 0).astype(BF).reshape(160, 5, head_dim)
    branch_group = gather_rows(branch_mine)
    output_part = dot(branch_group, attended_group, 0, 0)
    output_sum = scatter_context(output_part, BF)

    grad_prob = jnp.einsum("qhd,kd->hqk", grad_attended, values, preferred_element_type=F32)
    spread = jnp.sum(prob * grad_prob, axis=-1, keepdims=True)
    grad_scores = (prob * (grad_prob - spread)).astype(BF)
    grad_queries = jnp.einsum("hqk,kd->qhd", grad_scores, keys, preferred_element_type=F32)
    grad_query_pre = (
        rotate(grad_queries * query_scale, cosine, -sine_part).reshape(160, 1280).astype(BF)
    )
    grad_query_group = columns_out(quarters(grad_query_pre))
    grad_keys = jnp.einsum("hqk,qhd->kd", grad_scores, queries, preferred_element_type=F32)
    grad_values = jnp.einsum("hqk,qhd->kd", prob_low, grad_attended, preferred_element_type=F32)
    keep = jnp.where(t == 0, grad_keys, grad_values)
    give = jnp.where(t == 0, grad_values, grad_keys)
    kv_sum = scatter_context(keep + shift(give, T, 1), F32)
    keys_back = rotate(kv_sum[:, None], cosine_nat, -sine_nat)[:, 0]
    kv_back = jnp.where(t == 0, keys_back, kv_sum).astype(BF)
    kv_back = jnp.where(t == 0, kv_back, jnp.concatenate([kv_back[80:], kv_back[:80]]))
    grad_kv_group = columns_out(quarters(kv_back))
    grad_qkv_group = jnp.concatenate([grad_query_group, grad_kv_group], axis=1)
    grad_normed = scatter_rows(dot(grad_qkv_group, w_qkv, 1, 1))
    tokens_mine = grad_h_mine + norm_back(grad_normed, x_mine, inverse_one, gain_one)
    tokens_grad = halves_home(from_piece_order(tokens_mine.astype(BF)), t)

    qkv_part = dot(normed, grad_qkv_group, 0, 0)
    qkv_sum = scatter_context(qkv_part, BF)
    attn_sum = jnp.concatenate([qkv_sum, output_sum], axis=1).astype(BF)
    attn_home = lax.all_to_all(attn_sum.reshape(4, 40, 704), Y, 0, 0, tiled=True).astype(F32)
    query_grad = joined(attn_home[:, :, :320])
    kv_grad_half = joined(attn_home[:, :, 320:384])
    output_grad = joined(attn_home[:, :, 384:])
    kv_grad_other = shift(kv_grad_half, T, 1)
    keyval_grad = jnp.where(
        t == 0,
        jnp.concatenate([kv_grad_half, kv_grad_other], axis=1),
        jnp.concatenate([kv_grad_other, kv_grad_half], axis=1),
    )
    mlp_home = lax.all_to_all(mlp_sum.reshape(4, 40, 2880), Y, 0, 0, tiled=True).astype(F32)
    gate_grad = joined(mlp_home[:, :, :960])
    up_grad = joined(mlp_home[:, :, 960:1920])
    down_grad = joined(mlp_home[:, :, 1920:])

    one_part = jnp.sum(w_query.astype(F32) * query_grad, axis=1) + jnp.sum(
        keyval_half.astype(F32) * kv_grad_half, axis=1
    )
    two_part = jnp.sum(w_gate.astype(F32) * gate_grad + w_up.astype(F32) * up_grad, axis=1)
    both = jnp.stack([one_part, two_part])
    both = both + shift(both, T, 1)
    attn_gain_grad = both[0] / attn_gain.astype(F32)
    mlp_gain_grad = both[1] / mlp_gain.astype(F32)

    return (
        block_out[None],
        tokens_grad[None],
        attn_gain_grad,
        query_grad,
        keyval_grad,
        output_grad,
        mlp_gain_grad,
        gate_grad,
        up_grad,
        down_grad,
    )


def solution(mesh):
    torus = Mesh(
        mesh.devices.reshape(mesh.shape["shard"], 4, 4, mesh.shape["tensor"]),
        ("shard", "context_0", "context_1", "tensor"),
    )
    in_specs = (
        P("shard", CONTEXT, None),
        P("shard"),
        P(SHARD_CONTEXT),
        P(SHARD_CONTEXT, "tensor"),
        P(SHARD_CONTEXT, None),
        P(SHARD_CONTEXT, "tensor"),
        P(SHARD_CONTEXT),
        P(SHARD_CONTEXT, "tensor"),
        P(SHARD_CONTEXT, "tensor"),
        P(SHARD_CONTEXT, "tensor"),
        P("shard", CONTEXT, None),
    )
    out_specs = (
        P("shard", CONTEXT, None),
        P("shard", CONTEXT, None),
        P(SHARD_CONTEXT),
        P(SHARD_CONTEXT, "tensor"),
        P(SHARD_CONTEXT, None),
        P(SHARD_CONTEXT, "tensor"),
        P(SHARD_CONTEXT),
        P(SHARD_CONTEXT, "tensor"),
        P(SHARD_CONTEXT, "tensor"),
        P(SHARD_CONTEXT, "tensor"),
    )
    return jax.shard_map(
        shards, mesh=torus, in_specs=in_specs, out_specs=out_specs, check_vma=False
    )
```

time: 1670 us -> 777 us (0.47)
  waiting for transfers between devices: 1160 us -> 181 us
  starting transfers between devices: 6.41 us -> 231 us
  matrix products: 172 us -> 98.7 us
  local copies, waits for them, and re-layouts: 218 us -> 168 us
  blocking collectives: 29.7 us -> 0 us
    unnamed x7 -> x2, waiting for transfers between devices: 841 us -> 0.69 us
    all_gather x1, waiting for transfers between devices: 306 us -> 0.01 us  [shards(): w_mlp = lax.all_gather(mlp_block, CONTEXT, axis=0, tiled=True)]
    ppermute x0 -> x123, starting transfers between devices: none -> 216 us  [shift(): return lax.ppermute(x, axis, [(i, (i + by) % n) for i in range(n)])]
    ppermute x0 -> x123, waiting for transfers between devices: none -> 173 us  [shift(): return lax.ppermute(x, axis, [(i, (i + by) % n) for i in range(n)])]
    concatenate x2 -> x8, local copies, waits for them, and re-layouts: 136 us -> 9.01 us  [the longest x4 5.66 us: gather_rows(): return jnp.concatenate([own, shift(own, T, 1)], axis=0)]
    dot_general x24 -> x18, matrix products: 172 us -> 98.7 us  [the longest x12 73.9 us: dot(): lax.dot_general(a, b, (((da,), (db,)), ((), ())), preferred_element_type=...]
    dynamic_update_slice x0 -> x55, local copies, waits for them, and re-layouts: none -> 58.1 us  [the longest x51 45 us: placed(): out = lax.dynamic_update_slice(out, jnp.expand_dims(block, dim), start)]
    unnamed x81 -> x188, local copies, waits for them, and re-layouts: 9.52 us -> 45.7 us
  transfers between devices with their start and end apart: 6 -> 129, of which waited for: 4 -> 41; matrix products, arithmetic and copies ran while one was open for 8% -> 32% of each run, Pallas kernels for 0% -> 0%
where the time goes in v1:
time: 777 us; the launch traced here: 765 us
  starting transfers between devices  231 us (30%)
  waiting for transfers between devices  181 us (23%)
  local copies, waits for them, and re-layouts  168 us (22%)
  matrix products  98.7 us (13%)
  other arithmetic  68.9 us (9%)
  between operations  17.6 us (2%)
    ppermute x123, starting transfers between devices, shift(): return lax.ppermute(x, axis, [(i, (i + by) % n) for i in range(n)])  216 us
    ppermute x123, waiting for transfers between devices, shift(): return lax.ppermute(x, axis, [(i, (i + by) % n) for i in range(n)])  173 us
    dot_general x12, matrix products, dot(): lax.dot_general(a, b, (((da,), (db,)), ((), ())), preferred_element_type=...  73.9 us
    unnamed x188, local copies, waits for them, and re-layouts  45.7 us
    dynamic_update_slice x51, local copies, waits for them, and re-layouts, placed(): out = lax.dynamic_update_slice(out, jnp.expand_dims(block, dim), start)  45 us
    concatenate x1, other arithmetic, shards(): mlp_part = jnp.concatenate([gate_up_part, down_part], axis=1)  16.1 us
  transfers between devices with their start and end apart: 129, of which 41 were waited for; matrix products, arithmetic and copies ran while one was open for 32% of the time, Pallas kernels for 0%

profile of v1, /device:TPU:1, one launch (start us, length us, event | category | flops | bytes accessed | tf_op | source)
XLA Modules:
  0.0 765.1 jit_solution(14472656926142551361)
XLA Ops:
  82.1 7.1 collective-permute-done.3
  100.3 10.6 %collective-permute-done.10 = bf16[4,88,384]{2,1,0:T(8,128)(2,1)S(1)} collective-permute-done((bf16[4,88,384]{2,1,0:T(8,128)(2,1)S(1)}, bf16[4,88,384]{2,1,0:T(8,128)(2,1)S(1)}, u32[]{:S(2)}, u32[]{:S(2)}) %collective-permute-start.10) | collective-permute-done | bytes 270368 | tf_op jit(solution)/shard_map/ppermute | solution.py:20
  114.1 4.7 collective-permute-done.11
  162.5 16.5 %collective-permute-start.15 = (bf16[320,2560]{1,0:T(8,128)(2,1)S(1)}, bf16[320,2560]{1,0:T(8,128)(2,1)S(1)}, u32[]{:S(2)}, u32[]{:S(2)}) collective-permute-start(bf16[320,2560]{1,0:T(8,128)(2,1)S(1)} %pad_maximum_fusion.2), channel_id=1, source_target_pairs={{0,1},{1,0},{2,3},{3,2},{4,5},{5,4},{6,7},{7,6},{8,9},{9,8},{10,11... | collective-permute-start | bytes 4915208 | tf_op jit(solution)/shard_map/ppermute | solution.py:20
  201.3 35.5 %collective-permute-done.16 = bf16[160,384]{1,0:T(8,128)(2,1)S(1)} collective-permute-done((bf16[160,384]{1,0:T(8,128)(2,1)S(1)}, bf16[160,384]{1,0:T(8,128)(2,1)S(1)}, u32[]{:S(2)}, u32[]{:S(2)}) %collective-permute-start.16) | collective-permute-done | bytes 122912 | tf_op jit(solution)/shard_map/ppermute | solution.py:20
  274.4 15.1 %collective-permute-start.31 = (bf16[2560,256]{1,0:T(8,128)(2,1)}, bf16[2560,256]{1,0:T(8,128)(2,1)}, u32[]{:S(2)}, u32[]{:S(2)}) collective-permute-start(bf16[2560,256]{1,0:T(8,128)(2,1)} %bitcast.68), channel_id=1, source_target_pairs={{0,1},{1,0},{2,3},{3,2},{4,5},{5,4},{6,7},{7,6},{8,9},{9,8},{10,11... | collective-permute-start | bytes 3932168 | tf_op jit(solution)/shard_map/ppermute | solution.py:20
  304.3 5.3 fusion.155
  315.0 7.6 collective-permute-done.57
  324.0 9.7 %collective-permute-done.59 = bf16[80,2560]{1,0:T(8,128)(2,1)S(1)} collective-permute-done((bf16[80,2560]{1,0:T(8,128)(2,1)S(1)}, bf16[80,2560]{1,0:T(8,128)(2,1)S(1)}, u32[]{:S(2)}, u32[]{:S(2)}) %collective-permute-start.59) | collective-permute-done | bytes 409632 | tf_op jit(solution)/shard_map/ppermute | solution.py:20
  341.8 7.6 collective-permute-done.48
  351.2 9.3 %collective-permute-done.50 = bf16[80,2560]{1,0:T(8,128)(2,1)S(1)} collective-permute-done((bf16[80,2560]{1,0:T(8,128)(2,1)S(1)}, bf16[80,2560]{1,0:T(8,128)(2,1)S(1)}, u32[]{:S(2)}, u32[]{:S(2)}) %collective-permute-start.50) | collective-permute-done | bytes 409632 | tf_op jit(solution)/shard_map/ppermute | solution.py:20
  367.0 10.9 %fusion.2 = f32[640,1920]{1,0:T(8,128)S(1)} fusion(bf16[640,2560]{1,0:T(8,128)(2,1)} %constant_dynamic-update-slice_fusion.5, bf16[2560,2880]{1,0:T(8,128)(2,1)} %all-gather.2.cloned.1.call-done), kind=kOutput, calls=%fused_computation.4 | convolution fusion | flops 6291456000 | bytes 18022400 | tf_op jit(solution)/shard_map/dot_general | solution.py:165
  377.9 8.8 %fusion.22 = (bf16[640,960]{1,0:T(8,128)(2,1)S(1)}, bf16[640,960]{1,0:T(8,128)(2,1)}, bf16[640,960]{1,0:T(8,128)(2,1)S(1)}) fusion(f32[640,1920]{1,0:T(8,128)S(1)} %fusion.2, bf16[640,2560]{1,0:T(8,128)(2,1)S(1)} %copy-done.56, bf16[2560,2880]{1,0:T(8,128)(2,1)} %all-gather.2.cloned.1.call-done), kind=kOutput, calls=%fused_computation.41 | convolution fusion | flops 3161702400 | bytes 17121280 | tf_op jit(solution)/shard_map/dot_general | solution.py:165
  391.1 11.2 %convolution_convert_fusion = bf16[2560,1920]{0,1:T(8,128)(2,1)S(1)} fusion(bf16[640,2560]{1,0:T(8,128)(2,1)} %constant_dynamic-update-slice_fusion.5, bf16[640,960]{1,0:T(8,128)(2,1)} %get-tuple-element.74, bf16[640,960]{1,0:T(8,128)(2,1)S(1)} %get-tuple-element.73), kind=kOutput, calls=%fused_computation.1 | convolution fusion | flops 6301286400 | bytes 15564800 | tf_op jit(solution)/shard_map/dot_general | solution.py:165
  402.3 16.1 %pad_maximum_fusion = bf16[2560,2880]{0,1:T(8,128)(2,1)} fusion(bf16[2560,960]{0,1:T(8,128)(2,1)S(1)} %convolution_convert_fusion.1, bf16[2560,1920]{0,1:T(8,128)(2,1)S(1)} %convolution_convert_fusion), kind=kLoop, calls=%fused_computation | loop fusion | flops 29491200 | bytes 29491200 | tf_op jit(solution)/shard_map/concatenate | solution.py:275
  418.4 20.0 %copy.371 = bf16[2560,2880]{1,0:T(8,128)(2,1)} copy(bf16[2560,2880]{0,1:T(8,128)(2,1)} %pad_maximum_fusion) | data formatting | bytes 29491200
  438.4 6.0 fusion.14
  446.2 10.0 %fusion = f32[640,2560]{1,0:T(8,128)S(1)} fusion(bf16[2560,2880]{1,0:T(8,128)(2,1)} %all-gather.2.cloned.1.call-done, bf16[640,960]{1,0:T(8,128)(2,1)S(1)} %copy-done.76, bf16[640,960]{1,0:T(8,128)(2,1)S(1)} %copy-done.75), kind=kOutput, calls=%fused_computation.2 | convolution fusion | flops 6296371200 | bytes 18841600 | tf_op jit(solution)/shard_map/dot_general | solution.py:165
  464.3 5.2 collective-permute-done.53
  470.1 7.6 collective-permute-done.55
  477.7 9.4 %collective-permute-done.62 = bf16[80,2560]{1,0:T(8,128)(2,1)S(1)} collective-permute-done((bf16[80,2560]{1,0:T(8,128)(2,1)S(1)}, bf16[80,2560]{1,0:T(8,128)(2,1)S(1)}, u32[]{:S(2)}, u32[]{:S(2)}) %collective-permute-start.62) | collective-permute-done | bytes 409632 | tf_op jit(solution)/shard_map/ppermute | solution.py:20
  487.0 8.2 %collective-permute-done.64 = bf16[80,2560]{1,0:T(8,128)(2,1)S(1)} collective-permute-done((bf16[80,2560]{1,0:T(8,128)(2,1)S(1)}, bf16[80,2560]{1,0:T(8,128)(2,1)S(1)}, u32[]{:S(2)}, u32[]{:S(2)}) %collective-permute-start.64) | collective-permute-done | bytes 409632 | tf_op jit(solution)/shard_map/ppermute | solution.py:20
  505.0 4.4 collective-permute-done.106
  518.5 4.9 convolution_convert_fusion.4
  523.5 7.2 fusion.4
  551.9 5.4 broadcast_select_fusion
  567.3 4.7 convolution_convert_fusion.3
  664.2 12.6 %collective-permute-start.85 = (bf16[320,2560]{1,0:T(8,128)(2,1)}, bf16[320,2560]{1,0:T(8,128)(2,1)}, u32[]{:S(2)}, u32[]{:S(2)}) collective-permute-start(bf16[320,2560]{1,0:T(8,128)(2,1)} %slice.484), channel_id=1, source_target_pairs={{0,1},{1,0},{2,3},{3,2},{4,5},{5,4},{6,7},{7,6},{8,9},{9,8},{10,11... | collective-permute-start | bytes 4915208 | tf_op jit(solution)/shard_map/ppermute | solution.py:20
  703.7 4.8 fusion.137
  714.5 4.7 collective-permute-start.122
  720.4 5.2 collective-permute-done.88
  735.1 7.0 collective-permute-start.89
  (708 shorter events, 444.4 us)
Async XLA Ops:
  8.7 40.2 %collective-permute-start.32 = (bf16[20,1280]{1,0:T(8,128)(2,1)}, bf16[20,1280]{1,0:T(8,128)(2,1)}, u32[]{:S(2)}, u32[]{:S(2)}) collective-permute-start(bf16[20,1280]{1,0:T(8,128)(2,1)} %get-tuple-element.171), channel_id=1, source_target_pairs={{0,24},{8,0},{16,8},{24,16},{1,25},{9,1},{17,9},{25,17},{2,26},{10... | collective-permute-start | bytes 153608 | tf_op jit(solution)/shard_map/ppermute | solution.py:20
  12.0 38.8 %collective-permute-start.33 = (bf16[20,1280]{1,0:T(8,128)(2,1)}, bf16[20,1280]{1,0:T(8,128)(2,1)}, u32[]{:S(2)}, u32[]{:S(2)}) collective-permute-start(bf16[20,1280]{1,0:T(8,128)(2,1)} %get-tuple-element.171), channel_id=1, source_target_pairs={{0,16},{8,24},{16,0},{24,8},{1,17},{9,25},{17,1},{25,9},{2,18},{10... | collective-permute-start | bytes 153608 | tf_op jit(solution)/shard_map/ppermute | solution.py:20
  12.6 39.7 %collective-permute-start.34 = (bf16[20,1280]{1,0:T(8,128)(2,1)}, bf16[20,1280]{1,0:T(8,128)(2,1)}, u32[]{:S(2)}, u32[]{:S(2)}) collective-permute-start(bf16[20,1280]{1,0:T(8,128)(2,1)} %get-tuple-element.171), channel_id=1, source_target_pairs={{0,8},{8,16},{16,24},{24,0},{1,9},{9,17},{17,25},{25,1},{2,10},{10... | collective-permute-start | bytes 153608 | tf_op jit(solution)/shard_map/ppermute | solution.py:20
  13.2 44.3 %collective-permute-start.38 = (bf16[20,1280]{1,0:T(8,128)(2,1)}, bf16[20,1280]{1,0:T(8,128)(2,1)S(1)}, u32[]{:S(2)}, u32[]{:S(2)}) collective-permute-start(bf16[20,1280]{1,0:T(8,128)(2,1)} %get-tuple-element.170), channel_id=1, source_target_pairs={{0,6},{2,0},{4,2},{6,4},{1,7},{3,1},{5,3},{7,5},{8,14},{10,8},{12,... | collective-permute-start | bytes 153608 | tf_op jit(solution)/shard_map/ppermute | solution.py:20
  16.9 41.2 %collective-permute-start.39 = (bf16[20,1280]{1,0:T(8,128)(2,1)}, bf16[20,1280]{1,0:T(8,128)(2,1)S(1)}, u32[]{:S(2)}, u32[]{:S(2)}) collective-permute-start(bf16[20,1280]{1,0:T(8,128)(2,1)} %get-tuple-element.170), channel_id=1, source_target_pairs={{0,4},{2,6},{4,0},{6,2},{1,5},{3,7},{5,1},{7,3},{8,12},{10,14},{12... | collective-permute-start | bytes 153608 | tf_op jit(solution)/shard_map/ppermute | solution.py:20
  43.0 324.0 %all-gather.2.cloned.1.call-start = ((), (), s32[]{:S(2)}) async-start(), calls=%async_computation.5 | async-start | bytes 16015360 | tf_op jit(solution)/shard_map/all_gather | solution.py:214
  43.7 683.6 %reduce-scatter.4.cloned.1.call-start = ((), (), s32[]{:S(2)}) async-start(), calls=%async_computation.6 | async-start | bytes 16015360 | tf_op jit(solution)/shard_map/reduce_scatter | solution.py:276
  53.7 69.7 %collective-permute-start.35 = (bf16[4,20,1280]{2,1,0:T(8,128)(2,1)}, bf16[4,20,1280]{2,1,0:T(8,128)(2,1)}, u32[]{:S(2)}, u32[]{:S(2)}) collective-permute-start(bf16[4,20,1280]{2,1,0:T(8,128)(2,1)} %bitcast_dynamic-update-slice_fusion.31), channel_id=1, source_target_pairs={{0,6},{2,0},{4,2},{6,4},{1,7},{3,1},{5,3},{7,5},{8,14},{10,8},{12,... | collective-permute-start | bytes 614408 | tf_op jit(solution)/shard_map/ppermute | solution.py:20
  56.0 68.0 %collective-permute-start.36 = (bf16[4,20,1280]{2,1,0:T(8,128)(2,1)}, bf16[4,20,1280]{2,1,0:T(8,128)(2,1)}, u32[]{:S(2)}, u32[]{:S(2)}) collective-permute-start(bf16[4,20,1280]{2,1,0:T(8,128)(2,1)} %bitcast_dynamic-update-slice_fusion.31), channel_id=1, source_target_pairs={{0,4},{2,6},{4,0},{6,2},{1,5},{3,7},{5,1},{7,3},{8,12},{10,14},{12... | collective-permute-start | bytes 614408 | tf_op jit(solution)/shard_map/ppermute | solution.py:20
  57.5 68.2 %collective-permute-start.37 = (bf16[4,20,1280]{2,1,0:T(8,128)(2,1)}, bf16[4,20,1280]{2,1,0:T(8,128)(2,1)}, u32[]{:S(2)}, u32[]{:S(2)}) collective-permute-start(bf16[4,20,1280]{2,1,0:T(8,128)(2,1)} %bitcast_dynamic-update-slice_fusion.31), channel_id=1, source_target_pairs={{0,2},{2,4},{4,6},{6,0},{1,3},{3,5},{5,7},{7,1},{8,10},{10,12},{12... | collective-permute-start | bytes 614408 | tf_op jit(solution)/shard_map/ppermute | solution.py:20
  120.7 39.8 %collective-permute-start.12 = (bf16[80,2560]{1,0:T(8,128)(2,1)}, bf16[80,2560]{1,0:T(8,128)(2,1)S(1)}, u32[]{:S(2)}, u32[]{:S(2)}) collective-permute-start(bf16[80,2560]{1,0:T(8,128)(2,1)} %get-tuple-element.70), channel_id=1, source_target_pairs={{0,96},{32,0},{64,32},{96,64},{1,97},{33,1},{65,33},{97,65},{2,98}... | collective-permute-start | bytes 1228808 | tf_op jit(solution)/shard_map/ppermute | solution.py:20
  123.4 37.6 %collective-permute-start.13 = (bf16[80,2560]{1,0:T(8,128)(2,1)}, bf16[80,2560]{1,0:T(8,128)(2,1)}, u32[]{:S(2)}, u32[]{:S(2)}) collective-permute-start(bf16[80,2560]{1,0:T(8,128)(2,1)} %get-tuple-element.70), channel_id=1, source_target_pairs={{0,64},{32,96},{64,0},{96,32},{1,65},{33,97},{65,1},{97,33},{2,66}... | collective-permute-start | bytes 1228808 | tf_op jit(solution)/shard_map/ppermute | solution.py:20
  124.0 37.0 %collective-permute-start.14 = (bf16[80,2560]{1,0:T(8,128)(2,1)}, bf16[80,2560]{1,0:T(8,128)(2,1)}, u32[]{:S(2)}, u32[]{:S(2)}) collective-permute-start(bf16[80,2560]{1,0:T(8,128)(2,1)} %get-tuple-element.70), channel_id=1, source_target_pairs={{0,32},{32,64},{64,96},{96,0},{1,33},{33,65},{65,97},{97,1},{2,34}... | collective-permute-start | bytes 1228808 | tf_op jit(solution)/shard_map/ppermute | solution.py:20
  127.2 26.8 %collective-permute-start.43 = (bf16[4,20,1280]{2,1,0:T(8,128)(2,1)}, bf16[4,20,1280]{2,1,0:T(8,128)(2,1)}, u32[]{:S(2)}, u32[]{:S(2)}) collective-permute-start(bf16[4,20,1280]{2,1,0:T(8,128)(2,1)} %bitcast_dynamic-update-slice_fusion.27), channel_id=1, source_target_pairs={{0,8},{8,16},{16,24},{24,0},{1,9},{9,17},{17,25},{25,1},{2,10},{10... | collective-permute-start | bytes 614408 | tf_op jit(solution)/shard_map/ppermute | solution.py:20
  156.8 31.4 %collective-permute-start.44 = (bf16[16,40,1280]{2,1,0:T(8,128)(2,1)}, bf16[16,40,1280]{2,1,0:T(8,128)(2,1)S(1)}, u32[]{:S(2)}, u32[]{:S(2)}) collective-permute-start(bf16[16,40,1280]{2,1,0:T(8,128)(2,1)} %bitcast.482), channel_id=1, source_target_pairs={{0,96},{32,0},{64,32},{96,64},{1,97},{33,1},{65,33},{97,65},{2,98}... | collective-permute-start | bytes 4915208 | tf_op jit(solution)/shard_map/ppermute | solution.py:20
  159.9 36.6 %collective-permute-start.45 = (bf16[16,40,1280]{2,1,0:T(8,128)(2,1)}, bf16[16,40,1280]{2,1,0:T(8,128)(2,1)S(1)}, u32[]{:S(2)}, u32[]{:S(2)}) collective-permute-start(bf16[16,40,1280]{2,1,0:T(8,128)(2,1)} %bitcast.483), channel_id=1, source_target_pairs={{0,64},{32,96},{64,0},{96,32},{1,65},{33,97},{65,1},{97,33},{2,66}... | collective-permute-start | bytes 4915208 | tf_op jit(solution)/shard_map/ppermute | solution.py:20
  160.5 129.0 %collective-permute-start.46 = (bf16[16,40,1280]{2,1,0:T(8,128)(2,1)}, bf16[16,40,1280]{2,1,0:T(8,128)(2,1)}, u32[]{:S(2)}, u32[]{:S(2)}) collective-permute-start(bf16[16,40,1280]{2,1,0:T(8,128)(2,1)} %bitcast.484), channel_id=1, source_target_pairs={{0,32},{32,64},{64,96},{96,0},{1,33},{33,65},{65,97},{97,1},{2,34}... | collective-permute-start | bytes 4915208 | tf_op jit(solution)/shard_map/ppermute | solution.py:20
  162.5 27.1 %collective-permute-start.15 = (bf16[320,2560]{1,0:T(8,128)(2,1)S(1)}, bf16[320,2560]{1,0:T(8,128)(2,1)S(1)}, u32[]{:S(2)}, u32[]{:S(2)}) collective-permute-start(bf16[320,2560]{1,0:T(8,128)(2,1)S(1)} %pad_maximum_fusion.2), channel_id=1, source_target_pairs={{0,1},{1,0},{2,3},{3,2},{4,5},{5,4},{6,7},{7,6},{8,9},{9,8},{10,11... | collective-permute-start | bytes 4915208 | tf_op jit(solution)/shard_map/ppermute | solution.py:20
  191.6 45.2 %collective-permute-start.16 = (bf16[160,384]{1,0:T(8,128)(2,1)S(1)}, bf16[160,384]{1,0:T(8,128)(2,1)S(1)}, u32[]{:S(2)}, u32[]{:S(2)}) collective-permute-start(bf16[160,384]{1,0:T(8,128)(2,1)S(1)} %bitcast.548), channel_id=1, source_target_pairs={{0,32},{32,64},{64,96},{96,0},{1,33},{33,65},{65,97},{97,1},{2,34}... | collective-permute-start | bytes 368648 | tf_op jit(solution)/shard_map/ppermute | solution.py:20
  193.3 43.8 %collective-permute-start.17 = (bf16[160,384]{1,0:T(8,128)(2,1)S(1)}, bf16[160,384]{1,0:T(8,128)(2,1)S(1)}, u32[]{:S(2)}, u32[]{:S(2)}) collective-permute-start(bf16[160,384]{1,0:T(8,128)(2,1)S(1)} %bitcast.543), channel_id=1, source_target_pairs={{0,64},{32,96},{64,0},{96,32},{1,65},{33,97},{65,1},{97,33},{2,66}... | collective-permute-start | bytes 368648 | tf_op jit(solution)/shard_map/ppermute | solution.py:20
  195.9 41.4 %collective-permute-start.18 = (bf16[160,384]{1,0:T(8,128)(2,1)S(1)}, bf16[160,384]{1,0:T(8,128)(2,1)S(1)}, u32[]{:S(2)}, u32[]{:S(2)}) collective-permute-start(bf16[160,384]{1,0:T(8,128)(2,1)S(1)} %bitcast.541), channel_id=1, source_target_pairs={{0,96},{32,0},{64,32},{96,64},{1,97},{33,1},{65,33},{97,65},{2,98}... | collective-permute-start | bytes 368648 | tf_op jit(solution)/shard_map/ppermute | solution.py:20
  335.1 26.2 %collective-permute-start.60 = (bf16[320,2560]{1,0:T(8,128)(2,1)}, bf16[320,2560]{1,0:T(8,128)(2,1)}, u32[]{:S(2)}, u32[]{:S(2)}) collective-permute-start(bf16[320,2560]{1,0:T(8,128)(2,1)} %pad_maximum_fusion.4), channel_id=1, source_target_pairs={{0,1},{1,0},{2,3},{3,2},{4,5},{5,4},{6,7},{7,6},{8,9},{9,8},{10,11... | collective-permute-start | bytes 4915208 | tf_op jit(solution)/shard_map/ppermute | solution.py:20
  514.2 30.0 %collective-permute-start.102 = (bf16[80,2560]{1,0:T(8,128)(2,1)}, bf16[80,2560]{1,0:T(8,128)(2,1)S(1)}, u32[]{:S(2)}, u32[]{:S(2)}) collective-permute-start(bf16[80,2560]{1,0:T(8,128)(2,1)} %get-tuple-element.53), channel_id=1, source_target_pairs={{0,96},{32,0},{64,32},{96,64},{1,97},{33,1},{65,33},{97,65},{2,98}... | collective-permute-start | bytes 1228808 | tf_op jit(solution)/shard_map/ppermute | solution.py:20
  514.4 30.7 %collective-permute-start.103 = (bf16[80,2560]{1,0:T(8,128)(2,1)}, bf16[80,2560]{1,0:T(8,128)(2,1)}, u32[]{:S(2)}, u32[]{:S(2)}) collective-permute-start(bf16[80,2560]{1,0:T(8,128)(2,1)} %get-tuple-element.53), channel_id=1, source_target_pairs={{0,64},{32,96},{64,0},{96,32},{1,65},{33,97},{65,1},{97,33},{2,66}... | collective-permute-start | bytes 1228808 | tf_op jit(solution)/shard_map/ppermute | solution.py:20
  514.7 31.3 %collective-permute-start.104 = (bf16[80,2560]{1,0:T(8,128)(2,1)}, bf16[80,2560]{1,0:T(8,128)(2,1)}, u32[]{:S(2)}, u32[]{:S(2)}) collective-permute-start(bf16[80,2560]{1,0:T(8,128)(2,1)} %get-tuple-element.53), channel_id=1, source_target_pairs={{0,32},{32,64},{64,96},{96,0},{1,33},{33,65},{65,97},{97,1},{2,34}... | collective-permute-start | bytes 1228808 | tf_op jit(solution)/shard_map/ppermute | solution.py:20
  517.3 40.7 %collective-permute-start.56 = (bf16[80,2560]{1,0:T(8,128)(2,1)}, bf16[80,2560]{1,0:T(8,128)(2,1)}, u32[]{:S(2)}, u32[]{:S(2)}) collective-permute-start(bf16[80,2560]{1,0:T(8,128)(2,1)} %copy.329), channel_id=1, source_target_pairs={{0,1},{1,0},{2,3},{3,2},{4,5},{5,4},{6,7},{7,6},{8,9},{9,8},{10,11... | collective-permute-start | bytes 1228808 | tf_op jit(solution)/shard_map/ppermute | solution.py:20
  540.3 35.6 %collective-permute-start.66 = (bf16[160,320]{1,0:T(8,128)(2,1)}, bf16[160,320]{1,0:T(8,128)(2,1)}, u32[]{:S(2)}, u32[]{:S(2)}) collective-permute-start(bf16[160,320]{1,0:T(8,128)(2,1)} %bitcast.470), channel_id=1, source_target_pairs={{0,96},{32,0},{64,32},{96,64},{1,97},{33,1},{65,33},{97,65},{2,98}... | collective-permute-start | bytes 307208 | tf_op jit(solution)/shard_map/ppermute | solution.py:20
  544.2 34.4 %collective-permute-start.67 = (bf16[160,320]{1,0:T(8,128)(2,1)}, bf16[160,320]{1,0:T(8,128)(2,1)}, u32[]{:S(2)}, u32[]{:S(2)}) collective-permute-start(bf16[160,320]{1,0:T(8,128)(2,1)} %bitcast.469), channel_id=1, source_target_pairs={{0,64},{32,96},{64,0},{96,32},{1,65},{33,97},{65,1},{97,33},{2,66}... | collective-permute-start | bytes 307208 | tf_op jit(solution)/shard_map/ppermute | solution.py:20
  545.1 33.5 %collective-permute-start.68 = (bf16[160,320]{1,0:T(8,128)(2,1)}, bf16[160,320]{1,0:T(8,128)(2,1)}, u32[]{:S(2)}, u32[]{:S(2)}) collective-permute-start(bf16[160,320]{1,0:T(8,128)(2,1)} %bitcast.468), channel_id=1, source_target_pairs={{0,32},{32,64},{64,96},{96,0},{1,33},{33,65},{65,97},{97,1},{2,34}... | collective-permute-start | bytes 307208 | tf_op jit(solution)/shard_map/ppermute | solution.py:20
  558.0 43.5 %collective-permute-start.69 = (f32[2560,256]{1,0:T(8,128)}, f32[2560,256]{1,0:T(8,128)}, u32[]{:S(2)}, u32[]{:S(2)}) collective-permute-start(f32[2560,256]{1,0:T(8,128)} %get-tuple-element.185), channel_id=1, source_target_pairs={{0,1},{1,0},{2,3},{3,2},{4,5},{5,4},{6,7},{7,6},{8,9},{9,8},{10,11... | collective-permute-start | bytes 7864328 | tf_op jit(solution)/shard_map/ppermute | solution.py:20
  664.2 39.5 %collective-permute-start.85 = (bf16[320,2560]{1,0:T(8,128)(2,1)}, bf16[320,2560]{1,0:T(8,128)(2,1)}, u32[]{:S(2)}, u32[]{:S(2)}) collective-permute-start(bf16[320,2560]{1,0:T(8,128)(2,1)} %slice.484), channel_id=1, source_target_pairs={{0,1},{1,0},{2,3},{3,2},{4,5},{5,4},{6,7},{7,6},{8,9},{9,8},{10,11... | collective-permute-start | bytes 4915208 | tf_op jit(solution)/shard_map/ppermute | solution.py:20
  714.5 29.4 %collective-permute-start.122 = (f32[40,256]{1,0:T(8,128)}, f32[40,256]{1,0:T(8,128)}, u32[]{:S(2)}, u32[]{:S(2)}) collective-permute-start(f32[40,256]{1,0:T(8,128)} %reshape.821), channel_id=1, source_target_pairs={{0,1},{1,0},{2,3},{3,2},{4,5},{5,4},{6,7},{7,6},{8,9},{9,8},{10,11... | collective-permute-start | bytes 122888 | tf_op jit(solution)/shard_map/ppermute | solution.py:20
  (178 other events, 2334.8 us)
Sparse Core Ops, SparseCore 0:
  46.0 138.8 all-gather.1
  438.6 100.5 reduce-scatter.3

commit v2 on v1

v2 whole, which is shorter than its diff:
```python
import functools

import jax
import jax.numpy as jnp
from jax import lax
from jax.experimental import pallas as pl
from jax.experimental.pallas import tpu as pltpu
from jax.sharding import Mesh
from jax.sharding import PartitionSpec as P

WINDOW = 2048
SHARD_CONTEXT = ("shard", "context_0", "context_1")
CONTEXT = ("context_0", "context_1")
PIECES = ("context_0", "context_1", "shard")
Y, X, Z, T = "shard", "context_0", "context_1", "tensor"
VMEM = pltpu.CompilerParams(vmem_limit_bytes=48 * 2**20)

EPSILON = 1e-06
NEGATIVE_FILL = -1e30
BF = jnp.bfloat16
F32 = jnp.float32


def shift(x, axis, by):
    n = lax.axis_size(axis)
    return lax.ppermute(x, axis, [(i, (i + by) % n) for i in range(n)])


def exchange(blocks, axis):
    return lax.all_to_all(blocks, axis, 0, 0, tiled=True)


def after(x, *others):
    return lax.optimization_barrier((x, *others))[0]


def ring_blocks(x, axis):
    return [x, shift(x, axis, -1), shift(x, axis, 2), shift(x, axis, 1)]


def place_kernel(axis, sign, lead, *refs):
    blocks, out, sems = refs[:-2], refs[-2], refs[-1]
    me = lax.axis_index(axis)
    copies = []
    for i, block in enumerate(blocks):
        first, rows, r = lead[i]
        j = lax.rem(me + (sign * r) % 4, 4)
        dst = out.at[j] if first is None else out.at[pl.ds(first, rows), j]
        copies.append(pltpu.make_async_copy(block, dst, sems.at[i]))
    for copy in copies:
        copy.start()
    for copy in copies:
        copy.wait()


def place(blocks, axis, shape, sign=1, lead=None):
    if lead is None:
        lead = [(None, 0, r) for r in range(4)]
    return pl.pallas_call(
        functools.partial(place_kernel, axis, sign, lead),
        out_shape=jax.ShapeDtypeStruct(shape, blocks[0].dtype),
        in_specs=[pl.BlockSpec(memory_space=pl.ANY)] * len(blocks),
        out_specs=pl.BlockSpec(memory_space=pl.ANY),
        scratch_shapes=[pltpu.SemaphoreType.DMA((len(blocks),))],
        compiler_params=VMEM,
    )(*blocks)


def gather_rows(mine):
    own = jnp.concatenate(ring_blocks(mine, Y), axis=0)
    return own, shift(own, T, 1)


def scatter_rows(own, other, weight, db):
    far = dot(other, weight, 1, db).astype(BF)
    low = (dot(own, weight, 1, db) + shift(far, T, 1).astype(F32)).astype(BF)
    total = low[:80].astype(F32)
    for r in (1, 3, 2):
        total = total + shift(low[80 * r : 80 * r + 80], Y, r).astype(F32)
    return total, low


def rows_home(own, other):
    blocks = []
    for r in range(4):
        block = jnp.concatenate([own[80 * r : 80 * r + 80], other[80 * r : 80 * r + 80]])
        blocks.append(shift(block, Y, r) if r else block)
    return place(blocks, Y, (4, *blocks[0].shape), sign=-1)


def columns_out(blocks):
    me = lax.axis_index(Y)
    got = [None] * 4
    for r in range(4):
        block = lax.dynamic_index_in_dim(blocks, (me + r) % 4, 0, keepdims=False)
        got[(4 - r) % 4] = shift(block, Y, r) if r else block
    return jnp.concatenate([b[:80] for b in got]), jnp.concatenate([b[80:] for b in got])


def gather_output(w_output):
    line = place(ring_blocks(w_output, X), X, (4, 40, 1280))
    lead = [(0, 4, r) for r in range(4)]
    plane = place(ring_blocks(line, Z), Z, (4, 4, 40, 1280), lead=lead).reshape(16, 40, 1280)
    before, behind = shift(plane, Y, 1), shift(plane, Y, -1)
    far_one, far_two = shift(before[:8], Y, 1), shift(behind[8:], Y, -1)
    lead = [(0, 16, 0), (0, 16, 1), (0, 16, 3), (0, 8, 2), (8, 8, 2)]
    blocks = (plane, behind, before, far_one, far_two)
    return place(blocks, Y, (16, 4, 40, 1280), lead=lead).reshape(2560, 1280)


def summed_over(parts, axis, dim):
    me = lax.axis_index(axis)
    total = lax.dynamic_index_in_dim(parts, me, dim, keepdims=False).astype(F32)
    for r in (1, 3, 2):
        block = lax.dynamic_index_in_dim(parts, (me + r) % 4, dim, keepdims=False)
        total = total + shift(block, axis, r).astype(F32)
    return total


def quarters(x):
    rows = x.shape[0]
    return x.reshape(rows, 4, -1).swapaxes(0, 1)


def joined(blocks):
    return blocks.swapaxes(0, 1).reshape(blocks.shape[1], -1)


def pack_kernel(q_ref, kv_ref, gains_ref, gate_ref, up_ref, down_ref, attn_ref, mlp_ref):
    attn_ref[...] = jnp.zeros_like(attn_ref)
    mlp_ref[...] = jnp.zeros_like(mlp_ref)
    for j in range(4):
        attn_ref[j, :40, :320] = q_ref[:, 320 * j : 320 * j + 320]
        attn_ref[j, :40, 320:] = kv_ref[:, 64 * j : 64 * j + 64]
        attn_ref[j, 40:48, :128] = gains_ref[...]
        mlp_ref[j, :, :960] = gate_ref[:, 960 * j : 960 * j + 960]
        mlp_ref[j, :, 1024:1984] = up_ref[:, 960 * j : 960 * j + 960]
        mlp_ref[j, :, 2048:3008] = down_ref[:, 960 * j : 960 * j + 960]


def pack(w_query, keyval_half, gains, w_gate, w_up, w_down):
    return pl.pallas_call(
        pack_kernel,
        out_shape=(
            jax.ShapeDtypeStruct((4, 48, 384), BF),
            jax.ShapeDtypeStruct((4, 40, 3072), BF),
        ),
        compiler_params=VMEM,
    )(w_query, keyval_half, gains, w_gate, w_up, w_down)


def mlp_grad_kernel(xa, xb, ya, yb, ga, gb, ha, hb, out):
    j = pl.program_id(1)

    def product(left_a, left_b, right_a, right_b):
        out[...] = (dot(left_a[...], right_a[...], 0, 0) + dot(left_b[...], right_b[...], 0, 0)).astype(BF)

    @pl.when(j < 2)
    def _():
        product(xa, xb, ga, gb)

    @pl.when(j == 2)
    def _():
        product(ya, yb, ha, hb)


def mlp_grads(normed, grads, gate_up, hidden):
    rows = 256
    left = pl.BlockSpec((320, rows), lambda i, j: (0, i))
    pair = pl.BlockSpec((320, 1024), lambda i, j: (0, jnp.minimum(j, 1)))
    whole = pl.BlockSpec((320, 1024), lambda i, j: (0, 0))
    return pl.pallas_call(
        mlp_grad_kernel,
        grid=(2560 // rows, 3),
        out_shape=jax.ShapeDtypeStruct((2560, 3072), BF),
        in_specs=[left, left, left, left, pair, pair, whole, whole],
        out_specs=pl.BlockSpec((rows, 1024), lambda i, j: (i, j)),
        compiler_params=VMEM,
        cost_estimate=pl.CostEstimate(flops=2 * 640 * 2560 * 3072, bytes_accessed=2 * 2560 * 3072, transcendentals=0),
    )(*normed, *grads, *gate_up, *hidden)


def to_piece_order(x):
    rows = x.shape[0]
    return x.reshape(rows, 4, 16, 40).swapaxes(1, 2).reshape(rows, 2560)


def from_piece_order(x):
    rows = x.shape[0]
    return x.reshape(rows, 16, 4, 40).swapaxes(1, 2).reshape(rows, 2560)


def halves_home(mine, t):
    other = shift(mine, T, 1)
    return jnp.where(t == 0, jnp.concatenate([mine, other]), jnp.concatenate([other, mine]))


def inverse_root(values):
    return lax.rsqrt(jnp.mean(values * values, axis=-1, keepdims=True) + EPSILON)


def norm_back(grad, values, inverse, gain):
    scaled = gain * grad
    return inverse * scaled - values * inverse**3 * jnp.mean(
        scaled * values, axis=-1, keepdims=True
    )


def angles(position, head_dim):
    quarter = head_dim // 4
    frequency = 10000.0 ** (-jnp.arange(quarter, dtype=F32) / quarter)
    phase_angle = position[:, None].astype(F32) * frequency[None, :]
    return (jnp.cos(phase_angle), jnp.sin(phase_angle))


def rotate(values, cosine, sine_part):
    quarter = cosine.shape[-1]
    first_half = values[..., :quarter]
    second = values[..., quarter : 2 * quarter]
    cos_rows = cosine[:, None, :]
    sin_rows = sine_part[:, None, :]
    return jnp.concatenate(
        [
            first_half * cos_rows - second * sin_rows,
            second * cos_rows + first_half * sin_rows,
            values[..., 2 * quarter :],
        ],
        axis=-1,
    )


def dot(a, b, da, db):
    return lax.dot_general(a, b, (((da,), (db,)), ((), ())), preferred_element_type=F32)


def feed_forward(gate_up, grad_hidden):
    gate_pre, up_pre = gate_up[:, :1024], gate_up[:, 1024:]
    activated, gelu_pull = jax.vjp(jax.nn.gelu, gate_pre)
    hidden = (activated * up_pre).astype(BF)
    grad_gate = gelu_pull(grad_hidden * up_pre)[0].astype(BF)
    grad_up = (grad_hidden * activated).astype(BF)
    return hidden, jnp.concatenate([grad_gate, grad_up], axis=1)


def shards(
    tokens,
    lengths,
    attn_gain,
    w_query,
    w_keyval,
    w_output,
    mlp_gain,
    w_gate,
    w_up,
    w_down,
    cotangent,
):
    t = lax.axis_index(T)
    piece = lax.axis_index(CONTEXT)
    head_dim = 256
    query_scale = head_dim ** (-0.5)
    seq_count = 2560
    padding = seq_count - lengths[0]
    row_start = piece * 160
    natural = row_start + jnp.arange(160, dtype=jnp.int32)
    turned = row_start + (jnp.arange(160, dtype=jnp.int32) + t * 80) % 160
    live_turned = turned >= padding
    live_mine = live_turned[:80, None]

    x_low = to_piece_order(lax.dynamic_slice_in_dim(tokens[0], t * 80, 80, 0))
    cot_mine = to_piece_order(lax.dynamic_slice_in_dim(cotangent[0], t * 80, 80, 0))
    grad_mine = jnp.where(live_mine, cot_mine, jnp.zeros_like(cot_mine))
    x_mine = x_low.astype(F32)
    x_halves = gather_rows(x_low)

    keyval_half = lax.dynamic_slice_in_dim(w_keyval, t * 256, 256, 1)
    gains = jnp.concatenate([attn_gain, mlp_gain])[None, :]
    gains = jnp.pad(gains, ((0, 7), (0, 48)))
    attn_blocks, mlp_blocks = pack(w_query, keyval_half, gains, w_gate, w_up, w_down)
    attn_copies = jnp.broadcast_to(attn_blocks[None], (16, 4, 48, 384)).reshape(64, 48, 384)
    attn_all = exchange(attn_copies, PIECES)
    w_qkv = attn_all[:, :40].reshape(2560, 384)
    gain_one = attn_all[:, 40, :40].reshape(1, 2560).astype(F32)
    gain_two = attn_all[:, 40, 40:80].reshape(1, 2560).astype(F32)
    me = lax.axis_index(Y)
    mlp_got = []
    for r in range(4):
        block = lax.dynamic_index_in_dim(mlp_blocks, (me + r) % 4, 0, keepdims=False)
        mlp_got.append(shift(block, Y, r) if r else block)
    mlp_block = place(mlp_got, Y, (4, 40, 3072), sign=-1).reshape(160, 3072)
    w_mlp = lax.all_gather(mlp_block, CONTEXT, axis=0, tiled=True)
    w_gate_up = w_mlp[:, :2048]
    w_down_all = w_mlp[:, 2048:]
    w_out = gather_output(after(w_output, mlp_blocks))

    normed, projected = [], []
    for x_half in x_halves:
        x_rows = x_half.astype(F32)
        normed.append((x_rows * inverse_root(x_rows) * gain_one).astype(BF))
        projected.append(dot(normed[-1], w_qkv, 1, 0).astype(BF))
    home = rows_home(*projected)
    query_pre = joined(home[:, :, :320]).reshape(160, 5, head_dim).astype(F32)
    cosine, sine_part = angles(turned - padding, head_dim)
    queries = (rotate(query_pre, cosine, sine_part) * query_scale).astype(BF)
    keyval_turned = joined(home[:, :, 320:])
    keyval_own = jnp.where(
        t == 0, keyval_turned, jnp.concatenate([keyval_turned[80:], keyval_turned[:80]])
    )
    cosine_nat, sine_nat = angles(natural - padding, head_dim)
    keys_own = rotate(keyval_own[:, None].astype(F32), cosine_nat, sine_nat)[:, 0].astype(BF)
    kv_own = jnp.where(t == 0, keys_own, keyval_own)
    kv_mine = exchange(jnp.broadcast_to(kv_own[None], (16, 160, 256)), CONTEXT).reshape(2560, 256)
    kv_other = shift(kv_mine, T, 1)
    keys = jnp.where(t == 0, kv_mine, kv_other)
    values = jnp.where(t == 0, kv_other, kv_mine)

    key_index = jnp.arange(seq_count, dtype=jnp.int32)
    offset = turned[:, None] - key_index[None, :]
    allowed = ((offset >= 0) & (offset < WINDOW) & (key_index >= padding)[None, :])[None]
    live = live_turned[None, :, None]
    scores = jnp.einsum("qhd,kd->hqk", queries, keys, preferred_element_type=F32)
    row_top = jnp.max(jnp.where(allowed, scores, NEGATIVE_FILL), axis=-1, keepdims=True)
    row_top = jnp.where(live, row_top, 0.0)
    weights_exp = jnp.where(allowed, jnp.exp(scores - row_top), 0.0)
    row_total = jnp.where(live, jnp.sum(weights_exp, axis=-1, keepdims=True), 1.0)
    prob = weights_exp / row_total
    prob_low = prob.astype(BF)
    attended = jnp.einsum("hqk,kd->qhd", prob_low, values, preferred_element_type=F32)
    attended = attended.reshape(160, 1280).astype(BF)

    branch = dot(attended, w_out, 1, 1)
    hidden_mine = x_mine + branch[:80] + shift(branch[80:], T, 1)

    inverse_two = inverse_root(hidden_mine)
    grad_halves = gather_rows(after(grad_mine, w_out))
    grad_halves = lax.optimization_barrier((*grad_halves, branch))[:2]
    normed_two = gather_rows((hidden_mine * inverse_two * gain_two).astype(BF))
    attended_halves = columns_out(quarters(after(attended, *normed_two)))
    hidden, grad_gate_up = [None, None], [None, None]
    for i in (0, 1):
        gate_up = dot(normed_two[i], w_gate_up, 1, 0)
        grad_hidden = dot(grad_halves[i], w_down_all, 1, 0)
        hidden[i], grad_gate_up[i] = feed_forward(gate_up, grad_hidden)
    grad_normed_two, normed_two_low = scatter_rows(*grad_gate_up, w_gate_up, 1)

    late = lax.optimization_barrier((*grad_gate_up, *hidden, normed_two_low))
    mlp_part = mlp_grads(normed_two, grad_halves, late[:2], late[2:4])
    mlp_sum = lax.psum_scatter(mlp_part, CONTEXT, scatter_dimension=0, tiled=True)

    grad_h_mine = grad_mine.astype(F32) + norm_back(
        grad_normed_two, hidden_mine, inverse_two, gain_two
    )
    branch_mine = grad_h_mine.astype(BF)
    branch_low = jnp.concatenate([branch_mine, shift(branch_mine, T, 1)])
    grad_attended = dot(branch_low, w_out, 1, 0).astype(BF).reshape(160, 5, head_dim)
    branch_halves = gather_rows(branch_mine)

    grad_prob = jnp.einsum("qhd,kd->hqk", grad_attended, values, preferred_element_type=F32)
    spread = jnp.sum(prob * grad_prob, axis=-1, keepdims=True)
    grad_scores = (prob * (grad_prob - spread)).astype(BF)
    grad_queries = jnp.einsum("hqk,kd->qhd", grad_scores, keys, preferred_element_type=F32)
    grad_query_pre = (
        rotate(grad_queries * query_scale, cosine, -sine_part).reshape(160, 1280).astype(BF)
    )
    grad_scores_late = after(grad_scores, grad_query_pre)
    grad_query_halves = columns_out(quarters(grad_query_pre))
    grad_keys = jnp.einsum(
        "hqk,qhd->kd", grad_scores_late, queries, preferred_element_type=F32
    )
    grad_values = jnp.einsum("hqk,qhd->kd", prob_low, grad_attended, preferred_element_type=F32)
    keep = jnp.where(t == 0, grad_keys, grad_values)
    give = jnp.where(t == 0, grad_values, grad_keys).astype(BF)
    kv_part = (keep + shift(give, T, 1).astype(F32)).astype(BF).reshape(4, 4, 160, 256)
    kv_line = summed_over(kv_part, X, 0).astype(BF)
    kv_sum = summed_over(kv_line, Z, 0)

    output_halves = lax.optimization_barrier((*branch_halves, kv_part))[:2]
    output_part = sum(dot(output_halves[i], attended_halves[i], 0, 0) for i in (0, 1))
    output_home = exchange(output_part.astype(BF).reshape(64, 40, 320), PIECES)

    keys_back = rotate(kv_sum[:, None], cosine_nat, -sine_nat)[:, 0]
    kv_back = jnp.where(t == 0, keys_back, kv_sum).astype(BF)
    kv_back = jnp.where(t == 0, kv_back, jnp.concatenate([kv_back[80:], kv_back[:80]]))
    grad_kv_halves = columns_out(quarters(kv_back))
    grad_qkv = [
        jnp.concatenate([q, kv], axis=1) for q, kv in zip(grad_query_halves, grad_kv_halves)
    ]
    qkv_part = sum(dot(normed[i], grad_qkv[i], 0, 0) for i in (0, 1))
    qkv_home = exchange(qkv_part.astype(BF).reshape(64, 40, 384), PIECES)
    grad_normed, _ = scatter_rows(*grad_qkv, w_qkv, 1)
    inverse_one = inverse_root(x_mine)
    tokens_mine = grad_h_mine + norm_back(grad_normed, x_mine, inverse_one, gain_one)
    tokens_grad = halves_home(from_piece_order(tokens_mine.astype(BF)), t)

    hidden_late = lax.optimization_barrier((*hidden, kv_part))[:2]
    mlp_mine, _ = scatter_rows(*hidden_late, w_down_all, 1)
    block_mine = jnp.where(live_mine, hidden_mine + mlp_mine, 0.0).astype(BF)
    block_out = halves_home(from_piece_order(block_mine), t)

    def owned(home):
        return joined(jnp.sum(home.reshape(16, 4, 40, -1).astype(F32), axis=0))

    query_grad = owned(qkv_home[:, :, :320])
    kv_grad_half = owned(qkv_home[:, :, 320:])
    output_grad = owned(output_home)
    kv_grad_other = shift(kv_grad_half, T, 1)
    keyval_grad = jnp.where(
        t == 0,
        jnp.concatenate([kv_grad_half, kv_grad_other], axis=1),
        jnp.concatenate([kv_grad_other, kv_grad_half], axis=1),
    )
    mlp_got = []
    mlp_rows = mlp_sum.reshape(4, 40, 3072)
    for r in range(4):
        block = lax.dynamic_index_in_dim(mlp_rows, (me + r) % 4, 0, keepdims=False)
        mlp_got.append(shift(block, Y, r) if r else block)
    mlp_home = place(mlp_got, Y, (4, 40, 3072), sign=-1).astype(F32)
    gate_grad = joined(mlp_home[:, :, :960])
    up_grad = joined(mlp_home[:, :, 1024:1984])
    down_grad = joined(mlp_home[:, :, 2048:3008])

    one_part = jnp.sum(w_query.astype(F32) * query_grad, axis=1) + jnp.sum(
        keyval_half.astype(F32) * kv_grad_half, axis=1
    )
    two_part = jnp.sum(w_gate.astype(F32) * gate_grad + w_up.astype(F32) * up_grad, axis=1)
    both = jnp.stack([one_part, two_part])
    both = both + shift(both, T, 1)
    attn_gain_grad = both[0] / attn_gain.astype(F32)
    mlp_gain_grad = both[1] / mlp_gain.astype(F32)

    return (
        block_out[None],
        tokens_grad[None],
        attn_gain_grad,
        query_grad,
        keyval_grad,
        output_grad,
        mlp_gain_grad,
        gate_grad,
        up_grad,
        down_grad,
    )


def solution(mesh):
    torus = Mesh(
        mesh.devices.reshape(mesh.shape["shard"], 4, 4, mesh.shape["tensor"]),
        ("shard", "context_0", "context_1", "tensor"),
    )
    in_specs = (
        P("shard", CONTEXT, None),
        P("shard"),
        P(SHARD_CONTEXT),
        P(SHARD_CONTEXT, "tensor"),
        P(SHARD_CONTEXT, None),
        P(SHARD_CONTEXT, "tensor"),
        P(SHARD_CONTEXT),
        P(SHARD_CONTEXT, "tensor"),
        P(SHARD_CONTEXT, "tensor"),
        P(SHARD_CONTEXT, "tensor"),
        P("shard", CONTEXT, None),
    )
    out_specs = (
        P("shard", CONTEXT, None),
        P("shard", CONTEXT, None),
        P(SHARD_CONTEXT),
        P(SHARD_CONTEXT, "tensor"),
        P(SHARD_CONTEXT, None),
        P(SHARD_CONTEXT, "tensor"),
        P(SHARD_CONTEXT),
        P(SHARD_CONTEXT, "tensor"),
        P(SHARD_CONTEXT, "tensor"),
        P(SHARD_CONTEXT, "tensor"),
    )
    return jax.shard_map(
        shards, mesh=torus, in_specs=in_specs, out_specs=out_specs, check_vma=False
    )
```

time: 777 us -> 771 us (level)
  Pallas kernels: 0 us -> 134 us
  starting transfers between devices: 231 us -> 145 us
  local copies, waits for them, and re-layouts: 168 us -> 94.5 us
  waiting for transfers between devices: 181 us -> 223 us
  other arithmetic: 68.9 us -> 43.9 us
    pallas_call x0 -> x8, Pallas kernels: none -> 134 us  [the longest x6 104 us: place(): pl.pallas_call(functools.partial(place_kernel, axis, sign, lead), out_sha...]
    ppermute x123 -> x70, starting transfers between devices: 216 us -> 114 us  [shift(): return lax.ppermute(x, axis, [(i, (i + by) % n) for i in range(n)])]
    dynamic_update_slice x55 -> x0, local copies, waits for them, and re-layouts: 58.1 us -> none  [the longest x51 45 us: placed(): out = lax.dynamic_update_slice(out, jnp.expand_dims(block, dim), start)]
    ppermute x123 -> x70, waiting for transfers between devices: 173 us -> 211 us  [shift(): return lax.ppermute(x, axis, [(i, (i + by) % n) for i in range(n)])]
    unnamed x188 -> x219, local copies, waits for them, and re-layouts: 45.7 us -> 24.3 us
    concatenate x5 -> x6, other arithmetic: 16.9 us -> 0.26 us  [the longest x2 0.21 us: feed_forward(): return (hidden, jnp.concatenate([grad_gate, grad_up], axis=1))]
    all_to_all x4, starting transfers between devices: 15.2 us -> 31.6 us  [exchange(): return lax.all_to_all(blocks, axis, 0, 0, tiled=True)]
    dot_general x12 -> x18, matrix products: 73.9 us -> 78.6 us  [dot(): lax.dot_general(a, b, (((da,), (db,)), ((), ())), preferred_element_type=...]
  transfers between devices with their start and end apart: 129 -> 76, of which waited for: 41 -> 27; matrix products, arithmetic and copies ran while one was open for 32% -> 24% of each run, Pallas kernels for 0% -> 13%
where the time goes in v2:
time: 771 us; the launch traced here: 757 us
  waiting for transfers between devices  223 us (29%)
  starting transfers between devices  145 us (19%)
  Pallas kernels  134 us (17%)
  matrix products  99.3 us (13%)
  local copies, waits for them, and re-layouts  94.5 us (12%)
  other arithmetic  43.9 us (6%)
  between operations  17.2 us (2%)
    ppermute x70, waiting for transfers between devices, shift(): return lax.ppermute(x, axis, [(i, (i + by) % n) for i in range(n)])  211 us
    ppermute x70, starting transfers between devices, shift(): return lax.ppermute(x, axis, [(i, (i + by) % n) for i in range(n)])  114 us
    pallas_call x6, Pallas kernels, place(): pl.pallas_call(functools.partial(place_kernel, axis, sign, lead), out_sha...  104 us
    dot_general x18, matrix products, dot(): lax.dot_general(a, b, (((da,), (db,)), ((), ())), preferred_element_type=...  78.6 us
    all_to_all x4, starting transfers between devices, exchange(): return lax.all_to_all(blocks, axis, 0, 0, tiled=True)  31.6 us
    pallas_call x1, Pallas kernels, mlp_grads(): pl.pallas_call(mlp_grad_kernel, grid=(2560 // rows, 3), out_shape=jax.Sha...  29.5 us
    unnamed x219, local copies, waits for them, and re-layouts  24.3 us
  transfers between devices with their start and end apart: 76, of which 27 were waited for; matrix products, arithmetic and copies ran while one was open for 24% of the time, Pallas kernels for 13%

profile of v2, /device:TPU:1, one launch (start us, length us, event | category | flops | bytes accessed | tf_op | source)
XLA Modules:
  0.0 756.8 jit_solution(8174232825575615497)
XLA Ops:
  22.1 6.3 collective-permute-done.23.refs_2_
  36.8 9.7 %all-to-all-start = ((bf16[64,48,384]{2,1,0:T(8,128)(2,1)}), bf16[64,48,384]{2,1,0:T(8,128)(2,1)S(1)}, u32[]{:S(2)}, u32[]{:S(2)}) async-start(bf16[64,48,384]{2,1,0:T(8,128)(2,1)} %bitcast.5), calls=%async_computation | async-start | bytes 4718592 | tf_op jit(solution)/shard_map/all_to_all | solution.py:30
  48.6 5.6 collective-permute-done.1
  64.9 6.2 collective-permute-start.3
  81.9 7.7 %all-to-all-done = bf16[64,48,384]{2,1,0:T(8,128)(2,1)S(1)} async-done(((bf16[64,48,384]{2,1,0:T(8,128)(2,1)}), bf16[64,48,384]{2,1,0:T(8,128)(2,1)S(1)}, u32[]{:S(2)}, u32[]{:S(2)}) %all-to-all-start) | async-done | bytes 2359328 | tf_op jit(solution)/shard_map/all_to_all | solution.py:30
  117.3 32.3 %collective-permute-done.11.refs_1_ = bf16[4,40,1280]{2,1,0:T(8,128)(2,1)S(1)} collective-permute-done((bf16[4,40,1280]{2,1,0:T(8,128)(2,1)S(1)}, bf16[4,40,1280]{2,1,0:T(8,128)(2,1)S(1)}, u32[]{:S(2)}, u32[]{:S(2)}) %collective-permute-start.11) | collective-permute-done | bytes 409632 | tf_op jit(solution)/shard_map/ppermute | solution.py:26
  151.0 14.1 %collective-permute-done.13.refs_3_ = bf16[4,40,1280]{2,1,0:T(8,128)(2,1)S(1)} collective-permute-done((bf16[4,40,1280]{2,1,0:T(8,128)(2,1)S(1)}, bf16[4,40,1280]{2,1,0:T(8,128)(2,1)S(1)}, u32[]{:S(2)}, u32[]{:S(2)}) %collective-permute-start.13) | collective-permute-done | bytes 409632 | tf_op jit(solution)/shard_map/ppermute | solution.py:26
  174.2 26.1 %collective-permute-done.15.refs_2_ = bf16[16,40,1280]{2,1,0:T(8,128)(2,1)} collective-permute-done((bf16[16,40,1280]{2,1,0:T(8,128)(2,1)S(1)}, bf16[16,40,1280]{2,1,0:T(8,128)(2,1)}, u32[]{:S(2)}, u32[]{:S(2)}) %collective-permute-start.15) | collective-permute-done | bytes 1638432 | tf_op jit(solution)/shard_map/ppermute | solution.py:26
  220.0 100.4 %shard_map.190 = bf16[16,4,40,1280]{3,2,1,0:T(8,128)(2,1)} custom-call(bf16[16,40,1280]{2,1,0:T(8,128)(2,1)S(1)} %bitcast.254, bf16[16,40,1280]{2,1,0:T(8,128)(2,1)S(1)} %collective-permute-done.14.refs_1_, bf16[16,40,1280]{2,1,0:T(8,128)(2,1)} %collective-permute-done.15.refs_2_, bf16[8,40,1280]{2,1,0:T(8,128)(2,1)} %collective-permute-done.16.refs_3_, ...), custom_call_target="tpu_custom_call" | custom-call | tf_op jit(solution)/shard_map/pallas_call | solution.py:59
  334.7 5.2 collective-permute-start.18
  344.1 16.9 %collective-permute-done.26 = bf16[80,2560]{1,0:T(8,128)(2,1)} collective-permute-done((bf16[80,2560]{1,0:T(8,128)(2,1)S(1)}, bf16[80,2560]{1,0:T(8,128)(2,1)}, u32[]{:S(2)}, u32[]{:S(2)}) %collective-permute-start.26) | collective-permute-done | bytes 409632 | tf_op jit(solution)/shard_map/ppermute | solution.py:26
  370.6 6.2 collective-permute-done.21
  376.8 9.6 %collective-permute-done.20 = bf16[80,2560]{1,0:T(8,128)(2,1)S(1)} collective-permute-done((bf16[80,2560]{1,0:T(8,128)(2,1)S(1)}, bf16[80,2560]{1,0:T(8,128)(2,1)S(1)}, u32[]{:S(2)}, u32[]{:S(2)}) %collective-permute-start.20) | collective-permute-done | bytes 409632 | tf_op jit(solution)/shard_map/ppermute | solution.py:26
  392.4 6.9 fusion.10
  399.3 5.2 fusion.61
  404.5 7.8 %fusion.26 = bf16[320,2560]{1,0:T(8,128)(2,1)S(1)} fusion(bf16[2560,3072]{1,0:T(8,128)(2,1)} %all-gather.2.cloned.1.call-done, bf16[320,1024]{1,0:T(8,128)(2,1)S(1)} %get-tuple-element.93, bf16[320,1024]{1,0:T(8,128)(2,1)S(1)} %get-tuple-element.92), kind=kOutput, calls=%fused_computation.36 | convolution fusion | flops 3358883840 | bytes 13434880 | tf_op jit(solution)/shard_map/dot_general | solution.py:233
  413.1 6.4 fusion.12
  421.0 5.2 fusion.54
  426.3 8.7 %fusion.21 = bf16[320,2560]{1,0:T(8,128)(2,1)} fusion(bf16[2560,3072]{1,0:T(8,128)(2,1)} %all-gather.2.cloned.1.call-done, bf16[320,2560]{1,0:T(8,128)(2,1)S(1)} %collective-permute-done.30, bf16[320,1024]{1,0:T(8,128)(2,1)S(1)} %get-tuple-element.91, bf16[320,1024]{1,0:T(8,128)(2,1)S(1)} %get-tuple-element.90), kind=kOutput, calls=%fused_computation.33 | convolution fusion | flops 3360522240 | bytes 15073280 | tf_op jit(solution)/shard_map/dot_general | solution.py:233
  435.0 29.5 %shard_map.192 = bf16[2560,3072]{1,0:T(8,128)(2,1)} custom-call(bf16[320,2560]{1,0:T(8,128)(2,1)S(1)} %pad_maximum_fusion.1.xa, bf16[320,2560]{1,0:T(8,128)(2,1)} %collective-permute-done.25.xb, bf16[320,2560]{1,0:T(8,128)(2,1)} %copy-done.64, bf16[320,2560]{1,0:T(8,128)(2,1)} %copy-done.94, bf16[320,2048]{1,0:T(8,128)(2,1)S(1)} %pad_maximum_fusion.3.ga, ...), custom_call_target="tpu_custom_call" | custom-call | flops 10066329600 | bytes 15728640 | tf_op jit(solution)/shard_map/pallas_call | solution.py:172
  478.5 7.7 %collective-permute-done.33 = bf16[80,2560]{1,0:T(8,128)(2,1)S(1)} collective-permute-done((bf16[80,2560]{1,0:T(8,128)(2,1)S(1)}, bf16[80,2560]{1,0:T(8,128)(2,1)S(1)}, u32[]{:S(2)}, u32[]{:S(2)}) %collective-permute-start.33) | collective-permute-done | bytes 409632 | tf_op jit(solution)/shard_map/ppermute | solution.py:26
  486.2 6.1 collective-permute-done.32
  548.5 5.6 convolution_convert_fusion.1
  559.7 22.6 %collective-permute-done.45 = bf16[4,160,256]{1,2,0:T(8,128)(2,1)S(1)} collective-permute-done((bf16[4,160,256]{1,2,0:T(8,128)(2,1)}, bf16[4,160,256]{1,2,0:T(8,128)(2,1)S(1)}, u32[]{:S(2)}, u32[]{:S(2)}) %collective-permute-start.45) | collective-permute-done | bytes 327712 | tf_op jit(solution)/shard_map/ppermute | solution.py:26
  583.8 6.2 collective-permute-start.49
  604.8 6.9 all-to-all-start.3
  618.6 13.8 %collective-permute-done.52 = bf16[160,64]{1,0:T(8,128)(2,1)S(1)} collective-permute-done((bf16[160,64]{1,0:T(8,128)(2,1)S(1)}, bf16[160,64]{1,0:T(8,128)(2,1)S(1)}, u32[]{:S(2)}, u32[]{:S(2)}) %collective-permute-start.52) | collective-permute-done | bytes 20512 | tf_op jit(solution)/shard_map/ppermute | solution.py:26
  636.4 5.9 collective-permute-start.53
  655.6 10.6 %all-to-all-start.2 = ((bf16[64,40,384]{2,1,0:T(8,128)(2,1)}), bf16[64,40,384]{2,1,0:T(8,128)(2,1)}, u32[]{:S(2)}, u32[]{:S(2)}) async-start(bf16[64,40,384]{2,1,0:T(8,128)(2,1)} %bitcast.284), calls=%async_computation.2 | async-start | bytes 3932160 | tf_op jit(solution)/shard_map/all_to_all | solution.py:30
  670.4 11.2 %collective-permute-done.37 = bf16[80,2560]{1,0:T(8,128)(2,1)S(1)} collective-permute-done((bf16[80,2560]{1,0:T(8,128)(2,1)S(1)}, bf16[80,2560]{1,0:T(8,128)(2,1)S(1)}, u32[]{:S(2)}, u32[]{:S(2)}) %collective-permute-start.37) | collective-permute-done | bytes 409632 | tf_op jit(solution)/shard_map/ppermute | solution.py:26
  705.6 5.3 collective-permute-done.55
  727.6 6.6 collective-permute-done.58.refs_1_
  (532 shorter events, 315.3 us)
Async XLA Ops:
  7.2 385.2 %all-gather.2.cloned.1.call-start = ((), (), s32[]{:S(2)}) async-start(), calls=%async_computation.5 | async-start | bytes 16711680 | tf_op jit(solution)/shard_map/all_gather | solution.py:291
  32.2 21.9 %collective-permute-start.1 = (bf16[80,2560]{1,0:T(8,128)(2,1)S(1)}, bf16[80,2560]{1,0:T(8,128)(2,1)S(1)}, u32[]{:S(2)}, u32[]{:S(2)}) collective-permute-start(bf16[80,2560]{1,0:T(8,128)(2,1)S(1)} %copy.181), channel_id=1, source_target_pairs={{0,64},{32,96},{64,0},{96,32},{1,65},{33,97},{65,1},{97,33},{2,66}... | collective-permute-start | bytes 1228808 | tf_op jit(solution)/shard_map/ppermute | solution.py:26
  36.8 52.8 %all-to-all-start = ((bf16[64,48,384]{2,1,0:T(8,128)(2,1)}), bf16[64,48,384]{2,1,0:T(8,128)(2,1)S(1)}, u32[]{:S(2)}, u32[]{:S(2)}) async-start(bf16[64,48,384]{2,1,0:T(8,128)(2,1)} %bitcast.5), calls=%async_computation | async-start | bytes 4718592 | tf_op jit(solution)/shard_map/all_to_all | solution.py:30
  71.1 41.9 %collective-permute-start.8 = (bf16[40,1280]{1,0:T(8,128)(2,1)S(1)}, bf16[40,1280]{1,0:T(8,128)(2,1)S(1)}, u32[]{:S(2)}, u32[]{:S(2)}) collective-permute-start(bf16[40,1280]{1,0:T(8,128)(2,1)S(1)} %copy-done.8), channel_id=1, source_target_pairs={{0,24},{8,0},{16,8},{24,16},{1,25},{9,1},{17,9},{25,17},{2,26},{10... | collective-permute-start | bytes 307208 | tf_op jit(solution)/shard_map/ppermute | solution.py:26
  73.2 39.8 %collective-permute-start.9 = (bf16[40,1280]{1,0:T(8,128)(2,1)S(1)}, bf16[40,1280]{1,0:T(8,128)(2,1)S(1)}, u32[]{:S(2)}, u32[]{:S(2)}) collective-permute-start(bf16[40,1280]{1,0:T(8,128)(2,1)S(1)} %copy-done.8), channel_id=1, source_target_pairs={{0,16},{8,24},{16,0},{24,8},{1,17},{9,25},{17,1},{25,9},{2,18},{10... | collective-permute-start | bytes 307208 | tf_op jit(solution)/shard_map/ppermute | solution.py:26
  108.5 59.6 %all-to-all-start.1 = ((bf16[16,160,256]{2,1,0:T(8,128)(2,1)}), bf16[16,160,256]{2,1,0:T(8,128)(2,1)}, u32[]{:S(2)}, u32[]{:S(2)}) async-start(bf16[16,160,256]{2,1,0:T(8,128)(2,1)} %broadcast_in_dim.63), calls=%async_computation.1 | async-start | bytes 2621440 | tf_op jit(solution)/shard_map/all_to_all | solution.py:30
  112.9 604.8 %reduce-scatter.2.cloned.1.call-start = ((), (), s32[]{:S(2)}) async-start(), calls=%async_computation.6 | async-start | bytes 16711680 | tf_op jit(solution)/shard_map/reduce_scatter | solution.py:348
  113.6 35.9 %collective-permute-start.11 = (bf16[4,40,1280]{2,1,0:T(8,128)(2,1)S(1)}, bf16[4,40,1280]{2,1,0:T(8,128)(2,1)S(1)}, u32[]{:S(2)}, u32[]{:S(2)}) collective-permute-start(bf16[4,40,1280]{2,1,0:T(8,128)(2,1)S(1)} %shard_map.188.refs_0_), channel_id=1, source_target_pairs={{0,6},{2,0},{4,2},{6,4},{1,7},{3,1},{5,3},{7,5},{8,14},{10,8},{12,... | collective-permute-start | bytes 1228808 | tf_op jit(solution)/shard_map/ppermute | solution.py:26
  116.1 34.9 %collective-permute-start.12 = (bf16[4,40,1280]{2,1,0:T(8,128)(2,1)S(1)}, bf16[4,40,1280]{2,1,0:T(8,128)(2,1)S(1)}, u32[]{:S(2)}, u32[]{:S(2)}) collective-permute-start(bf16[4,40,1280]{2,1,0:T(8,128)(2,1)S(1)} %shard_map.188.refs_0_), channel_id=1, source_target_pairs={{0,4},{2,6},{4,0},{6,2},{1,5},{3,7},{5,1},{7,3},{8,12},{10,14},{12... | collective-permute-start | bytes 1228808 | tf_op jit(solution)/shard_map/ppermute | solution.py:26
  116.7 48.4 %collective-permute-start.13 = (bf16[4,40,1280]{2,1,0:T(8,128)(2,1)S(1)}, bf16[4,40,1280]{2,1,0:T(8,128)(2,1)S(1)}, u32[]{:S(2)}, u32[]{:S(2)}) collective-permute-start(bf16[4,40,1280]{2,1,0:T(8,128)(2,1)S(1)} %shard_map.188.refs_0_), channel_id=1, source_target_pairs={{0,2},{2,4},{4,6},{6,0},{1,3},{3,5},{5,7},{7,1},{8,10},{10,12},{12... | collective-permute-start | bytes 1228808 | tf_op jit(solution)/shard_map/ppermute | solution.py:26
  165.4 34.9 %collective-permute-start.15 = (bf16[16,40,1280]{2,1,0:T(8,128)(2,1)S(1)}, bf16[16,40,1280]{2,1,0:T(8,128)(2,1)}, u32[]{:S(2)}, u32[]{:S(2)}) collective-permute-start(bf16[16,40,1280]{2,1,0:T(8,128)(2,1)S(1)} %bitcast.252), channel_id=1, source_target_pairs={{0,32},{32,64},{64,96},{96,0},{1,33},{33,65},{65,97},{97,1},{2,34}... | collective-permute-start | bytes 4915208 | tf_op jit(solution)/shard_map/ppermute | solution.py:26
  166.2 36.2 %collective-permute-start.14 = (bf16[16,40,1280]{2,1,0:T(8,128)(2,1)S(1)}, bf16[16,40,1280]{2,1,0:T(8,128)(2,1)S(1)}, u32[]{:S(2)}, u32[]{:S(2)}) collective-permute-start(bf16[16,40,1280]{2,1,0:T(8,128)(2,1)S(1)} %bitcast.253), channel_id=1, source_target_pairs={{0,96},{32,0},{64,32},{96,64},{1,97},{33,1},{65,33},{97,65},{2,98}... | collective-permute-start | bytes 4915208 | tf_op jit(solution)/shard_map/ppermute | solution.py:26
  168.2 152.3 %collective-permute-start.7 = (bf16[2560,256]{1,0:T(8,128)(2,1)}, bf16[2560,256]{1,0:T(8,128)(2,1)}, u32[]{:S(2)}, u32[]{:S(2)}) collective-permute-start(bf16[2560,256]{1,0:T(8,128)(2,1)} %bitcast.15), channel_id=1, source_target_pairs={{0,1},{1,0},{2,3},{3,2},{4,5},{5,4},{6,7},{7,6},{8,9},{9,8},{10,11... | collective-permute-start | bytes 3932168 | tf_op jit(solution)/shard_map/ppermute | solution.py:26
  334.7 27.2 %collective-permute-start.18 = (f32[80,2560]{1,0:T(8,128)}, f32[80,2560]{1,0:T(8,128)}, u32[]{:S(2)}, u32[]{:S(2)}) collective-permute-start(f32[80,2560]{1,0:T(8,128)} %slice.383), channel_id=1, source_target_pairs={{0,1},{1,0},{2,3},{3,2},{4,5},{5,4},{6,7},{7,6},{8,9},{9,8},{10,11... | collective-permute-start | bytes 2457608 | tf_op jit(solution)/shard_map/ppermute | solution.py:26
  343.4 25.7 %collective-permute-start.27 = (bf16[80,2560]{1,0:T(8,128)(2,1)S(1)}, bf16[80,2560]{1,0:T(8,128)(2,1)S(1)}, u32[]{:S(2)}, u32[]{:S(2)}) collective-permute-start(bf16[80,2560]{1,0:T(8,128)(2,1)S(1)} %broadcast_select_fusion.6), channel_id=1, source_target_pairs={{0,64},{32,96},{64,0},{96,32},{1,65},{33,97},{65,1},{97,33},{2,66}... | collective-permute-start | bytes 1228808 | tf_op jit(solution)/shard_map/ppermute | solution.py:26
  343.5 25.6 %collective-permute-start.28 = (bf16[80,2560]{1,0:T(8,128)(2,1)S(1)}, bf16[80,2560]{1,0:T(8,128)(2,1)S(1)}, u32[]{:S(2)}, u32[]{:S(2)}) collective-permute-start(bf16[80,2560]{1,0:T(8,128)(2,1)S(1)} %broadcast_select_fusion.6), channel_id=1, source_target_pairs={{0,32},{32,64},{64,96},{96,0},{1,33},{33,65},{65,97},{97,1},{2,34}... | collective-permute-start | bytes 1228808 | tf_op jit(solution)/shard_map/ppermute | solution.py:26
  364.2 22.2 %collective-permute-start.20 = (bf16[80,2560]{1,0:T(8,128)(2,1)S(1)}, bf16[80,2560]{1,0:T(8,128)(2,1)S(1)}, u32[]{:S(2)}, u32[]{:S(2)}) collective-permute-start(bf16[80,2560]{1,0:T(8,128)(2,1)S(1)} %multiply_convert_fusion.4), channel_id=1, source_target_pairs={{0,64},{32,96},{64,0},{96,32},{1,65},{33,97},{65,1},{97,33},{2,66}... | collective-permute-start | bytes 1228808 | tf_op jit(solution)/shard_map/ppermute | solution.py:26
  468.3 29.5 %collective-permute-start.68 = (bf16[160,320]{1,0:T(8,128)(2,1)S(1)}, bf16[160,320]{1,0:T(8,128)(2,1)S(1)}, u32[]{:S(2)}, u32[]{:S(2)}) collective-permute-start(bf16[160,320]{1,0:T(8,128)(2,1)S(1)} %bitcast.300), channel_id=1, source_target_pairs={{0,64},{32,96},{64,0},{96,32},{1,65},{33,97},{65,1},{97,33},{2,66}... | collective-permute-start | bytes 307208 | tf_op jit(solution)/shard_map/ppermute | solution.py:26
  475.1 23.4 %collective-permute-start.67 = (bf16[160,320]{1,0:T(8,128)(2,1)S(1)}, bf16[160,320]{1,0:T(8,128)(2,1)S(1)}, u32[]{:S(2)}, u32[]{:S(2)}) collective-permute-start(bf16[160,320]{1,0:T(8,128)(2,1)S(1)} %bitcast.301), channel_id=1, source_target_pairs={{0,96},{32,0},{64,32},{96,64},{1,97},{33,1},{65,33},{97,65},{2,98}... | collective-permute-start | bytes 307208 | tf_op jit(solution)/shard_map/ppermute | solution.py:26
  499.1 27.8 %collective-permute-start.65 = (bf16[80,2560]{1,0:T(8,128)(2,1)}, bf16[80,2560]{1,0:T(8,128)(2,1)}, u32[]{:S(2)}, u32[]{:S(2)}) collective-permute-start(bf16[80,2560]{1,0:T(8,128)(2,1)} %get-tuple-element.82), channel_id=1, source_target_pairs={{0,32},{32,64},{64,96},{96,0},{1,33},{33,65},{65,97},{97,1},{2,34}... | collective-permute-start | bytes 1228808 | tf_op jit(solution)/shard_map/ppermute | solution.py:26
  499.1 30.1 %collective-permute-start.64 = (bf16[80,2560]{1,0:T(8,128)(2,1)}, bf16[80,2560]{1,0:T(8,128)(2,1)}, u32[]{:S(2)}, u32[]{:S(2)}) collective-permute-start(bf16[80,2560]{1,0:T(8,128)(2,1)} %get-tuple-element.82), channel_id=1, source_target_pairs={{0,64},{32,96},{64,0},{96,32},{1,65},{33,97},{65,1},{97,33},{2,66}... | collective-permute-start | bytes 1228808 | tf_op jit(solution)/shard_map/ppermute | solution.py:26
  500.6 30.6 %collective-permute-start.63 = (bf16[80,2560]{1,0:T(8,128)(2,1)}, bf16[80,2560]{1,0:T(8,128)(2,1)}, u32[]{:S(2)}, u32[]{:S(2)}) collective-permute-start(bf16[80,2560]{1,0:T(8,128)(2,1)} %get-tuple-element.82), channel_id=1, source_target_pairs={{0,96},{32,0},{64,32},{96,64},{1,97},{33,1},{65,33},{97,65},{2,98}... | collective-permute-start | bytes 1228808 | tf_op jit(solution)/shard_map/ppermute | solution.py:26
  534.6 60.0 %collective-permute-start.66 = (bf16[320,2560]{1,0:T(8,128)(2,1)}, bf16[320,2560]{1,0:T(8,128)(2,1)}, u32[]{:S(2)}, u32[]{:S(2)}) collective-permute-start(bf16[320,2560]{1,0:T(8,128)(2,1)} %pad_maximum_fusion.2), channel_id=1, source_target_pairs={{0,1},{1,0},{2,3},{3,2},{4,5},{5,4},{6,7},{7,6},{8,9},{9,8},{10,11... | collective-permute-start | bytes 4915208 | tf_op jit(solution)/shard_map/ppermute | solution.py:26
  546.0 36.2 %collective-permute-start.45 = (bf16[4,160,256]{1,2,0:T(8,128)(2,1)}, bf16[4,160,256]{1,2,0:T(8,128)(2,1)S(1)}, u32[]{:S(2)}, u32[]{:S(2)}) collective-permute-start(bf16[4,160,256]{1,2,0:T(8,128)(2,1)} %bitcast.295), channel_id=1, source_target_pairs={{0,24},{8,0},{16,8},{24,16},{1,25},{9,1},{17,9},{25,17},{2,26},{10... | collective-permute-start | bytes 983048 | tf_op jit(solution)/shard_map/ppermute | solution.py:26
  547.9 34.4 %collective-permute-start.44 = (bf16[4,160,256]{1,2,0:T(8,128)(2,1)}, bf16[4,160,256]{1,2,0:T(8,128)(2,1)}, u32[]{:S(2)}, u32[]{:S(2)}) collective-permute-start(bf16[4,160,256]{1,2,0:T(8,128)(2,1)} %bitcast.296), channel_id=1, source_target_pairs={{0,8},{8,16},{16,24},{24,0},{1,9},{9,17},{17,25},{25,1},{2,10},{10... | collective-permute-start | bytes 983048 | tf_op jit(solution)/shard_map/ppermute | solution.py:26
  554.1 89.8 %collective-permute-start.36 = (bf16[320,2560]{1,0:T(8,128)(2,1)}, bf16[320,2560]{1,0:T(8,128)(2,1)}, u32[]{:S(2)}, u32[]{:S(2)}) collective-permute-start(bf16[320,2560]{1,0:T(8,128)(2,1)} %convolution_convert_fusion.1), channel_id=1, source_target_pairs={{0,1},{1,0},{2,3},{3,2},{4,5},{5,4},{6,7},{7,6},{8,9},{9,8},{10,11... | collective-permute-start | bytes 4915208 | tf_op jit(solution)/shard_map/ppermute | solution.py:26
  583.8 28.0 %collective-permute-start.49 = (bf16[160,256]{0,1:T(8,128)(2,1)S(1)}, bf16[160,256]{0,1:T(8,128)(2,1)S(1)}, u32[]{:S(2)}, u32[]{:S(2)}) collective-permute-start(bf16[160,256]{0,1:T(8,128)(2,1)S(1)} %get-tuple-element.127), channel_id=1, source_target_pairs={{0,4},{2,6},{4,0},{6,2},{1,5},{3,7},{5,1},{7,3},{8,12},{10,14},{12... | collective-permute-start | bytes 245768 | tf_op jit(solution)/shard_map/ppermute | solution.py:26
  590.0 21.8 %collective-permute-start.48 = (bf16[160,256]{0,1:T(8,128)(2,1)S(1)}, bf16[160,256]{0,1:T(8,128)(2,1)S(1)}, u32[]{:S(2)}, u32[]{:S(2)}) collective-permute-start(bf16[160,256]{0,1:T(8,128)(2,1)S(1)} %get-tuple-element.128), channel_id=1, source_target_pairs={{0,6},{2,0},{4,2},{6,4},{1,7},{3,1},{5,3},{7,5},{8,14},{10,8},{12,... | collective-permute-start | bytes 245768 | tf_op jit(solution)/shard_map/ppermute | solution.py:26
  604.8 50.8 %all-to-all-start.3 = ((bf16[64,40,320]{2,1,0:T(8,128)(2,1)}), bf16[64,40,320]{2,1,0:T(8,128)(2,1)}, u32[]{:S(2)}, u32[]{:S(2)}) async-start(bf16[64,40,320]{2,1,0:T(8,128)(2,1)} %bitcast.261), calls=%async_computation.4 | async-start | bytes 3932160 | tf_op jit(solution)/shard_map/all_to_all | solution.py:30
  636.4 48.9 %collective-permute-start.53 = (bf16[320,2560]{1,0:T(8,128)(2,1)}, bf16[320,2560]{1,0:T(8,128)(2,1)}, u32[]{:S(2)}, u32[]{:S(2)}) collective-permute-start(bf16[320,2560]{1,0:T(8,128)(2,1)} %convolution_convert_fusion), channel_id=1, source_target_pairs={{0,1},{1,0},{2,3},{3,2},{4,5},{5,4},{6,7},{7,6},{8,9},{9,8},{10,11... | collective-permute-start | bytes 4915208 | tf_op jit(solution)/shard_map/ppermute | solution.py:26
  651.8 29.8 %collective-permute-start.37 = (bf16[80,2560]{1,0:T(8,128)(2,1)S(1)}, bf16[80,2560]{1,0:T(8,128)(2,1)S(1)}, u32[]{:S(2)}, u32[]{:S(2)}) collective-permute-start(bf16[80,2560]{1,0:T(8,128)(2,1)S(1)} %get-tuple-element.102), channel_id=1, source_target_pairs={{0,32},{32,64},{64,96},{96,0},{1,33},{33,65},{65,97},{97,1},{2,34}... | collective-permute-start | bytes 1228808 | tf_op jit(solution)/shard_map/ppermute | solution.py:26
  655.6 40.7 %all-to-all-start.2 = ((bf16[64,40,384]{2,1,0:T(8,128)(2,1)}), bf16[64,40,384]{2,1,0:T(8,128)(2,1)}, u32[]{:S(2)}, u32[]{:S(2)}) async-start(bf16[64,40,384]{2,1,0:T(8,128)(2,1)} %bitcast.284), calls=%async_computation.2 | async-start | bytes 3932160 | tf_op jit(solution)/shard_map/all_to_all | solution.py:30
  (144 other events, 2260.8 us)
Sparse Core Ops, SparseCore 0:
  29.5 165.4 all-gather.1
  464.7 123.7 reduce-scatter.1

commit v3 on v2

v3 whole, which is shorter than its diff:
```python
import functools

import jax
import jax.numpy as jnp
from jax import lax
from jax.experimental import pallas as pl
from jax.experimental.pallas import tpu as pltpu
from jax.sharding import Mesh
from jax.sharding import PartitionSpec as P

WINDOW = 2048
SHARD_CONTEXT = ("shard", "context_0", "context_1")
CONTEXT = ("context_0", "context_1")
PIECES = ("context_0", "context_1", "shard")
Y, X, Z, T = "shard", "context_0", "context_1", "tensor"
VMEM = pltpu.CompilerParams(vmem_limit_bytes=48 * 2**20)
ANYWHERE = pl.BlockSpec(memory_space=pl.ANY)

EPSILON = 1e-06
NEGATIVE_FILL = -1e30
BF = jnp.bfloat16
F32 = jnp.float32


def shift(x, axis, by):
    n = lax.axis_size(axis)
    return lax.ppermute(x, axis, [(i, (i + by) % n) for i in range(n)])


def exchange(blocks, axis):
    return lax.all_to_all(blocks, axis, 0, 0, tiled=True)


def nothing(*refs):
    pass


def after(x, *others):
    return pl.pallas_call(
        nothing,
        out_shape=jax.ShapeDtypeStruct(x.shape, x.dtype),
        in_specs=[ANYWHERE] * (1 + len(others)),
        out_specs=ANYWHERE,
        input_output_aliases={0: 0},
        compiler_params=VMEM,
    )(x, *others)


def small_trip(x):
    return shift(x.reshape(-1, x.shape[-1])[:8, :128], T, 1)


def ring_blocks(x, axis):
    return [x, shift(x, axis, -1), shift(x, axis, 2), shift(x, axis, 1)]


def place_kernel(axis, sign, *refs):
    blocks, out, sems = refs[:-2], refs[-2], refs[-1]
    me = lax.axis_index(axis)
    copies = []
    for r, block in enumerate(blocks):
        j = lax.rem(me + (sign * r) % 4, 4)
        copies.append(pltpu.make_async_copy(block, out.at[j], sems.at[r]))
    for copy in copies:
        copy.start()
    for copy in copies:
        copy.wait()


def place(blocks, axis, sign=1):
    return pl.pallas_call(
        functools.partial(place_kernel, axis, sign),
        out_shape=jax.ShapeDtypeStruct((4, *blocks[0].shape), blocks[0].dtype),
        in_specs=[pl.BlockSpec(memory_space=pl.ANY)] * 4,
        out_specs=pl.BlockSpec(memory_space=pl.ANY),
        scratch_shapes=[pltpu.SemaphoreType.DMA((4,))],
        compiler_params=VMEM,
    )(*blocks)


def gather_rows(mine):
    own = exchange(jnp.broadcast_to(mine[None], (4, *mine.shape)), Y).reshape(320, -1)
    return jnp.concatenate([own, shift(own, T, 1)])


def scatter_parts(parts, weight, db):
    far = dot(parts[320:], weight, 1, db).astype(BF)
    near = dot(parts[:320], weight, 1, db) + shift(far, T, 1).astype(F32)
    return near.astype(BF).reshape(4, 80, -1)


def scatter_sum(low):
    return jnp.sum(exchange(low, Y).astype(F32), axis=0)


def scatter_sum_permutes(low):
    me = lax.axis_index(Y)
    total = lax.dynamic_index_in_dim(low, me, 0, keepdims=False).astype(F32)
    for r in (1, 3, 2):
        block = lax.dynamic_index_in_dim(low, (me + r) % 4, 0, keepdims=False)
        total = total + shift(block, Y, r).astype(F32)
    return total


def by_half(blocks):
    cols = blocks.shape[2]
    return blocks.reshape(4, 2, 80, cols).swapaxes(0, 1).reshape(640, cols)


def columns_out(x):
    return by_half(exchange(quarters(x), Y))


def columns_out_permutes(x):
    me = lax.axis_index(Y)
    blocks = quarters(x)
    got = []
    for r in range(4):
        block = lax.dynamic_index_in_dim(blocks, (me + r) % 4, 0, keepdims=False)
        got.append(shift(block, Y, r) if r else block)
    return by_half(place(got, Y, sign=-1))


def assemble_kernel(own_ref, behind_ref, before_ref, far_one_ref, far_two_ref, _, out_ref):
    me = lax.axis_index(Y)
    i = pl.program_id(0)
    out_ref[0, me] = own_ref[0]
    out_ref[0, lax.rem(me + 1, 4)] = behind_ref[0]
    out_ref[0, lax.rem(me + 3, 4)] = before_ref[0]

    @pl.when(i < 8)
    def _():
        out_ref[0, lax.rem(me + 2, 4)] = far_one_ref[0]

    @pl.when(i >= 8)
    def _():
        out_ref[0, lax.rem(me + 2, 4)] = far_two_ref[0]


def assemble(blocks, first):
    cols = blocks[0].shape[-1]
    whole = pl.BlockSpec((1, 40, cols), lambda i: (i, 0, 0))
    low = pl.BlockSpec((1, 40, cols), lambda i: (jnp.minimum(i, 7), 0, 0))
    high = pl.BlockSpec((1, 40, cols), lambda i: (jnp.maximum(i, 8) - 8, 0, 0))
    return pl.pallas_call(
        assemble_kernel,
        grid=(16,),
        out_shape=jax.ShapeDtypeStruct((16, 4, 40, cols), BF),
        in_specs=[whole, whole, whole, low, high, ANYWHERE],
        out_specs=pl.BlockSpec((1, 4, 40, cols), lambda i: (i, 0, 0, 0)),
        compiler_params=VMEM,
    )(*blocks, first).reshape(2560, cols)


def quarters(x):
    rows = x.shape[0]
    return x.reshape(rows, 4, -1).swapaxes(0, 1)


def joined(blocks):
    return blocks.swapaxes(0, 1).reshape(blocks.shape[1], -1)


def pack_attention_kernel(q_ref, kv_ref, gains_ref, attn_ref):
    attn_ref[...] = jnp.zeros_like(attn_ref)
    for j in range(4):
        attn_ref[j, :40, :320] = q_ref[:, 320 * j : 320 * j + 320]
        attn_ref[j, :40, 320:] = kv_ref[:, 64 * j : 64 * j + 64]
        attn_ref[j, 40:48, :128] = gains_ref[...]


def pack_attention(w_query, keyval_half, gains):
    return pl.pallas_call(
        pack_attention_kernel,
        out_shape=jax.ShapeDtypeStruct((4, 48, 384), BF),
        compiler_params=VMEM,
    )(w_query, keyval_half, gains)


def pack_mlp_kernel(gate_ref, up_ref, down_ref, _, mlp_ref):
    mlp_ref[...] = jnp.zeros_like(mlp_ref)
    for j in range(4):
        mlp_ref[j, :, :960] = gate_ref[:, 960 * j : 960 * j + 960]
        mlp_ref[j, :, 1024:1984] = up_ref[:, 960 * j : 960 * j + 960]
        mlp_ref[j, :, 2048:3008] = down_ref[:, 960 * j : 960 * j + 960]


def pack_mlp(w_gate, w_up, w_down, first):
    whole = pl.BlockSpec(memory_space=pltpu.VMEM)
    return pl.pallas_call(
        pack_mlp_kernel,
        out_shape=jax.ShapeDtypeStruct((4, 40, 3072), BF),
        in_specs=[whole, whole, whole, ANYWHERE],
        compiler_params=VMEM,
    )(w_gate, w_up, w_down, first)


def mlp_grad_kernel(x_ref, y_ref, gate_up_ref, hidden_ref, _, out_ref):
    j = pl.program_id(0)

    @pl.when(j < 2)
    def _():
        out_ref[...] = dot(x_ref[...], gate_up_ref[...], 0, 0).astype(BF)

    @pl.when(j == 2)
    def _():
        out_ref[...] = dot(y_ref[...], hidden_ref[...], 0, 0).astype(BF)


def mlp_grads(normed, grads, gate_up, hidden, first):
    rows = 512
    return pl.pallas_call(
        mlp_grad_kernel,
        grid=(3, 2560 // rows),
        out_shape=jax.ShapeDtypeStruct((2560, 3072), BF),
        in_specs=[
            pl.BlockSpec((640, rows), lambda j, i: (0, jnp.where(j < 2, i, 4))),
            pl.BlockSpec((640, rows), lambda j, i: (0, jnp.where(j < 2, 0, i))),
            pl.BlockSpec((640, 1024), lambda j, i: (0, jnp.minimum(j, 1))),
            pl.BlockSpec((640, 1024), lambda j, i: (0, 0)),
            ANYWHERE,
        ],
        out_specs=pl.BlockSpec((rows, 1024), lambda j, i: (i, j)),
        compiler_params=VMEM,
        cost_estimate=pl.CostEstimate(
            flops=2 * 640 * 2560 * 3072, bytes_accessed=2 * 2560 * 3072, transcendentals=0
        ),
    )(normed, grads, gate_up, hidden, first)


def to_piece_order(x):
    rows = x.shape[0]
    return x.reshape(rows, 4, 16, 40).swapaxes(1, 2).reshape(rows, 2560)


def inverse_root(values):
    return lax.rsqrt(jnp.mean(values * values, axis=-1, keepdims=True) + EPSILON)


def norm_back(grad, values, inverse, gain):
    scaled = gain * grad
    return inverse * scaled - values * inverse**3 * jnp.mean(
        scaled * values, axis=-1, keepdims=True
    )


def angles(position, head_dim):
    quarter = head_dim // 4
    frequency = 10000.0 ** (-jnp.arange(quarter, dtype=F32) / quarter)
    phase_angle = position[:, None].astype(F32) * frequency[None, :]
    return (jnp.cos(phase_angle), jnp.sin(phase_angle))


def rotate(values, cosine, sine_part):
    quarter = cosine.shape[-1]
    first_half = values[..., :quarter]
    second = values[..., quarter : 2 * quarter]
    cos_rows = cosine[:, None, :]
    sin_rows = sine_part[:, None, :]
    return jnp.concatenate(
        [
            first_half * cos_rows - second * sin_rows,
            second * cos_rows + first_half * sin_rows,
            values[..., 2 * quarter :],
        ],
        axis=-1,
    )


def dot(a, b, da, db):
    return lax.dot_general(a, b, (((da,), (db,)), ((), ())), preferred_element_type=F32)


def project_kernel(own_ref, other_ref, gain_ref, weight_ref, normed_ref, grad_ref, out_ref):
    def rows(block):
        x = block[:80].astype(F32)
        normed = (x * inverse_root(x) * gain_ref[...]).astype(BF)
        normed_ref[...] = normed
        grad_ref[...] = block[80:]
        out_ref[0] = dot(normed, weight_ref[...], 1, 0).astype(BF)

    i = pl.program_id(0)

    @pl.when(i < 4)
    def _():
        rows(own_ref[0])

    @pl.when(i >= 4)
    def _():
        rows(other_ref[0])


def project(own, other, gain, weight):
    return pl.pallas_call(
        project_kernel,
        grid=(8,),
        out_shape=(
            jax.ShapeDtypeStruct((640, 2560), BF),
            jax.ShapeDtypeStruct((640, 2560), BF),
            jax.ShapeDtypeStruct((4, 160, 384), BF),
        ),
        in_specs=[
            pl.BlockSpec((1, 160, 2560), lambda i: (jnp.minimum(i, 3), 0, 0)),
            pl.BlockSpec((1, 160, 2560), lambda i: (jnp.maximum(i, 4) - 4, 0, 0)),
            pl.BlockSpec((1, 2560), lambda i: (0, 0)),
            pl.BlockSpec((2560, 384), lambda i: (0, 0)),
        ],
        out_specs=(
            pl.BlockSpec((80, 2560), lambda i: (i, 0)),
            pl.BlockSpec((80, 2560), lambda i: (i, 0)),
            pl.BlockSpec((1, 80, 384), lambda i: (i % 4, i // 4, 0)),
        ),
        compiler_params=VMEM,
    )(own, other, gain, weight)


def owned_kernel(home_ref, out_ref):
    for j in range(4):
        total = home_ref[j].astype(F32)
        for p in range(1, 16):
            total = total + home_ref[4 * p + j].astype(F32)
        out_ref[:, 320 * j : 320 * j + 320] = total


def owned(home):
    return pl.pallas_call(
        owned_kernel, out_shape=jax.ShapeDtypeStruct((40, 1280), F32), compiler_params=VMEM
    )(home)


def owned_qkv_kernel(home_ref, query_ref, keyval_ref, query_out, keyval_out, gain_out):
    gain = jnp.zeros((40, 1), F32)
    for j in range(4):
        total = home_ref[j].astype(F32)
        for p in range(1, 16):
            total = total + home_ref[4 * p + j].astype(F32)
        query_out[:, 320 * j : 320 * j + 320] = total[:, :320]
        keyval_out[:, 64 * j : 64 * j + 64] = total[:, 320:]
    for weight, grad in ((query_ref, query_out), (keyval_ref, keyval_out)):
        gain += jnp.sum(weight[...].astype(F32) * grad[...], axis=1, keepdims=True)
    gain_out[...] = jnp.broadcast_to(gain, (40, 128))


def owned_qkv(home, w_query, keyval_half):
    return pl.pallas_call(
        owned_qkv_kernel,
        out_shape=(
            jax.ShapeDtypeStruct((40, 1280), F32),
            jax.ShapeDtypeStruct((40, 256), F32),
            jax.ShapeDtypeStruct((40, 128), F32),
        ),
        compiler_params=VMEM,
    )(home, w_query, keyval_half)


def owned_mlp_kernel(b0, b1, b2, b3, gate_ref, up_ref, gate_out, up_out, down_out, gain_out, held):
    me = lax.axis_index(Y)
    for r, block in enumerate((b0, b1, b2, b3)):
        held[lax.rem(me + 4 - r, 4)] = block[...]
    for j in range(4):
        columns = slice(960 * j, 960 * j + 960)
        gate_out[:, columns] = held[j, :, :960].astype(F32)
        up_out[:, columns] = held[j, :, 1024:1984].astype(F32)
        down_out[:, columns] = held[j, :, 2048:3008].astype(F32)
    products = gate_ref[...].astype(F32) * gate_out[...] + up_ref[...].astype(F32) * up_out[...]
    gain_out[...] = jnp.broadcast_to(jnp.sum(products, axis=1, keepdims=True), (40, 128))


def owned_mlp(blocks, w_gate, w_up):
    wide = jax.ShapeDtypeStruct((40, 3840), F32)
    return pl.pallas_call(
        owned_mlp_kernel,
        out_shape=(wide, wide, wide, jax.ShapeDtypeStruct((40, 128), F32)),
        scratch_shapes=[pltpu.VMEM((4, 40, 3072), BF)],
        compiler_params=VMEM,
    )(*blocks, w_gate, w_up)


def token_order_kernel(x_ref, out_ref):
    for j in range(4):
        for p in range(16):
            to, at = 40 * (16 * j + p), 40 * (4 * p + j)
            out_ref[:, to : to + 40] = x_ref[:, at : at + 40].astype(BF)


def from_piece_order(x):
    return pl.pallas_call(
        token_order_kernel, out_shape=jax.ShapeDtypeStruct(x.shape, BF), compiler_params=VMEM
    )(x)


def halves_kernel(mine_ref, other_ref, _, out_ref):
    at = 80 * lax.axis_index(T)
    out_ref[pl.ds(pl.multiple_of(at, 16), 80), :] = mine_ref[...]
    out_ref[pl.ds(pl.multiple_of(80 - at, 16), 80), :] = other_ref[...]


def halves_home(mine, first):
    whole = pl.BlockSpec(memory_space=pltpu.VMEM)
    return pl.pallas_call(
        halves_kernel,
        out_shape=jax.ShapeDtypeStruct((160, mine.shape[1]), BF),
        in_specs=[whole, whole, ANYWHERE],
        compiler_params=VMEM,
    )(mine, shift(mine, T, 1), first)


def feed_forward(gate_up, grad_hidden):
    gate_pre, up_pre = gate_up[:, :1024], gate_up[:, 1024:]
    activated, gelu_pull = jax.vjp(jax.nn.gelu, gate_pre)
    hidden = (activated * up_pre).astype(BF)
    grad_gate = gelu_pull(grad_hidden * up_pre)[0].astype(BF)
    grad_up = (grad_hidden * activated).astype(BF)
    return hidden, jnp.concatenate([grad_gate, grad_up], axis=1)


def shards(
    tokens,
    lengths,
    attn_gain,
    w_query,
    w_keyval,
    w_output,
    mlp_gain,
    w_gate,
    w_up,
    w_down,
    cotangent,
):
    t = lax.axis_index(T)
    me = lax.axis_index(Y)
    piece = lax.axis_index(CONTEXT)
    head_dim = 256
    query_scale = head_dim ** (-0.5)
    seq_count = 2560
    padding = seq_count - lengths[0]
    row_start = piece * 160
    natural = row_start + jnp.arange(160, dtype=jnp.int32)
    turned = row_start + (jnp.arange(160, dtype=jnp.int32) + t * 80) % 160
    live_turned = turned >= padding
    live_mine = live_turned[:80, None]

    out_piece = lax.all_gather(w_output, CONTEXT, axis=0, tiled=True).reshape(16, 40, 1280)

    x_low = to_piece_order(lax.dynamic_slice_in_dim(tokens[0], t * 80, 80, 0))
    cot_mine = to_piece_order(lax.dynamic_slice_in_dim(cotangent[0], t * 80, 80, 0))
    grad_mine = jnp.where(live_mine, cot_mine, jnp.zeros_like(cot_mine))
    x_mine = x_low.astype(F32)
    both_blocks = ring_blocks(jnp.concatenate([x_low, grad_mine]), Y)
    both_own = place(both_blocks, Y)
    both_other = shift(both_own, T, 1)

    keyval_half = lax.dynamic_slice_in_dim(w_keyval, t * 256, 256, 1)
    gains = jnp.concatenate([attn_gain, mlp_gain])[None, :]
    gains = jnp.pad(gains, ((0, 7), (0, 48)))
    attn_blocks = pack_attention(w_query, keyval_half, gains)
    attn_copies = jnp.broadcast_to(attn_blocks[None], (16, 4, 48, 384)).reshape(64, 48, 384)
    attn_all = exchange(attn_copies, PIECES)
    w_qkv = attn_all[:, :40].reshape(2560, 384)
    gain_one = attn_all[:, 40, :40].reshape(1, 2560).astype(F32)
    gain_two = attn_all[:, 40, 40:80].reshape(1, 2560).astype(F32)
    mlp_blocks = pack_mlp(w_gate, w_up, w_down, both_blocks[1])
    mlp_got = []
    for r in range(4):
        block = lax.dynamic_index_in_dim(mlp_blocks, (me + r) % 4, 0, keepdims=False)
        mlp_got.append(shift(block, Y, r) if r else block)
    mlp_block = place(mlp_got, Y, sign=-1).reshape(160, 3072)
    w_mlp = lax.all_gather(mlp_block, CONTEXT, axis=0, tiled=True)
    w_gate_up = w_mlp[:, :2048]
    w_down_all = w_mlp[:, 2048:]
    before, behind = shift(out_piece, Y, 1), shift(out_piece, Y, -1)
    far_one, far_two = shift(before[:8], Y, 1), shift(behind[8:], Y, -1)

    normed, grad_group, projected = project(both_own, both_other, gain_one, w_qkv)
    home = exchange(projected, Y)
    keyval_turned = joined(home[:, :, 320:])
    keyval_own = jnp.where(
        t == 0, keyval_turned, jnp.concatenate([keyval_turned[80:], keyval_turned[:80]])
    )
    cosine_nat, sine_nat = angles(natural - padding, head_dim)
    keys_own = rotate(keyval_own[:, None].astype(F32), cosine_nat, sine_nat)[:, 0].astype(BF)
    kv_own = jnp.where(t == 0, keys_own, keyval_own)
    kv_mine = exchange(jnp.broadcast_to(kv_own[None], (16, 160, 256)), CONTEXT).reshape(2560, 256)
    kv_other = shift(kv_mine, T, 1)
    keys = jnp.where(t == 0, kv_mine, kv_other)
    values = jnp.where(t == 0, kv_other, kv_mine)
    query_pre = joined(home[:, :, :320]).reshape(160, 5, head_dim).astype(F32)
    cosine, sine_part = angles(turned - padding, head_dim)
    queries = (rotate(query_pre, cosine, sine_part) * query_scale).astype(BF)

    key_index = jnp.arange(seq_count, dtype=jnp.int32)
    offset = turned[:, None] - key_index[None, :]
    allowed = ((offset >= 0) & (offset < WINDOW) & (key_index >= padding)[None, :])[None]
    live = live_turned[None, :, None]
    scores = jnp.einsum("qhd,kd->hqk", queries, keys, preferred_element_type=F32)
    row_top = jnp.max(jnp.where(allowed, scores, NEGATIVE_FILL), axis=-1, keepdims=True)
    row_top = jnp.where(live, row_top, 0.0)
    weights_exp = jnp.where(allowed, jnp.exp(scores - row_top), 0.0)
    row_total = jnp.where(live, jnp.sum(weights_exp, axis=-1, keepdims=True), 1.0)
    prob = weights_exp / row_total
    prob_low = prob.astype(BF)
    attended = jnp.einsum("hqk,kd->qhd", prob_low, values, preferred_element_type=F32)
    attended = attended.reshape(160, 1280).astype(BF)

    w_out = assemble((out_piece, behind, before, far_one, far_two), attended)
    branch = dot(attended, w_out, 1, 1)
    hidden_mine = x_mine + branch[:80] + shift(branch[80:], T, 1)

    inverse_two = inverse_root(hidden_mine)
    normed_two = gather_rows((hidden_mine * inverse_two * gain_two).astype(BF))
    attended_group = columns_out(after(attended, normed_two))
    gate_up = dot(normed_two, w_gate_up, 1, 0)
    grad_hidden = dot(grad_group, w_down_all, 1, 0)
    hidden, grad_gate_up = feed_forward(gate_up, grad_hidden)
    normed_two_low = scatter_parts(grad_gate_up, w_gate_up, 1)
    grad_normed_two = scatter_sum(normed_two_low)

    trip = small_trip(normed_two_low)
    mlp_part = mlp_grads(normed_two, grad_group, grad_gate_up, hidden, trip)
    mlp_sum = lax.psum_scatter(mlp_part, CONTEXT, scatter_dimension=0, tiled=True)
    mlp_low = scatter_parts(after(hidden, mlp_part), w_down_all, 1)

    grad_h_mine = grad_mine.astype(F32) + norm_back(
        grad_normed_two, hidden_mine, inverse_two, gain_two
    )
    branch_mine = grad_h_mine.astype(BF)
    branch_low = jnp.concatenate([branch_mine, shift(branch_mine, T, 1)])
    grad_attended = dot(branch_low, w_out, 1, 0).astype(BF).reshape(160, 5, head_dim)
    branch_own = place(ring_blocks(branch_mine, Y), Y).reshape(320, 2560)
    branch_group = jnp.concatenate([branch_own, shift(branch_own, T, 1)])

    grad_prob = jnp.einsum("qhd,kd->hqk", grad_attended, values, preferred_element_type=F32)
    spread = jnp.sum(prob * grad_prob, axis=-1, keepdims=True)
    grad_scores = (prob * (grad_prob - spread)).astype(BF)
    grad_keys = jnp.einsum("hqk,qhd->kd", grad_scores, queries, preferred_element_type=F32)
    grad_values = jnp.einsum("hqk,qhd->kd", prob_low, grad_attended, preferred_element_type=F32)
    keep = jnp.where(t == 0, grad_keys, grad_values)
    give = jnp.where(t == 0, grad_values, grad_keys).astype(BF)
    grad_queries = jnp.einsum("hqk,kd->qhd", grad_scores, keys, preferred_element_type=F32)
    grad_query_pre = (
        rotate(grad_queries * query_scale, cosine, -sine_part).reshape(160, 1280).astype(BF)
    )
    kv_part = (keep + shift(give, T, 1).astype(F32)).astype(BF).reshape(16, 160, 256)
    kv_sum = jnp.sum(exchange(kv_part, CONTEXT).astype(F32), axis=0)
    grad_query_group = columns_out_permutes(grad_query_pre)

    late_group = after(attended_group, small_trip(kv_part))
    output_part = dot(branch_group, late_group, 0, 0).astype(BF).reshape(64, 40, 320)
    output_home = exchange(after(output_part, kv_sum), PIECES)
    mlp_mine = scatter_sum_permutes(after(mlp_low, output_part))
    block_mine = jnp.where(live_mine, hidden_mine + mlp_mine, 0.0)

    keys_back = rotate(kv_sum[:, None], cosine_nat, -sine_nat)[:, 0]
    kv_back = jnp.where(t == 0, keys_back, kv_sum).astype(BF)
    kv_back = jnp.where(t == 0, kv_back, jnp.concatenate([kv_back[80:], kv_back[:80]]))
    grad_kv_group = columns_out_permutes(kv_back)
    grad_qkv = jnp.concatenate([grad_query_group, grad_kv_group], axis=1)
    qkv_part = dot(normed, grad_qkv, 0, 0).astype(BF).reshape(64, 40, 384)
    qkv_home = exchange(qkv_part, PIECES)
    grad_normed = scatter_sum_permutes(scatter_parts(grad_qkv, w_qkv, 1))
    inverse_one = inverse_root(x_mine)
    tokens_mine = grad_h_mine + norm_back(grad_normed, x_mine, inverse_one, gain_one)
    output_grad = owned(output_home)
    mlp_got = []
    mlp_rows = mlp_sum.reshape(4, 40, 3072)
    for r in range(4):
        block = lax.dynamic_index_in_dim(mlp_rows, (me + r) % 4, 0, keepdims=False)
        mlp_got.append(shift(block, Y, r) if r else block)
    gate_grad, up_grad, down_grad, two_part = owned_mlp(mlp_got, w_gate, w_up)
    block_out = halves_home(from_piece_order(block_mine), kv_sum)
    tokens_grad = halves_home(from_piece_order(tokens_mine), two_part)

    query_grad, kv_half, one_part = owned_qkv(qkv_home, w_query, keyval_half)
    mine = jnp.concatenate([kv_half, one_part, two_part], axis=1)
    other = shift(mine, T, 1)
    kv_other = other[:, :256]
    keyval_grad = jnp.where(
        t == 0,
        jnp.concatenate([kv_half, kv_other], axis=1),
        jnp.concatenate([kv_other, kv_half], axis=1),
    )
    attn_gain_grad = (mine[:, 256] + other[:, 256]) / attn_gain.astype(F32)
    mlp_gain_grad = (mine[:, 384] + other[:, 384]) / mlp_gain.astype(F32)

    return (
        block_out[None],
        tokens_grad[None],
        attn_gain_grad,
        query_grad,
        keyval_grad,
        output_grad,
        mlp_gain_grad,
        gate_grad,
        up_grad,
        down_grad,
    )


def solution(mesh):
    torus = Mesh(
        mesh.devices.reshape(mesh.shape["shard"], 4, 4, mesh.shape["tensor"]),
        ("shard", "context_0", "context_1", "tensor"),
    )
    in_specs = (
        P("shard", CONTEXT, None),
        P("shard"),
        P(SHARD_CONTEXT),
        P(SHARD_CONTEXT, "tensor"),
        P(SHARD_CONTEXT, None),
        P(SHARD_CONTEXT, "tensor"),
        P(SHARD_CONTEXT),
        P(SHARD_CONTEXT, "tensor"),
        P(SHARD_CONTEXT, "tensor"),
        P(SHARD_CONTEXT, "tensor"),
        P("shard", CONTEXT, None),
    )
    out_specs = (
        P("shard", CONTEXT, None),
        P("shard", CONTEXT, None),
        P(SHARD_CONTEXT),
        P(SHARD_CONTEXT, "tensor"),
        P(SHARD_CONTEXT, None),
        P(SHARD_CONTEXT, "tensor"),
        P(SHARD_CONTEXT),
        P(SHARD_CONTEXT, "tensor"),
        P(SHARD_CONTEXT, "tensor"),
        P(SHARD_CONTEXT, "tensor"),
    )
    return jax.shard_map(
        shards, mesh=torus, in_specs=in_specs, out_specs=out_specs, check_vma=False
    )
```

time: 771 us -> 648 us (0.84)
  blocking collectives: 0 us -> 115 us
  Pallas kernels: 134 us -> 56 us
  local copies, waits for them, and re-layouts: 94.5 us -> 46.1 us
  waiting for transfers between devices: 223 us -> 180 us
  starting transfers between devices: 145 us -> 104 us
  other arithmetic: 43.9 us -> 31 us
  matrix products: 99.3 us -> 89.4 us
    all_to_all x0 -> x3, blocking collectives: none -> 115 us  [exchange(): return lax.all_to_all(blocks, axis, 0, 0, tiled=True)]
    pallas_call x8 -> x22, Pallas kernels: 134 us -> 56 us  [the longest x1 20.8 us: mlp_grads(): pl.pallas_call(mlp_grad_kernel, grid=(3, 2560 // rows), out_shape=jax.Sha...]
    ppermute x70 -> x43, waiting for transfers between devices: 211 us -> 157 us  [shift(): return lax.ppermute(x, axis, [(i, (i + by) % n) for i in range(n)])]
    ppermute x70 -> x43, starting transfers between devices: 114 us -> 71.4 us  [shift(): return lax.ppermute(x, axis, [(i, (i + by) % n) for i in range(n)])]
    all_to_all x4 -> x6, waiting for transfers between devices: 11.8 us -> 22.7 us  [exchange(): return lax.all_to_all(blocks, axis, 0, 0, tiled=True)]
    unnamed x219 -> x157, local copies, waits for them, and re-layouts: 24.3 us -> 14.2 us
    ppermute x6 -> x0, local copies, waits for them, and re-layouts: 9.98 us -> none  [shift(): return lax.ppermute(x, axis, [(i, (i + by) % n) for i in range(n)])]
    dot_general x18 -> x12, matrix products: 78.6 us -> 68.9 us  [dot(): lax.dot_general(a, b, (((da,), (db,)), ((), ())), preferred_element_type=...]
  transfers between devices with their start and end apart: 76 -> 52, of which waited for: 27 -> 22; matrix products, arithmetic and copies ran while one was open for 24% -> 18% of each run, Pallas kernels for 13% -> 6%
where the time goes in v3:
time: 648 us; the launch traced here: 638 us
  waiting for transfers between devices  180 us (28%)
  blocking collectives  115 us (18%)
  starting transfers between devices  104 us (16%)
  matrix products  89.4 us (14%)
  Pallas kernels  56 us (9%)
  local copies, waits for them, and re-layouts  46.1 us (7%)
  other arithmetic  31 us (5%)
  between operations  16.3 us (3%)
    ppermute x43, waiting for transfers between devices, shift(): return lax.ppermute(x, axis, [(i, (i + by) % n) for i in range(n)])  157 us
    all_to_all x3, blocking collectives, exchange(): return lax.all_to_all(blocks, axis, 0, 0, tiled=True)  115 us
    ppermute x43, starting transfers between devices, shift(): return lax.ppermute(x, axis, [(i, (i + by) % n) for i in range(n)])  71.4 us
    dot_general x12, matrix products, dot(): lax.dot_general(a, b, (((da,), (db,)), ((), ())), preferred_element_type=...  68.9 us
    all_to_all x6, starting transfers between devices, exchange(): return lax.all_to_all(blocks, axis, 0, 0, tiled=True)  32.8 us
    all_to_all x6, waiting for transfers between devices, exchange(): return lax.all_to_all(blocks, axis, 0, 0, tiled=True)  22.7 us
    pallas_call x1, Pallas kernels, mlp_grads(): pl.pallas_call(mlp_grad_kernel, grid=(3, 2560 // rows), out_shape=jax.Sha...  20.8 us
    unnamed x157, local copies, waits for them, and re-layouts  14.2 us
  transfers between devices with their start and end apart: 52, of which 22 were waited for; matrix products, arithmetic and copies ran while one was open for 18% of the time, Pallas kernels for 6%

profile of v3, /device:TPU:1, one launch (start us, length us, event | category | flops | bytes accessed | tf_op | source)
XLA Modules:
  0.0 638.0 jit_solution(15532737170270870415)
XLA Ops:
  16.9 16.9 %collective-permute-done.refs_1_._ = bf16[160,2560]{1,0:T(8,128)(2,1)S(1)} collective-permute-done((bf16[160,2560]{1,0:T(8,128)(2,1)S(1)}, bf16[160,2560]{1,0:T(8,128)(2,1)S(1)}, u32[]{:S(2)}, u32[]{:S(2)}) %collective-permute-start) | collective-permute-done | bytes 819232 | tf_op jit(solution)/shard_map/ppermute | solution.py:27
  38.3 8.7 %collective-permute-done.13.refs_3_ = bf16[40,3072]{1,0:T(8,128)(2,1)S(1)} collective-permute-done((bf16[40,3072]{1,0:T(8,128)(2,1)S(1)}, bf16[40,3072]{1,0:T(8,128)(2,1)S(1)}, u32[]{:S(2)}, u32[]{:S(2)}) %collective-permute-start.13) | collective-permute-done | bytes 245792 | tf_op jit(solution)/shard_map/ppermute | solution.py:27
  47.0 4.7 collective-permute-done.11.refs_1_
  53.3 37.3 %collective-permute-done.2.refs_3_ = bf16[160,2560]{1,0:T(8,128)(2,1)S(1)} collective-permute-done((bf16[160,2560]{1,0:T(8,128)(2,1)S(1)}, bf16[160,2560]{1,0:T(8,128)(2,1)S(1)}, u32[]{:S(2)}, u32[]{:S(2)}) %collective-permute-start.2) | collective-permute-done | bytes 819232 | tf_op jit(solution)/shard_map/ppermute | solution.py:27
  94.6 66.0 %all_to_all.45 = bf16[64,48,384]{2,1,0:T(8,128)(2,1)S(1)} all-to-all(bf16[64,48,384]{2,1,0:T(8,128)(2,1)S(1)} %bitcast.231), channel_id=1, replica_groups=mesh['shard'=4,'context_0'=4,'context_1'=4,'tensor'=2] {'context_0','con..., dimensions={0} | all-to-all | bytes 4718592 | tf_op jit(solution)/shard_map/all_to_all | solution.py:31
  161.1 10.5 %shard_map.188 = (bf16[640,2560]{1,0:T(8,128)(2,1)S(1)}, bf16[640,2560]{1,0:T(8,128)(2,1)}, bf16[4,160,384]{2,1,0:T(8,128)(2,1)}) custom-call(bf16[4,160,2560]{2,1,0:T(8,128)(2,1)} %shard_map.186.own_ref, bf16[4,160,2560]{2,1,0:T(8,128)(2,1)} %collective-permute-done.3.other_ref, f32[1,2560]{1,0:T(1,128)S(1)} %reshape.621.gain_ref, ...), custom_call_target="tpu_custom_call" | custom-call | tf_op jit(solution)/shard_map/pallas_call | solution.py:294
  176.8 7.3 %all-to-all-done.1 = bf16[4,160,384]{2,1,0:T(8,128)(2,1)S(1)} async-done(((bf16[4,160,384]{2,1,0:T(8,128)(2,1)}), bf16[4,160,384]{2,1,0:T(8,128)(2,1)S(1)}, u32[]{:S(2)}, u32[]{:S(2)}) %all-to-all-start.1) | async-done | bytes 491552 | tf_op jit(solution)/shard_map/all_to_all | solution.py:31
  195.1 13.1 %all-to-all-done.2 = bf16[16,160,256]{2,1,0:T(8,128)(2,1)} async-done(((bf16[16,160,256]{2,1,0:T(8,128)(2,1)}), bf16[16,160,256]{2,1,0:T(8,128)(2,1)}, u32[]{:S(2)}, u32[]{:S(2)}) %all-to-all-start.2) | async-done | bytes 1310752 | tf_op jit(solution)/shard_map/all_to_all | solution.py:31
  219.8 8.8 %collective-permute-done.6.before_ref = bf16[16,40,1280]{2,1,0:T(8,128)(2,1)} collective-permute-done((bf16[16,40,1280]{2,1,0:T(8,128)(2,1)}, bf16[16,40,1280]{2,1,0:T(8,128)(2,1)}, u32[]{:S(2)}, u32[]{:S(2)}) %collective-permute-start.6) | collective-permute-done | bytes 1638432 | tf_op jit(solution)/shard_map/ppermute | solution.py:27
  247.1 10.2 %shard_map.189 = bf16[16,4,40,1280]{3,2,1,0:T(8,128)(2,1)} custom-call(bf16[16,40,1280]{2,1,0:T(8,128)(2,1)S(1)} %bitcast.224, bf16[16,40,1280]{2,1,0:T(8,128)(2,1)S(1)} %collective-permute-done.5.behind_ref, bf16[16,40,1280]{2,1,0:T(8,128)(2,1)} %collective-permute-done.6.before_ref, bf16[8,40,1280]{2,1,0:T(8,128)(2,1)S(1)} %collective-permute-done.7.far_one_ref, ...), custom_call_target="tpu_custom_call" | custom-call | tf_op jit(solution)/shard_map/pallas_call | solution.py:145
  257.3 5.1 fusion.145
  262.5 4.7 collective-permute-start.9
  271.0 24.7 %all_to_all.46 = bf16[4,80,2560]{2,1,0:T(8,128)(2,1)S(1)} all-to-all(bf16[4,80,2560]{2,1,0:T(8,128)(2,1)S(1)} %broadcast_in_dim.124), channel_id=1, replica_groups=mesh['shard'=4,'context_0'=4,'context_1'=4,'tensor'=2] {'shard'}, dimensions={0} | all-to-all | bytes 3276800 | tf_op jit(solution)/shard_map/all_to_all | solution.py:31
  295.7 12.7 %collective-permute-start.10 = (bf16[320,2560]{1,0:T(8,128)(2,1)S(1)}, bf16[320,2560]{1,0:T(8,128)(2,1)}, u32[]{:S(2)}, u32[]{:S(2)}) collective-permute-start(bf16[320,2560]{1,0:T(8,128)(2,1)S(1)} %bitcast.235), channel_id=1, source_target_pairs={{0,1},{1,0},{2,3},{3,2},{4,5},{5,4},{6,7},{7,6},{8,9},{9,8},{10,11... | collective-permute-start | bytes 4915208 | tf_op jit(solution)/shard_map/ppermute | solution.py:27
  311.6 10.3 %fusion.10 = f32[640,2048]{1,0:T(8,128)S(1)} fusion(bf16[2560,3072]{1,0:T(8,128)(2,1)} %all-gather.5.cloned.1.call-done, bf16[320,2560]{1,0:T(8,128)(2,1)} %collective-permute-done.10, bf16[320,2560]{1,0:T(8,128)(2,1)S(1)} %bitcast.236), kind=kOutput, calls=%fused_computation.14 | convolution fusion | flops 6717440000 | bytes 19005440 | tf_op jit(solution)/shard_map/dot_general | solution.py:271
  321.9 7.9 %fusion.37 = (bf16[640,1024]{1,0:T(8,128)(2,1)S(1)}, bf16[640,1024]{1,0:T(8,128)(2,1)S(1)}, bf16[640,1024]{1,0:T(8,128)(2,1)S(1)}) fusion(f32[640,2048]{1,0:T(8,128)S(1)} %fusion.10, bf16[640,2560]{1,0:T(8,128)(2,1)S(1)} %copy-done.68, bf16[2560,3072]{1,0:T(8,128)(2,1)} %all-gather.5.cloned.1.call-done), kind=kOutput, calls=%fused_computation.52 | convolution fusion | flops 3372482560 | bytes 17694720 | tf_op jit(solution)/shard_map/dot_general | solution.py:271
  329.8 8.0 %fusion.21 = bf16[320,2560]{1,0:T(8,128)(2,1)S(1)} fusion(bf16[2560,3072]{1,0:T(8,128)(2,1)} %all-gather.5.cloned.1.call-done, bf16[640,1024]{1,0:T(8,128)(2,1)S(1)} %get-tuple-element.42, bf16[640,1024]{1,0:T(8,128)(2,1)S(1)} %get-tuple-element.43), kind=kOutput, calls=%fused_computation.25 | convolution fusion | flops 3358883840 | bytes 14745600 | tf_op jit(solution)/shard_map/dot_general | solution.py:271
  341.6 7.6 %fusion.18 = bf16[320,2560]{1,0:T(8,128)(2,1)S(1)} fusion(bf16[2560,3072]{1,0:T(8,128)(2,1)} %all-gather.5.cloned.1.call-done, bf16[320,2560]{1,0:T(8,128)(2,1)S(1)} %collective-permute-done.14, bf16[640,1024]{1,0:T(8,128)(2,1)S(1)} %get-tuple-element.42, bf16[640,1024]{1,0:T(8,128)(2,1)S(1)} %get-tuple-element.43), kind=kOutput, calls=%fused_computation.24 | convolution fusion | flops 3360522240 | bytes 16384000 | tf_op jit(solution)/shard_map/dot_general | solution.py:271
  350.4 20.8 %shard_map.192.refs_1_ = bf16[2560,3072]{1,0:T(8,128)(2,1)} custom-call(bf16[640,2560]{1,0:T(8,128)(2,1)} %pad_maximum_fusion.1.x_ref.refs_1_, bf16[640,2560]{1,0:T(8,128)(2,1)} %get-tuple-element.21.y_ref, bf16[640,2048]{1,0:T(8,128)(2,1)S(1)} %pad_maximum_fusion.gate_up_ref, bf16[640,1024]{1,0:T(8,128)(2,1)S(1)} %get-tuple-element.44.hidden_ref.refs_0_, ...), custom_call_target="tpu_custom_call" | custom-call | flops 10066329600 | bytes 15728640 | tf_op jit(solution)/shard_map/pallas_call | solution.py:212
  371.2 23.9 %all_to_all.47 = bf16[4,80,2560]{2,1,0:T(8,128)(2,1)S(1)} all-to-all(bf16[4,80,2560]{2,1,0:T(8,128)(2,1)S(1)} %bitcast.249), channel_id=1, replica_groups=mesh['shard'=4,'context_0'=4,'context_1'=4,'tensor'=2] {'shard'}, dimensions={0} | all-to-all | bytes 3276800 | tf_op jit(solution)/shard_map/all_to_all | solution.py:31
  413.3 4.9 select_convert_fusion
  432.3 6.2 all-to-all-start.6
  438.6 5.8 convolution_convert_fusion.3
  490.0 6.1 fusion.17
  512.0 5.5 all-to-all-start.7
  527.3 23.2 %collective-permute-done.24 = bf16[80,2560]{1,0:T(8,128)(2,1)S(1)} collective-permute-done((bf16[80,2560]{1,0:T(8,128)(2,1)S(1)}, bf16[80,2560]{1,0:T(8,128)(2,1)S(1)}, u32[]{:S(2)}, u32[]{:S(2)}) %collective-permute-start.24) | collective-permute-done | bytes 409632 | tf_op jit(solution)/shard_map/ppermute | solution.py:27
  550.4 8.1 %collective-permute-done.26 = bf16[80,2560]{1,0:T(8,128)(2,1)S(1)} collective-permute-done((bf16[80,2560]{1,0:T(8,128)(2,1)S(1)}, bf16[80,2560]{1,0:T(8,128)(2,1)S(1)}, u32[]{:S(2)}, u32[]{:S(2)}) %collective-permute-start.26) | collective-permute-done | bytes 409632 | tf_op jit(solution)/shard_map/ppermute | solution.py:27
  562.9 5.1 collective-permute-done.35
  568.0 8.2 %collective-permute-done.37 = bf16[80,2560]{1,0:T(8,128)(2,1)S(1)} collective-permute-done((bf16[80,2560]{1,0:T(8,128)(2,1)S(1)}, bf16[80,2560]{1,0:T(8,128)(2,1)S(1)}, u32[]{:S(2)}, u32[]{:S(2)}) %collective-permute-start.37) | collective-permute-done | bytes 409632 | tf_op jit(solution)/shard_map/ppermute | solution.py:27
  577.0 9.0 %all-to-all-start.8 = ((bf16[64,40,320]{2,1,0:T(8,128)(2,1)}), bf16[64,40,320]{2,1,0:T(8,128)(2,1)S(1)}, u32[]{:S(2)}, u32[]{:S(2)}) async-start(bf16[64,40,320]{2,1,0:T(8,128)(2,1)} %shard_map.206), calls=%async_computation.9 | async-start | bytes 3932160 | tf_op jit(solution)/shard_map/all_to_all | solution.py:31
  598.3 15.0 %collective-permute-done.41.b3 = bf16[40,3072]{1,0:T(8,128)(2,1)S(1)} collective-permute-done((bf16[40,3072]{1,0:T(8,128)(2,1)S(1)}, bf16[40,3072]{1,0:T(8,128)(2,1)S(1)}, u32[]{:S(2)}, u32[]{:S(2)}) %collective-permute-start.41) | collective-permute-done | bytes 245792 | tf_op jit(solution)/shard_map/ppermute | solution.py:27
  614.8 5.6 collective-permute-done.39.b1
  (388 shorter events, 210.0 us)
Async XLA Ops:
  7.2 185.2 %all-gather.3.cloned.1.call-start = ((), (), s32[]{:S(2)}) async-start(), calls=%async_computation.10 | async-start | bytes 1740800 | tf_op jit(solution)/shard_map/all_gather | solution.py:443
  7.9 303.7 %all-gather.5.cloned.1.call-start = ((), (), s32[]{:S(2)}) async-start(), calls=%async_computation.11 | async-start | bytes 16711680 | tf_op jit(solution)/shard_map/all_gather | solution.py:468
  13.3 20.5 %collective-permute-start = (bf16[160,2560]{1,0:T(8,128)(2,1)S(1)}, bf16[160,2560]{1,0:T(8,128)(2,1)S(1)}, u32[]{:S(2)}, u32[]{:S(2)}) collective-permute-start(bf16[160,2560]{1,0:T(8,128)(2,1)S(1)} %pad_maximum_fusion.2.refs_0_), channel_id=1, source_target_pairs={{0,96},{32,0},{64,32},{96,64},{1,97},{33,1},{65,33},{97,65},{2,98}... | collective-permute-start | bytes 2457608 | tf_op jit(solution)/shard_map/ppermute | solution.py:27
  52.7 37.8 %collective-permute-start.2 = (bf16[160,2560]{1,0:T(8,128)(2,1)S(1)}, bf16[160,2560]{1,0:T(8,128)(2,1)S(1)}, u32[]{:S(2)}, u32[]{:S(2)}) collective-permute-start(bf16[160,2560]{1,0:T(8,128)(2,1)S(1)} %pad_maximum_fusion.2.refs_0_), channel_id=1, source_target_pairs={{0,32},{32,64},{64,96},{96,0},{1,33},{33,65},{65,97},{97,1},{2,34}... | collective-permute-start | bytes 2457608 | tf_op jit(solution)/shard_map/ppermute | solution.py:27
  52.8 37.8 %collective-permute-start.1 = (bf16[160,2560]{1,0:T(8,128)(2,1)S(1)}, bf16[160,2560]{1,0:T(8,128)(2,1)S(1)}, u32[]{:S(2)}, u32[]{:S(2)}) collective-permute-start(bf16[160,2560]{1,0:T(8,128)(2,1)S(1)} %pad_maximum_fusion.2.refs_0_), channel_id=1, source_target_pairs={{0,64},{32,96},{64,0},{96,32},{1,65},{33,97},{65,1},{97,33},{2,66}... | collective-permute-start | bytes 2457608 | tf_op jit(solution)/shard_map/ppermute | solution.py:27
  92.3 68.8 %collective-permute-start.3 = (bf16[4,160,2560]{2,1,0:T(8,128)(2,1)}, bf16[4,160,2560]{2,1,0:T(8,128)(2,1)}, u32[]{:S(2)}, u32[]{:S(2)}) collective-permute-start(bf16[4,160,2560]{2,1,0:T(8,128)(2,1)} %shard_map.186.own_ref), channel_id=1, source_target_pairs={{0,1},{1,0},{2,3},{3,2},{4,5},{5,4},{6,7},{7,6},{8,9},{9,8},{10,11... | collective-permute-start | bytes 9830408 | tf_op jit(solution)/shard_map/ppermute | solution.py:27
  186.9 21.3 %all-to-all-start.2 = ((bf16[16,160,256]{2,1,0:T(8,128)(2,1)}), bf16[16,160,256]{2,1,0:T(8,128)(2,1)}, u32[]{:S(2)}, u32[]{:S(2)}) async-start(bf16[16,160,256]{2,1,0:T(8,128)(2,1)} %broadcast_in_dim.117), calls=%async_computation.2 | async-start | bytes 2621440 | tf_op jit(solution)/shard_map/all_to_all | solution.py:31
  191.3 394.8 %reduce-scatter.2.cloned.1.call-start = ((), (), s32[]{:S(2)}) async-start(), calls=%async_computation.12 | async-start | bytes 16711680 | tf_op jit(solution)/shard_map/reduce_scatter | solution.py:520
  192.4 36.1 %collective-permute-start.6 = (bf16[16,40,1280]{2,1,0:T(8,128)(2,1)}, bf16[16,40,1280]{2,1,0:T(8,128)(2,1)}, u32[]{:S(2)}, u32[]{:S(2)}) collective-permute-start(bf16[16,40,1280]{2,1,0:T(8,128)(2,1)} %bitcast.222), channel_id=1, source_target_pairs={{0,32},{32,64},{64,96},{96,0},{1,33},{33,65},{65,97},{97,1},{2,34}... | collective-permute-start | bytes 4915208 | tf_op jit(solution)/shard_map/ppermute | solution.py:27
  193.1 36.7 %collective-permute-start.5 = (bf16[16,40,1280]{2,1,0:T(8,128)(2,1)}, bf16[16,40,1280]{2,1,0:T(8,128)(2,1)S(1)}, u32[]{:S(2)}, u32[]{:S(2)}) collective-permute-start(bf16[16,40,1280]{2,1,0:T(8,128)(2,1)} %bitcast.223), channel_id=1, source_target_pairs={{0,96},{32,0},{64,32},{96,64},{1,97},{33,1},{65,33},{97,65},{2,98}... | collective-permute-start | bytes 4915208 | tf_op jit(solution)/shard_map/ppermute | solution.py:27
  208.3 24.3 %collective-permute-start.4 = (bf16[2560,256]{1,0:T(8,128)(2,1)}, bf16[2560,256]{1,0:T(8,128)(2,1)}, u32[]{:S(2)}, u32[]{:S(2)}) collective-permute-start(bf16[2560,256]{1,0:T(8,128)(2,1)} %bitcast.18), channel_id=1, source_target_pairs={{0,1},{1,0},{2,3},{3,2},{4,5},{5,4},{6,7},{7,6},{8,9},{9,8},{10,11... | collective-permute-start | bytes 3932168 | tf_op jit(solution)/shard_map/ppermute | solution.py:27
  229.7 17.4 %collective-permute-start.7 = (bf16[8,40,1280]{2,1,0:T(8,128)(2,1)S(1)}, bf16[8,40,1280]{2,1,0:T(8,128)(2,1)S(1)}, u32[]{:S(2)}, u32[]{:S(2)}) collective-permute-start(bf16[8,40,1280]{2,1,0:T(8,128)(2,1)S(1)} %slice.188), channel_id=1, source_target_pairs={{0,32},{32,64},{64,96},{96,0},{1,33},{33,65},{65,97},{97,1},{2,34}... | collective-permute-start | bytes 2457608 | tf_op jit(solution)/shard_map/ppermute | solution.py:27
  426.1 19.6 %collective-permute-start.19 = (bf16[80,2560]{1,0:T(8,128)(2,1)S(1)}, bf16[80,2560]{1,0:T(8,128)(2,1)S(1)}, u32[]{:S(2)}, u32[]{:S(2)}) collective-permute-start(bf16[80,2560]{1,0:T(8,128)(2,1)S(1)} %copy-done.12), channel_id=1, source_target_pairs={{0,32},{32,64},{64,96},{96,0},{1,33},{33,65},{65,97},{97,1},{2,34}... | collective-permute-start | bytes 1228808 | tf_op jit(solution)/shard_map/ppermute | solution.py:27
  426.7 20.4 %collective-permute-start.18 = (bf16[80,2560]{1,0:T(8,128)(2,1)S(1)}, bf16[80,2560]{1,0:T(8,128)(2,1)S(1)}, u32[]{:S(2)}, u32[]{:S(2)}) collective-permute-start(bf16[80,2560]{1,0:T(8,128)(2,1)S(1)} %copy-done.12), channel_id=1, source_target_pairs={{0,64},{32,96},{64,0},{96,32},{1,65},{33,97},{65,1},{97,33},{2,66}... | collective-permute-start | bytes 1228808 | tf_op jit(solution)/shard_map/ppermute | solution.py:27
  428.5 19.2 %collective-permute-start.17 = (bf16[80,2560]{1,0:T(8,128)(2,1)S(1)}, bf16[80,2560]{1,0:T(8,128)(2,1)S(1)}, u32[]{:S(2)}, u32[]{:S(2)}) collective-permute-start(bf16[80,2560]{1,0:T(8,128)(2,1)S(1)} %copy-done.12), channel_id=1, source_target_pairs={{0,96},{32,0},{64,32},{96,64},{1,97},{33,1},{65,33},{97,65},{2,98}... | collective-permute-start | bytes 1228808 | tf_op jit(solution)/shard_map/ppermute | solution.py:27
  432.3 30.4 %all-to-all-start.6 = ((bf16[16,160,256]{2,1,0:T(8,128)(2,1)}), bf16[16,160,256]{2,1,0:T(8,128)(2,1)}, u32[]{:S(2)}, u32[]{:S(2)}) async-start(bf16[16,160,256]{2,1,0:T(8,128)(2,1)} %bitcast.240), calls=%async_computation.6 | async-start | bytes 2621440 | tf_op jit(solution)/shard_map/all_to_all | solution.py:31
  444.4 45.6 %collective-permute-start.16 = (bf16[320,2560]{1,0:T(8,128)(2,1)}, bf16[320,2560]{1,0:T(8,128)(2,1)}, u32[]{:S(2)}, u32[]{:S(2)}) collective-permute-start(bf16[320,2560]{1,0:T(8,128)(2,1)} %convolution_convert_fusion.3), channel_id=1, source_target_pairs={{0,1},{1,0},{2,3},{3,2},{4,5},{5,4},{6,7},{7,6},{8,9},{9,8},{10,11... | collective-permute-start | bytes 4915208 | tf_op jit(solution)/shard_map/ppermute | solution.py:27
  448.9 47.2 %collective-permute-start.20 = (bf16[320,2560]{1,0:T(8,128)(2,1)}, bf16[320,2560]{1,0:T(8,128)(2,1)}, u32[]{:S(2)}, u32[]{:S(2)}) collective-permute-start(bf16[320,2560]{1,0:T(8,128)(2,1)} %bitcast.34), channel_id=1, source_target_pairs={{0,1},{1,0},{2,3},{3,2},{4,5},{5,4},{6,7},{7,6},{8,9},{9,8},{10,11... | collective-permute-start | bytes 4915208 | tf_op jit(solution)/shard_map/ppermute | solution.py:27
  489.7 33.6 %collective-permute-start.34 = (bf16[320,2560]{1,0:T(8,128)(2,1)}, bf16[320,2560]{1,0:T(8,128)(2,1)}, u32[]{:S(2)}, u32[]{:S(2)}) collective-permute-start(bf16[320,2560]{1,0:T(8,128)(2,1)} %convolution_convert_fusion.1), channel_id=1, source_target_pairs={{0,1},{1,0},{2,3},{3,2},{4,5},{5,4},{6,7},{7,6},{8,9},{9,8},{10,11... | collective-permute-start | bytes 4915208 | tf_op jit(solution)/shard_map/ppermute | solution.py:27
  512.0 64.6 %all-to-all-start.7 = ((bf16[64,40,384]{2,1,0:T(8,128)(2,1)}), bf16[64,40,384]{2,1,0:T(8,128)(2,1)}, u32[]{:S(2)}, u32[]{:S(2)}) async-start(bf16[64,40,384]{2,1,0:T(8,128)(2,1)} %bitcast.247), calls=%async_computation.8 | async-start | bytes 3932160 | tf_op jit(solution)/shard_map/all_to_all | solution.py:31
  518.9 31.6 %collective-permute-start.24 = (bf16[80,2560]{1,0:T(8,128)(2,1)S(1)}, bf16[80,2560]{1,0:T(8,128)(2,1)S(1)}, u32[]{:S(2)}, u32[]{:S(2)}) collective-permute-start(bf16[80,2560]{1,0:T(8,128)(2,1)S(1)} %get-tuple-element.48), channel_id=1, source_target_pairs={{0,32},{32,64},{64,96},{96,0},{1,33},{33,65},{65,97},{97,1},{2,34}... | collective-permute-start | bytes 1228808 | tf_op jit(solution)/shard_map/ppermute | solution.py:27
  519.8 38.8 %collective-permute-start.26 = (bf16[80,2560]{1,0:T(8,128)(2,1)S(1)}, bf16[80,2560]{1,0:T(8,128)(2,1)S(1)}, u32[]{:S(2)}, u32[]{:S(2)}) collective-permute-start(bf16[80,2560]{1,0:T(8,128)(2,1)S(1)} %get-tuple-element.49), channel_id=1, source_target_pairs={{0,64},{32,96},{64,0},{96,32},{1,65},{33,97},{65,1},{97,33},{2,66}... | collective-permute-start | bytes 1228808 | tf_op jit(solution)/shard_map/ppermute | solution.py:27
  522.2 36.4 %collective-permute-start.25 = (bf16[80,2560]{1,0:T(8,128)(2,1)S(1)}, bf16[80,2560]{1,0:T(8,128)(2,1)S(1)}, u32[]{:S(2)}, u32[]{:S(2)}) collective-permute-start(bf16[80,2560]{1,0:T(8,128)(2,1)S(1)} %get-tuple-element.50), channel_id=1, source_target_pairs={{0,96},{32,0},{64,32},{96,64},{1,97},{33,1},{65,33},{97,65},{2,98}... | collective-permute-start | bytes 1228808 | tf_op jit(solution)/shard_map/ppermute | solution.py:27
  526.0 41.9 %collective-permute-start.35 = (bf16[80,2560]{1,0:T(8,128)(2,1)S(1)}, bf16[80,2560]{1,0:T(8,128)(2,1)S(1)}, u32[]{:S(2)}, u32[]{:S(2)}) collective-permute-start(bf16[80,2560]{1,0:T(8,128)(2,1)S(1)} %get-tuple-element.45), channel_id=1, source_target_pairs={{0,32},{32,64},{64,96},{96,0},{1,33},{33,65},{65,97},{97,1},{2,34}... | collective-permute-start | bytes 1228808 | tf_op jit(solution)/shard_map/ppermute | solution.py:27
  526.4 49.8 %collective-permute-start.37 = (bf16[80,2560]{1,0:T(8,128)(2,1)S(1)}, bf16[80,2560]{1,0:T(8,128)(2,1)S(1)}, u32[]{:S(2)}, u32[]{:S(2)}) collective-permute-start(bf16[80,2560]{1,0:T(8,128)(2,1)S(1)} %get-tuple-element.46), channel_id=1, source_target_pairs={{0,64},{32,96},{64,0},{96,32},{1,65},{33,97},{65,1},{97,33},{2,66}... | collective-permute-start | bytes 1228808 | tf_op jit(solution)/shard_map/ppermute | solution.py:27
  550.4 25.7 %collective-permute-start.36 = (bf16[80,2560]{1,0:T(8,128)(2,1)S(1)}, bf16[80,2560]{1,0:T(8,128)(2,1)S(1)}, u32[]{:S(2)}, u32[]{:S(2)}) collective-permute-start(bf16[80,2560]{1,0:T(8,128)(2,1)S(1)} %get-tuple-element.47), channel_id=1, source_target_pairs={{0,96},{32,0},{64,32},{96,64},{1,97},{33,1},{65,33},{97,65},{2,98}... | collective-permute-start | bytes 1228808 | tf_op jit(solution)/shard_map/ppermute | solution.py:27
  560.6 63.3 %collective-permute-start.27 = (bf16[80,2560]{1,0:T(8,128)(2,1)S(1)}, bf16[80,2560]{1,0:T(8,128)(2,1)S(1)}, u32[]{:S(2)}, u32[]{:S(2)}) collective-permute-start(bf16[80,2560]{1,0:T(8,128)(2,1)S(1)} %shard_map.198.mine_ref), channel_id=1, source_target_pairs={{0,1},{1,0},{2,3},{3,2},{4,5},{5,4},{6,7},{7,6},{8,9},{9,8},{10,11... | collective-permute-start | bytes 1228808 | tf_op jit(solution)/shard_map/ppermute | solution.py:27
  577.0 47.8 %all-to-all-start.8 = ((bf16[64,40,320]{2,1,0:T(8,128)(2,1)}), bf16[64,40,320]{2,1,0:T(8,128)(2,1)S(1)}, u32[]{:S(2)}, u32[]{:S(2)}) async-start(bf16[64,40,320]{2,1,0:T(8,128)(2,1)} %shard_map.206), calls=%async_computation.9 | async-start | bytes 3932160 | tf_op jit(solution)/shard_map/all_to_all | solution.py:31
  587.5 25.7 %collective-permute-start.41 = (bf16[40,3072]{1,0:T(8,128)(2,1)S(1)}, bf16[40,3072]{1,0:T(8,128)(2,1)S(1)}, u32[]{:S(2)}, u32[]{:S(2)}) collective-permute-start(bf16[40,3072]{1,0:T(8,128)(2,1)S(1)} %get-tuple-element.55), channel_id=1, source_target_pairs={{0,96},{32,0},{64,32},{96,64},{1,97},{33,1},{65,33},{97,65},{2,98}... | collective-permute-start | bytes 737288 | tf_op jit(solution)/shard_map/ppermute | solution.py:27
  589.8 24.9 %collective-permute-start.40 = (bf16[40,3072]{1,0:T(8,128)(2,1)S(1)}, bf16[40,3072]{1,0:T(8,128)(2,1)S(1)}, u32[]{:S(2)}, u32[]{:S(2)}) collective-permute-start(bf16[40,3072]{1,0:T(8,128)(2,1)S(1)} %get-tuple-element.56), channel_id=1, source_target_pairs={{0,64},{32,96},{64,0},{96,32},{1,65},{33,97},{65,1},{97,33},{2,66}... | collective-permute-start | bytes 737288 | tf_op jit(solution)/shard_map/ppermute | solution.py:27
  590.4 30.0 %collective-permute-start.39 = (bf16[40,3072]{1,0:T(8,128)(2,1)S(1)}, bf16[40,3072]{1,0:T(8,128)(2,1)S(1)}, u32[]{:S(2)}, u32[]{:S(2)}) collective-permute-start(bf16[40,3072]{1,0:T(8,128)(2,1)S(1)} %get-tuple-element.57), channel_id=1, source_target_pairs={{0,32},{32,64},{64,96},{96,0},{1,33},{33,65},{65,97},{97,1},{2,34}... | collective-permute-start | bytes 737288 | tf_op jit(solution)/shard_map/ppermute | solution.py:27
  593.8 31.9 %collective-permute-start.38 = (bf16[80,2560]{1,0:T(8,128)(2,1)S(1)}, bf16[80,2560]{1,0:T(8,128)(2,1)}, u32[]{:S(2)}, u32[]{:S(2)}) collective-permute-start(bf16[80,2560]{1,0:T(8,128)(2,1)S(1)} %shard_map.202.mine_ref), channel_id=1, source_target_pairs={{0,1},{1,0},{2,3},{3,2},{4,5},{5,4},{6,7},{7,6},{8,9},{9,8},{10,11... | collective-permute-start | bytes 1228808 | tf_op jit(solution)/shard_map/ppermute | solution.py:27
  (95 other events, 2162.6 us)
Sparse Core Ops, SparseCore 0:
  10.2 46.3 all-gather.2
  58.9 131.8 all-gather.4
  371.3 116.0 reduce-scatter.1

commit v4 on v3

v4 whole, which is shorter than its diff:
```python
import functools

import jax
import jax.numpy as jnp
from jax import lax
from jax.experimental import pallas as pl
from jax.experimental.pallas import tpu as pltpu
from jax.sharding import Mesh
from jax.sharding import PartitionSpec as P

WINDOW = 2048
SHARD_CONTEXT = ("shard", "context_0", "context_1")
CONTEXT = ("context_0", "context_1")
PIECES = ("context_0", "context_1", "shard")
Y, X, Z, T = "shard", "context_0", "context_1", "tensor"
VMEM = pltpu.CompilerParams(vmem_limit_bytes=48 * 2**20)
ANYWHERE = pl.BlockSpec(memory_space=pl.ANY)

EPSILON = 1e-06
NEGATIVE_FILL = -1e30
BF = jnp.bfloat16
F32 = jnp.float32


def shift(x, axis, by):
    n = lax.axis_size(axis)
    return lax.ppermute(x, axis, [(i, (i + by) % n) for i in range(n)])


def exchange(blocks, axis):
    return lax.all_to_all(blocks, axis, 0, 0, tiled=True)


def nothing(*refs):
    pass


def after(x, *others):
    return pl.pallas_call(
        nothing,
        out_shape=jax.ShapeDtypeStruct(x.shape, x.dtype),
        in_specs=[ANYWHERE] * (1 + len(others)),
        out_specs=ANYWHERE,
        input_output_aliases={0: 0},
        compiler_params=VMEM,
    )(x, *others)


def small_trip(x, *others):
    corner = x.reshape(-1, x.shape[-1])[:8, :128]
    return shift(after(corner, *others) if others else corner, T, 1)


def ring_blocks(x, axis):
    return [x, shift(x, axis, -1), shift(x, axis, 2), shift(x, axis, 1)]


def place_kernel(axis, sign, *refs):
    blocks, out = refs[:4], refs[-1]
    me = lax.axis_index(axis)
    for r, block in enumerate(blocks):
        out[lax.rem(me + (sign * r) % 4, 4)] = block[...]


def place(blocks, axis, *first, sign=1):
    whole = pl.BlockSpec(memory_space=pltpu.VMEM)
    return pl.pallas_call(
        functools.partial(place_kernel, axis, sign),
        out_shape=jax.ShapeDtypeStruct((4, *blocks[0].shape), blocks[0].dtype),
        in_specs=[whole] * 4 + [ANYWHERE] * len(first),
        out_specs=whole,
        compiler_params=VMEM,
    )(*blocks, *first)


def gather_rows(mine, *first):
    own = place(ring_blocks(mine, Y), Y, *first).reshape(320, -1)
    return own, shift(own, T, 1)


def rows_kernel(count, *refs):
    lefts, rights, (far_ref, near_ref) = refs[:count], refs[count : 2 * count], refs[-2:]
    total = dot(lefts[0][...], rights[0][...], 1, 1)
    for left, right in zip(lefts[1:], rights[1:]):
        total = total + dot(left[...], right[...], 1, 1)
    near_ref[...] = total[:320].astype(BF)
    far_ref[...] = total[320:].astype(BF)


def row_products(lefts, weight, at, width, *first):
    rows, count, n = 256, len(lefts), weight.shape[0]
    half = jax.ShapeDtypeStruct((320, n), BF)
    return pl.pallas_call(
        functools.partial(rows_kernel, count),
        grid=(n // rows,),
        out_shape=(half, half),
        in_specs=[pl.BlockSpec((640, width), lambda i: (0, 0))] * count
        + [pl.BlockSpec((rows, width), lambda i, j=j: (i, at + j)) for j in range(count)]
        + [ANYWHERE] * len(first),
        out_specs=(pl.BlockSpec((320, rows), lambda i: (0, i)),) * 2,
        compiler_params=VMEM,
    )(*lefts, *[weight] * count, *first)


def scatter_parts(lefts, weight, at, width, *first):
    far, near = row_products(lefts, weight, at, width, *first)
    return (near.astype(F32) + shift(far, T, 1).astype(F32)).astype(BF).reshape(4, 80, -1)


def scatter_blocks(low):
    me = lax.axis_index(Y)
    return [lax.dynamic_index_in_dim(low, (me + r) % 4, 0, keepdims=False) for r in range(4)]


def scatter_sum(blocks):
    return scatter_total(blocks[0], [shift(blocks[r], Y, r) for r in (1, 3, 2)])


def scatter_total(own, got):
    total = own.astype(F32)
    for block in got:
        total = total + block.astype(F32)
    return total


def outer_kernel(x_ref, g_ref, y_ref, h_ref, out_ref):
    split = g_ref.shape[1]
    out_ref[:, :split] = dot(x_ref[...], g_ref[...], 0, 0).astype(BF)
    out_ref[:, split:] = dot(y_ref[...], h_ref[...], 0, 0).astype(BF)


def outer(x, g, y, h):
    rows, n, cols = 512, x.shape[1], g.shape[1] + h.shape[1]
    left = pl.BlockSpec((640, rows), lambda i: (0, i))
    right = [pl.BlockSpec((640, a.shape[1]), lambda i: (0, 0)) for a in (g, h)]
    return pl.pallas_call(
        outer_kernel,
        grid=(n // rows,),
        out_shape=jax.ShapeDtypeStruct((n, cols), BF),
        in_specs=[left, right[0], left, right[1]],
        out_specs=pl.BlockSpec((rows, cols), lambda i: (i, 0)),
        compiler_params=VMEM,
    )(x, g, y, h)


def summed_over(parts, axis, dim):
    me = lax.axis_index(axis)
    own, *rest = [
        lax.dynamic_index_in_dim(parts, (me + r) % 4, dim, keepdims=False) for r in range(4)
    ]
    return scatter_total(own, [shift(rest[r - 1], axis, r) for r in (1, 3, 2)]).astype(BF)


def scatter_context(parts):
    grid = parts.reshape(4, 4, 160, -1)
    one = summed_over(grid[:, :, :80], X, 0)
    two = summed_over(grid[:, :, 80:], Z, 1)
    return jnp.concatenate([summed_over(one, Z, 0), summed_over(two, X, 0)])


def to_owners(sums):
    me = lax.axis_index(Y)
    rows = sums.reshape(4, 40, -1)
    got = []
    for r in range(4):
        block = lax.dynamic_index_in_dim(rows, (me + r) % 4, 0, keepdims=False)
        got.append(shift(block, Y, r) if r else block)
    return got


def by_half(blocks):
    cols = blocks.shape[2]
    return blocks.reshape(4, 2, 80, cols).swapaxes(0, 1).reshape(640, cols)


def columns_out(x):
    me = lax.axis_index(Y)
    blocks = quarters(x)
    got = []
    for r in range(4):
        block = lax.dynamic_index_in_dim(blocks, (me + r) % 4, 0, keepdims=False)
        got.append(shift(block, Y, r) if r else block)
    return by_half(place(got, Y, sign=-1))


def quarters(x):
    rows = x.shape[0]
    return x.reshape(rows, 4, -1).swapaxes(0, 1)


def joined(blocks):
    return blocks.swapaxes(0, 1).reshape(blocks.shape[1], -1)


def pack_attention_kernel(q_ref, kv_ref, gains_ref, _, attn_ref):
    attn_ref[...] = jnp.zeros_like(attn_ref)
    for j in range(4):
        attn_ref[j, :40, :320] = q_ref[:, 320 * j : 320 * j + 320]
        attn_ref[j, :40, 320:] = kv_ref[:, 64 * j : 64 * j + 64]
        attn_ref[j, 40:48, :128] = gains_ref[...]


def pack_attention(w_query, keyval_half, gains, first):
    whole = pl.BlockSpec(memory_space=pltpu.VMEM)
    return pl.pallas_call(
        pack_attention_kernel,
        out_shape=jax.ShapeDtypeStruct((4, 48, 384), BF),
        in_specs=[whole, whole, whole, ANYWHERE],
        compiler_params=VMEM,
    )(w_query, keyval_half, gains, first)


def pack_mlp_kernel(gate_ref, up_ref, down_ref, mlp_ref):
    mlp_ref[...] = jnp.zeros_like(mlp_ref)
    for j in range(4):
        mlp_ref[j, :, :960] = gate_ref[:, 960 * j : 960 * j + 960]
        mlp_ref[j, :, 1024:1984] = up_ref[:, 960 * j : 960 * j + 960]
        mlp_ref[j, :, 2048:3008] = down_ref[:, 960 * j : 960 * j + 960]


def pack_mlp(w_gate, w_up, w_down):
    return pl.pallas_call(
        pack_mlp_kernel,
        out_shape=jax.ShapeDtypeStruct((4, 40, 3072), BF),
        compiler_params=VMEM,
    )(w_gate, w_up, w_down)


def mlp_grad_kernel(x_ref, y_ref, gate_ref, up_ref, hidden_ref, *rest):
    out_ref = rest[-1]
    j = pl.program_id(0)

    @pl.when(j == 0)
    def _():
        out_ref[...] = dot(x_ref[...], gate_ref[...], 0, 0).astype(BF)

    @pl.when(j == 1)
    def _():
        out_ref[...] = dot(x_ref[...], up_ref[...], 0, 0).astype(BF)

    @pl.when(j == 2)
    def _():
        out_ref[...] = dot(y_ref[...], hidden_ref[...], 0, 0).astype(BF)


def mlp_grads(normed, grads, gate, up, hidden, *first):
    rows = 512
    whole = pl.BlockSpec((640, 1024), lambda j, i: (0, 0))
    return pl.pallas_call(
        mlp_grad_kernel,
        grid=(3, 2560 // rows),
        out_shape=jax.ShapeDtypeStruct((2560, 3072), BF),
        in_specs=[
            pl.BlockSpec((640, rows), lambda j, i: (0, jnp.where(j < 2, i, 4))),
            pl.BlockSpec((640, rows), lambda j, i: (0, jnp.where(j < 2, 0, i))),
            whole,
            whole,
            whole,
        ]
        + [ANYWHERE] * len(first),
        out_specs=pl.BlockSpec((rows, 1024), lambda j, i: (i, j)),
        compiler_params=VMEM,
    )(normed, grads, gate, up, hidden, *first)


def feed_forward_kernel(x_ref, y_ref, gate_ref, up_ref, down_ref, hidden_out, gate_out, up_out):
    gate = dot(x_ref[...], gate_ref[...], 1, 0)
    up = dot(x_ref[...], up_ref[...], 1, 0)
    grad = dot(y_ref[...], down_ref[...], 1, 0)
    scale = 0.7978845608028654
    square = gate * gate
    bent = jnp.tanh(scale * gate * (1.0 + 0.044715 * square))
    share = 0.5 * (1.0 + bent)
    slope = share + 0.5 * gate * (1.0 - bent * bent) * scale * (1.0 + 0.134145 * square)
    active = gate * share
    hidden_out[...] = (active * up).astype(BF)
    gate_out[...] = (grad * up * slope).astype(BF)
    up_out[...] = (grad * active).astype(BF)


def feed_forward(x, y, w_mlp):
    cols = 256
    steps = 1024 // cols
    part = jax.ShapeDtypeStruct((640, 1024), BF)
    whole = pl.BlockSpec((640, 2560), lambda j: (0, 0))
    out = pl.BlockSpec((640, cols), lambda j: (0, j))
    return pl.pallas_call(
        feed_forward_kernel,
        grid=(steps,),
        out_shape=(part, part, part),
        in_specs=[whole, whole]
        + [pl.BlockSpec((2560, cols), lambda j, k=k: (0, k * steps + j)) for k in range(3)],
        out_specs=(out, out, out),
        compiler_params=VMEM,
    )(x, y, w_mlp, w_mlp, w_mlp)


def to_piece_order(x):
    rows = x.shape[0]
    return x.reshape(rows, 4, 16, 40).swapaxes(1, 2).reshape(rows, 2560)


def inverse_root(values):
    return lax.rsqrt(jnp.mean(values * values, axis=-1, keepdims=True) + EPSILON)


def norm_back(grad, values, inverse, gain):
    scaled = gain * grad
    return inverse * scaled - values * inverse**3 * jnp.mean(
        scaled * values, axis=-1, keepdims=True
    )


def angles(position, head_dim):
    quarter = head_dim // 4
    frequency = 10000.0 ** (-jnp.arange(quarter, dtype=F32) / quarter)
    phase_angle = position[:, None].astype(F32) * frequency[None, :]
    return (jnp.cos(phase_angle), jnp.sin(phase_angle))


def rotate(values, cosine, sine_part):
    quarter = cosine.shape[-1]
    first_half = values[..., :quarter]
    second = values[..., quarter : 2 * quarter]
    cos_rows = cosine[:, None, :]
    sin_rows = sine_part[:, None, :]
    return jnp.concatenate(
        [
            first_half * cos_rows - second * sin_rows,
            second * cos_rows + first_half * sin_rows,
            values[..., 2 * quarter :],
        ],
        axis=-1,
    )


def dot(a, b, da, db):
    return lax.dot_general(a, b, (((da,), (db,)), ((), ())), preferred_element_type=F32)


def project_kernel(own_ref, other_ref, gain_ref, weight_ref, normed_ref, out_ref):
    def rows(block):
        x = block[...].astype(F32)
        normed = (x * inverse_root(x) * gain_ref[...]).astype(BF)
        normed_ref[...] = normed
        out_ref[0] = dot(normed, weight_ref[...], 1, 0).astype(BF)

    i = pl.program_id(0)

    @pl.when(i < 4)
    def _():
        rows(own_ref)

    @pl.when(i >= 4)
    def _():
        rows(other_ref)


def project(own, other, gain, weight):
    return pl.pallas_call(
        project_kernel,
        grid=(8,),
        out_shape=(
            jax.ShapeDtypeStruct((640, 2560), BF),
            jax.ShapeDtypeStruct((4, 160, 384), BF),
        ),
        in_specs=[
            pl.BlockSpec((80, 2560), lambda i: (jnp.minimum(i, 3), 0)),
            pl.BlockSpec((80, 2560), lambda i: (jnp.maximum(i, 4) - 4, 0)),
            pl.BlockSpec((1, 2560), lambda i: (0, 0)),
            pl.BlockSpec((2560, 384), lambda i: (0, 0)),
        ],
        out_specs=(
            pl.BlockSpec((80, 2560), lambda i: (i, 0)),
            pl.BlockSpec((1, 80, 384), lambda i: (i % 4, i // 4, 0)),
        ),
        compiler_params=VMEM,
    )(own, other, gain, weight)


def owned_kernel(b0, b1, b2, b3, query_ref, keyval_ref, *rest):
    query_out, keyval_out, output_out, gain_out, held = rest[-5:]
    me = lax.axis_index(Y)
    for r, block in enumerate((b0, b1, b2, b3)):
        held[lax.rem(me + 4 - r, 4)] = block[...]
    for j in range(4):
        total = held[j].astype(F32)
        query_out[:, 320 * j : 320 * j + 320] = total[:, :320]
        keyval_out[:, 64 * j : 64 * j + 64] = total[:, 320:384]
        output_out[:, 320 * j : 320 * j + 320] = total[:, 384:]
    gain = jnp.zeros((40, 1), F32)
    for weight, grad in ((query_ref, query_out), (keyval_ref, keyval_out)):
        gain += jnp.sum(weight[...].astype(F32) * grad[...], axis=1, keepdims=True)
    gain_out[...] = jnp.broadcast_to(gain, (40, 128))


def owned(blocks, w_query, keyval_half, *first):
    whole = pl.BlockSpec(memory_space=pltpu.VMEM)
    return pl.pallas_call(
        owned_kernel,
        in_specs=[whole] * 6 + [ANYWHERE] * len(first),
        out_shape=(
            jax.ShapeDtypeStruct((40, 1280), F32),
            jax.ShapeDtypeStruct((40, 256), F32),
            jax.ShapeDtypeStruct((40, 1280), F32),
            jax.ShapeDtypeStruct((40, 128), F32),
        ),
        scratch_shapes=[pltpu.VMEM((4, 40, 704), BF)],
        compiler_params=VMEM,
    )(*blocks, w_query, keyval_half, *first)


def owned_mlp_kernel(b0, b1, b2, b3, gate_ref, up_ref, gate_out, up_out, down_out, gain_out, held):
    me = lax.axis_index(Y)
    for r, block in enumerate((b0, b1, b2, b3)):
        held[lax.rem(me + 4 - r, 4)] = block[...]
    for j in range(4):
        columns = slice(960 * j, 960 * j + 960)
        gate_out[:, columns] = held[j, :, :960].astype(F32)
        up_out[:, columns] = held[j, :, 1024:1984].astype(F32)
        down_out[:, columns] = held[j, :, 2048:3008].astype(F32)
    products = gate_ref[...].astype(F32) * gate_out[...] + up_ref[...].astype(F32) * up_out[...]
    gain_out[...] = jnp.broadcast_to(jnp.sum(products, axis=1, keepdims=True), (40, 128))


def owned_mlp(blocks, w_gate, w_up):
    wide = jax.ShapeDtypeStruct((40, 3840), F32)
    return pl.pallas_call(
        owned_mlp_kernel,
        out_shape=(wide, wide, wide, jax.ShapeDtypeStruct((40, 128), F32)),
        scratch_shapes=[pltpu.VMEM((4, 40, 3072), BF)],
        compiler_params=VMEM,
    )(*blocks, w_gate, w_up)


def token_order_kernel(x_ref, out_ref):
    for j in range(4):
        for p in range(16):
            to, at = 40 * (16 * j + p), 40 * (4 * p + j)
            out_ref[:, to : to + 40] = x_ref[:, at : at + 40].astype(BF)


def from_piece_order(x):
    return pl.pallas_call(
        token_order_kernel, out_shape=jax.ShapeDtypeStruct(x.shape, BF), compiler_params=VMEM
    )(x)


def halves_kernel(mine_ref, other_ref, out_ref):
    at = 80 * lax.axis_index(T)
    out_ref[pl.ds(pl.multiple_of(at, 16), 80), :] = mine_ref[...]
    out_ref[pl.ds(pl.multiple_of(80 - at, 16), 80), :] = other_ref[...]


def halves_home(mine):
    return pl.pallas_call(
        halves_kernel,
        out_shape=jax.ShapeDtypeStruct((160, mine.shape[1]), BF),
        compiler_params=VMEM,
    )(mine, shift(mine, T, 1))


def shards(
    tokens,
    lengths,
    attn_gain,
    w_query,
    w_keyval,
    w_output,
    mlp_gain,
    w_gate,
    w_up,
    w_down,
    cotangent,
):
    t = lax.axis_index(T)
    me = lax.axis_index(Y)
    piece = lax.axis_index(CONTEXT)
    head_dim = 256
    query_scale = head_dim ** (-0.5)
    seq_count = 2560
    padding = seq_count - lengths[0]
    row_start = piece * 160
    natural = row_start + jnp.arange(160, dtype=jnp.int32)
    turned = row_start + (jnp.arange(160, dtype=jnp.int32) + t * 80) % 160
    live_turned = turned >= padding
    live_mine = live_turned[:80, None]

    w_out = lax.all_gather(w_output, PIECES, axis=0, tiled=True)

    x_low = to_piece_order(lax.dynamic_slice_in_dim(tokens[0], t * 80, 80, 0))
    cot_mine = to_piece_order(lax.dynamic_slice_in_dim(cotangent[0], t * 80, 80, 0))
    grad_mine = jnp.where(live_mine, cot_mine, jnp.zeros_like(cot_mine))
    x_mine = x_low.astype(F32)
    keyval_half = lax.dynamic_slice_in_dim(w_keyval, t * 256, 256, 1)
    gains = jnp.concatenate([attn_gain, mlp_gain])[None, :]
    gains = jnp.pad(gains, ((0, 7), (0, 48)))
    attn_blocks = pack_attention(w_query, keyval_half, gains, small_trip(x_low))
    attn_copies = jnp.broadcast_to(attn_blocks[None], (16, 4, 48, 384)).reshape(64, 48, 384)
    attn_all = exchange(attn_copies, PIECES)
    w_qkv = attn_all[:, :40].reshape(2560, 384)
    gain_one = attn_all[:, 40, :40].reshape(1, 2560).astype(F32)
    gain_two = attn_all[:, 40, 40:80].reshape(1, 2560).astype(F32)
    x_own, x_other = gather_rows(x_low, attn_all)
    mlp_blocks = pack_mlp(w_gate, w_up, w_down)
    mlp_got = to_owners(mlp_blocks)
    mlp_block = place(mlp_got, Y, x_own, sign=-1).reshape(160, 3072)
    w_mlp = lax.all_gather(mlp_block, CONTEXT, axis=0, tiled=True)

    normed, projected = project(x_own, x_other, gain_one, w_qkv)
    grad_own, grad_other = gather_rows(after(grad_mine, projected))
    home = exchange(projected, Y)
    keyval_turned = joined(home[:, :, 320:])
    keyval_own = jnp.where(
        t == 0, keyval_turned, jnp.concatenate([keyval_turned[80:], keyval_turned[:80]])
    )
    cosine_nat, sine_nat = angles(natural - padding, head_dim)
    keys_own = rotate(keyval_own[:, None].astype(F32), cosine_nat, sine_nat)[:, 0].astype(BF)
    kv_own = jnp.where(t == 0, keys_own, keyval_own)
    kv_mine = exchange(jnp.broadcast_to(kv_own[None], (16, 160, 256)), CONTEXT).reshape(2560, 256)
    grad_group = jnp.concatenate([grad_own, grad_other])
    kv_other = shift(kv_mine, T, 1)
    keys = jnp.where(t == 0, kv_mine, kv_other)
    values = jnp.where(t == 0, kv_other, kv_mine)
    query_pre = joined(home[:, :, :320]).reshape(160, 5, head_dim).astype(F32)
    cosine, sine_part = angles(turned - padding, head_dim)
    queries = (rotate(query_pre, cosine, sine_part) * query_scale).astype(BF)

    key_index = jnp.arange(seq_count, dtype=jnp.int32)
    offset = turned[:, None] - key_index[None, :]
    allowed = ((offset >= 0) & (offset < WINDOW) & (key_index >= padding)[None, :])[None]
    live = live_turned[None, :, None]
    scores = jnp.einsum("qhd,kd->hqk", queries, keys, preferred_element_type=F32)
    row_top = jnp.max(jnp.where(allowed, scores, NEGATIVE_FILL), axis=-1, keepdims=True)
    row_top = jnp.where(live, row_top, 0.0)
    weights_exp = jnp.where(allowed, jnp.exp(scores - row_top), 0.0)
    row_total = jnp.where(live, jnp.sum(weights_exp, axis=-1, keepdims=True), 1.0)
    prob = weights_exp / row_total
    prob_low = prob.astype(BF)
    attended = jnp.einsum("hqk,kd->qhd", prob_low, values, preferred_element_type=F32)
    attended = attended.reshape(160, 1280).astype(BF)

    branch = dot(attended, w_out, 1, 1)
    hidden_mine = x_mine + branch[:80] + shift(branch[80:], T, 1)

    inverse_two = inverse_root(hidden_mine)
    normed_two_mine = (hidden_mine * inverse_two * gain_two).astype(BF)
    normed_two = jnp.concatenate(gather_rows(after(normed_two_mine, grad_group)))
    hidden, grad_gate, grad_up = feed_forward(normed_two, grad_group, w_mlp)
    normed_two_low = scatter_parts((grad_gate, grad_up), w_mlp, 0, 1024)

    normed_two_blocks = scatter_blocks(normed_two_low)
    got = [shift(normed_two_blocks[r], Y, r) for r in (1, 3, 2)]
    trip = small_trip(normed_two_low, *normed_two_blocks[1:])
    mlp_low = scatter_parts((hidden,), w_mlp, 2, 1024, trip)
    attended_group = columns_out(attended)
    mlp_part = mlp_grads(
        normed_two, grad_group, grad_gate, grad_up, hidden, *got[:2], mlp_low, attended_group
    )
    mlp_sum = lax.psum_scatter(mlp_part, CONTEXT, scatter_dimension=0, tiled=True)
    grad_normed_two = scatter_total(after(normed_two_blocks[0], mlp_part), got)

    grad_h_mine = grad_mine.astype(F32) + norm_back(
        grad_normed_two, hidden_mine, inverse_two, gain_two
    )
    branch_mine = grad_h_mine.astype(BF)
    branch_low = jnp.concatenate([branch_mine, shift(branch_mine, T, 1)])
    grad_attended = dot(branch_low, w_out, 1, 0).astype(BF).reshape(160, 5, head_dim)
    branch_own, branch_other = gather_rows(branch_mine)
    branch_group = jnp.concatenate([branch_own, branch_other])

    grad_prob = jnp.einsum("qhd,kd->hqk", grad_attended, values, preferred_element_type=F32)
    spread = jnp.sum(prob * grad_prob, axis=-1, keepdims=True)
    grad_scores = (prob * (grad_prob - spread)).astype(BF)
    grad_keys = jnp.einsum("hqk,qhd->kd", grad_scores, queries, preferred_element_type=F32)
    grad_values = jnp.einsum("hqk,qhd->kd", prob_low, grad_attended, preferred_element_type=F32)
    keep = jnp.where(t == 0, grad_keys, grad_values)
    give = jnp.where(t == 0, grad_values, grad_keys).astype(BF)
    grad_queries = jnp.einsum("hqk,kd->qhd", grad_scores, keys, preferred_element_type=F32)
    grad_query_pre = (
        rotate(grad_queries * query_scale, cosine, -sine_part).reshape(160, 1280).astype(BF)
    )
    kv_part = (keep + shift(give, T, 1).astype(F32)).astype(BF).reshape(16, 160, 256)
    kv_part = after(kv_part, grad_query_pre)
    kv_home = after(exchange(kv_part, CONTEXT), branch_group)
    kv_sum = jnp.sum(kv_home.astype(F32), axis=0)
    grad_query_group = columns_out(grad_query_pre)

    keys_back = rotate(kv_sum[:, None], cosine_nat, -sine_nat)[:, 0]
    kv_back = jnp.where(t == 0, keys_back, kv_sum).astype(BF)
    kv_back = jnp.where(t == 0, kv_back, jnp.concatenate([kv_back[80:], kv_back[:80]]))
    grad_kv_group = columns_out(kv_back)
    grad_qkv = jnp.concatenate([grad_query_group, grad_kv_group], axis=1)
    normed_low = scatter_parts((grad_qkv,), w_qkv, 0, 384)
    normed_blocks = scatter_blocks(normed_low)
    part = outer(normed, grad_qkv, branch_group, attended_group)
    home = to_owners(scatter_context(part))

    mlp_mine = scatter_sum(scatter_blocks(after(mlp_low, *normed_blocks[1:])))
    block_mine = jnp.where(live_mine, hidden_mine + mlp_mine, 0.0)

    grad_normed = scatter_sum(normed_blocks)
    inverse_one = inverse_root(x_mine)
    tokens_mine = grad_h_mine + norm_back(grad_normed, x_mine, inverse_one, gain_one)
    gate_grad, up_grad, down_grad, two_part = owned_mlp(to_owners(mlp_sum), w_gate, w_up)
    block_out = halves_home(from_piece_order(block_mine))
    tokens_grad = halves_home(from_piece_order(tokens_mine))

    query_grad, kv_half, output_grad, one_part = owned(
        home, w_query, keyval_half, two_part, block_out, tokens_grad
    )
    mine = jnp.concatenate([kv_half, one_part, two_part], axis=1)
    other = shift(mine, T, 1)
    kv_other = other[:, :256]
    keyval_grad = jnp.where(
        t == 0,
        jnp.concatenate([kv_half, kv_other], axis=1),
        jnp.concatenate([kv_other, kv_half], axis=1),
    )
    attn_gain_grad = (mine[:, 256] + other[:, 256]) / attn_gain.astype(F32)
    mlp_gain_grad = (mine[:, 384] + other[:, 384]) / mlp_gain.astype(F32)

    return (
        block_out[None],
        tokens_grad[None],
        attn_gain_grad,
        query_grad,
        keyval_grad,
        output_grad,
        mlp_gain_grad,
        gate_grad,
        up_grad,
        down_grad,
    )


def solution(mesh):
    torus = Mesh(
        mesh.devices.reshape(mesh.shape["shard"], 4, 4, mesh.shape["tensor"]),
        ("shard", "context_0", "context_1", "tensor"),
    )
    in_specs = (
        P("shard", CONTEXT, None),
        P("shard"),
        P(SHARD_CONTEXT),
        P(SHARD_CONTEXT, "tensor"),
        P(SHARD_CONTEXT, None),
        P(SHARD_CONTEXT, "tensor"),
        P(SHARD_CONTEXT),
        P(SHARD_CONTEXT, "tensor"),
        P(SHARD_CONTEXT, "tensor"),
        P(SHARD_CONTEXT, "tensor"),
        P("shard", CONTEXT, None),
    )
    out_specs = (
        P("shard", CONTEXT, None),
        P("shard", CONTEXT, None),
        P(SHARD_CONTEXT),
        P(SHARD_CONTEXT, "tensor"),
        P(SHARD_CONTEXT, None),
        P(SHARD_CONTEXT, "tensor"),
        P(SHARD_CONTEXT),
        P(SHARD_CONTEXT, "tensor"),
        P(SHARD_CONTEXT, "tensor"),
        P(SHARD_CONTEXT, "tensor"),
    )
    return jax.shard_map(
        shards, mesh=torus, in_specs=in_specs, out_specs=out_specs, check_vma=False
    )
```

time: 648 us -> 601 us (0.927)
  the two profiles are of different devices: /device:TPU:1 before, /device:TPU:35 now
where the time goes in v4:
time: 601 us; the launch traced here: 591 us
  waiting for transfers between devices  243 us (40%)
  starting transfers between devices  122 us (20%)
  Pallas kernels  91.7 us (15%)
  local copies, waits for them, and re-layouts  50.8 us (8%)
  other arithmetic  36.9 us (6%)
  matrix products  29.3 us (5%)
  between operations  16.2 us (3%)
    ppermute x67, waiting for transfers between devices, shift(): return lax.ppermute(x, axis, [(i, (i + by) % n) for i in range(n)])  196 us
    ppermute x67, starting transfers between devices, shift(): return lax.ppermute(x, axis, [(i, (i + by) % n) for i in range(n)])  95.1 us
    all_to_all x4, waiting for transfers between devices, exchange(): return lax.all_to_all(blocks, axis, 0, 0, tiled=True)  41.8 us
    pallas_call x3, Pallas kernels, row_products(): pl.pallas_call(functools.partial(rows_kernel, count), grid=(n // rows,),...  27.6 us
    all_to_all x4, starting transfers between devices, exchange(): return lax.all_to_all(blocks, axis, 0, 0, tiled=True)  27.2 us
    pallas_call x1, Pallas kernels, mlp_grads(): pl.pallas_call(mlp_grad_kernel, grid=(3, 2560 // rows), out_shape=jax.Sha...  20.8 us
    unnamed x165, local copies, waits for them, and re-layouts  17.5 us
    pallas_call x1, Pallas kernels, feed_forward(): pl.pallas_call(feed_forward_kernel, grid=(steps,), out_shape=(part, part,...  16 us
  transfers between devices with their start and end apart: 74, of which 43 were waited for; matrix products, arithmetic and copies ran while one was open for 17% of the time, Pallas kernels for 5%

profile of v4, /device:TPU:35, one launch (start us, length us, event | category | flops | bytes accessed | tf_op | source)
XLA Modules:
  0.0 590.6 jit_solution(11204077960059187287)
XLA Ops:
  14.5 10.6 %all-to-all-start = ((bf16[64,48,384]{2,1,0:T(8,128)(2,1)}), bf16[64,48,384]{2,1,0:T(8,128)(2,1)S(1)}, u32[]{:S(2)}, u32[]{:S(2)}) async-start(bf16[64,48,384]{2,1,0:T(8,128)(2,1)} %bitcast.292), calls=%async_computation | async-start | bytes 4718592 | tf_op jit(solution)/shard_map/all_to_all | solution.py:31
  34.2 28.9 %collective-permute-done.2.refs_3_ = bf16[80,2560]{1,0:T(8,128)(2,1)} collective-permute-done((bf16[80,2560]{1,0:T(8,128)(2,1)S(1)}, bf16[80,2560]{1,0:T(8,128)(2,1)}, u32[]{:S(2)}, u32[]{:S(2)}) %collective-permute-start.2) | collective-permute-done | bytes 409632 | tf_op jit(solution)/shard_map/ppermute | solution.py:27
  63.1 9.3 %collective-permute-done.1.refs_2_ = bf16[80,2560]{1,0:T(8,128)(2,1)} collective-permute-done((bf16[80,2560]{1,0:T(8,128)(2,1)S(1)}, bf16[80,2560]{1,0:T(8,128)(2,1)}, u32[]{:S(2)}, u32[]{:S(2)}) %collective-permute-start.1) | collective-permute-done | bytes 409632 | tf_op jit(solution)/shard_map/ppermute | solution.py:27
  79.5 8.3 %collective-permute-done.15.refs_1_ = bf16[40,3072]{1,0:T(8,128)(2,1)} collective-permute-done((bf16[40,3072]{1,0:T(8,128)(2,1)}, bf16[40,3072]{1,0:T(8,128)(2,1)}, u32[]{:S(2)}, u32[]{:S(2)}) %collective-permute-start.15) | collective-permute-done | bytes 245792 | tf_op jit(solution)/shard_map/ppermute | solution.py:27
  95.1 8.1 %shard_map.188 = (bf16[640,2560]{1,0:T(8,128)(2,1)}, bf16[4,160,384]{2,1,0:T(8,128)(2,1)}) custom-call(bf16[320,2560]{1,0:T(8,128)(2,1)S(1)} %bitcast.270, bf16[320,2560]{1,0:T(8,128)(2,1)} %collective-permute-done.4.other_ref, f32[1,2560]{1,0:T(1,128)S(1)} %reshape.635.gain_ref, bf16[2560,384]{1,0:T(8,128)(2,1)S(1)} %bitcast.266), custom_call_target="tpu_custom_call" | custom-call | tf_op jit(solution)/shard_map/pallas_call | solution.py:360
  108.2 13.2 %all-to-all-done.1 = bf16[4,160,384]{2,1,0:T(8,128)(2,1)S(1)} async-done(((bf16[4,160,384]{2,1,0:T(8,128)(2,1)}), bf16[4,160,384]{2,1,0:T(8,128)(2,1)S(1)}, u32[]{:S(2)}, u32[]{:S(2)}) %all-to-all-start.1) | async-done | bytes 491552 | tf_op jit(solution)/shard_map/all_to_all | solution.py:31
  124.2 6.6 %all-to-all-start.2 = ((bf16[16,160,256]{2,1,0:T(8,128)(2,1)}), bf16[16,160,256]{2,1,0:T(8,128)(2,1)}, u32[]{:S(2)}, u32[]{:S(2)}) async-start(bf16[16,160,256]{2,1,0:T(8,128)(2,1)} %broadcast_in_dim.110), calls=%async_computation.2 | async-start | bytes 2621440 | tf_op jit(solution)/shard_map/all_to_all | solution.py:31
  132.1 18.6 %all-to-all-done.2 = bf16[16,160,256]{2,1,0:T(8,128)(2,1)} async-done(((bf16[16,160,256]{2,1,0:T(8,128)(2,1)}), bf16[16,160,256]{2,1,0:T(8,128)(2,1)}, u32[]{:S(2)}, u32[]{:S(2)}) %all-to-all-start.2) | async-done | bytes 1310752 | tf_op jit(solution)/shard_map/all_to_all | solution.py:31
  150.7 6.8 %collective-permute-start.5 = (bf16[2560,256]{1,0:T(8,128)(2,1)}, bf16[2560,256]{1,0:T(8,128)(2,1)}, u32[]{:S(2)}, u32[]{:S(2)}) collective-permute-start(bf16[2560,256]{1,0:T(8,128)(2,1)} %bitcast.16), channel_id=1, source_target_pairs={{0,1},{1,0},{2,3},{3,2},{4,5},{5,4},{6,7},{7,6},{8,9},{9,8},{10,11... | collective-permute-start | bytes 3932168 | tf_op jit(solution)/shard_map/ppermute | solution.py:27
  169.2 10.6 %collective-permute-done.9.refs_3_ = bf16[80,2560]{1,0:T(8,128)(2,1)S(1)} collective-permute-done((bf16[80,2560]{1,0:T(8,128)(2,1)S(1)}, bf16[80,2560]{1,0:T(8,128)(2,1)S(1)}, u32[]{:S(2)}, u32[]{:S(2)}) %collective-permute-start.9) | collective-permute-done | bytes 409632 | tf_op jit(solution)/shard_map/ppermute | solution.py:27
  193.2 5.2 fusion.103
  207.8 8.3 %collective-permute-done.13.refs_3_ = bf16[80,2560]{1,0:T(8,128)(2,1)S(1)} collective-permute-done((bf16[80,2560]{1,0:T(8,128)(2,1)S(1)}, bf16[80,2560]{1,0:T(8,128)(2,1)S(1)}, u32[]{:S(2)}, u32[]{:S(2)}) %collective-permute-start.13) | collective-permute-done | bytes 409632 | tf_op jit(solution)/shard_map/ppermute | solution.py:27
  216.2 9.6 %collective-permute-done.12.refs_2_ = bf16[80,2560]{1,0:T(8,128)(2,1)S(1)} collective-permute-done((bf16[80,2560]{1,0:T(8,128)(2,1)S(1)}, bf16[80,2560]{1,0:T(8,128)(2,1)S(1)}, u32[]{:S(2)}, u32[]{:S(2)}) %collective-permute-start.12) | collective-permute-done | bytes 409632 | tf_op jit(solution)/shard_map/ppermute | solution.py:27
  237.3 16.0 %shard_map.195 = (bf16[640,1024]{1,0:T(8,128)(2,1)S(1)}, bf16[640,1024]{1,0:T(8,128)(2,1)S(1)}, bf16[640,1024]{1,0:T(8,128)(2,1)S(1)}) custom-call(bf16[640,2560]{1,0:T(8,128)(2,1)} %pad_maximum_fusion.1.x_ref, bf16[640,2560]{1,0:T(8,128)(2,1)} %copy-done.2, bf16[2560,3072]{1,0:T(8,128)(2,1)} %all-gather.5.cloned.1.call-done.gate_ref.up_ref.down_ref.refs_2_.refs_3_.refs_1_, ...), custom_call_target="tpu_custom_call" | custom-call | tf_op jit(solution)/shard_map/pallas_call | solution.py:287
  253.3 12.2 %shard_map.196 = (bf16[320,2560]{1,0:T(8,128)(2,1)S(1)}, bf16[320,2560]{1,0:T(8,128)(2,1)S(1)}) custom-call(bf16[640,1024]{1,0:T(8,128)(2,1)S(1)} %get-tuple-element.31.refs_0_.gate_ref, bf16[640,1024]{1,0:T(8,128)(2,1)S(1)} %get-tuple-element.32.refs_1_.up_ref, ...), custom_call_target="tpu_custom_call" | custom-call | tf_op jit(solution)/shard_map/pallas_call | solution.py:93
  271.3 9.7 %shard_map.198 = (bf16[320,2560]{1,0:T(8,128)(2,1)}, bf16[320,2560]{1,0:T(8,128)(2,1)S(1)}) custom-call(bf16[640,1024]{1,0:T(8,128)(2,1)S(1)} %get-tuple-element.30.refs_0_.hidden_ref, bf16[2560,3072]{1,0:T(8,128)(2,1)} %all-gather.5.cloned.1.call-done.gate_ref.up_ref.down_ref.refs_2_.refs_3_.refs_1_, bf16[8,128]{1,0:T(8,128)(2,1)S(1)} %collective-permute-done.19.refs_2_), custom_call_target="tpu_custom_call" | custom-call | tf_op jit(solution)/shard_map/pallas_call | solution.py:93
  304.1 4.9 collective-permute-done.22.rest_1_
  311.9 20.8 %shard_map.200.refs_1_ = bf16[2560,3072]{1,0:T(8,128)(2,1)} custom-call(bf16[640,2560]{1,0:T(8,128)(2,1)} %pad_maximum_fusion.1.x_ref, bf16[640,2560]{1,0:T(8,128)(2,1)} %copy-done.2, bf16[640,1024]{1,0:T(8,128)(2,1)S(1)} %get-tuple-element.31.refs_0_.gate_ref, bf16[640,1024]{1,0:T(8,128)(2,1)S(1)} %copy-done.14, ...), custom_call_target="tpu_custom_call" | custom-call | tf_op jit(solution)/shard_map/pallas_call | solution.py:249
  334.6 10.2 %collective-permute-done.26 = bf16[80,2560]{1,0:T(8,128)(2,1)S(1)} collective-permute-done((bf16[80,2560]{1,0:T(8,128)(2,1)S(1)}, bf16[80,2560]{1,0:T(8,128)(2,1)S(1)}, u32[]{:S(2)}, u32[]{:S(2)}) %collective-permute-start.26) | collective-permute-done | bytes 409632 | tf_op jit(solution)/shard_map/ppermute | solution.py:27
  372.2 17.9 %collective-permute-done.34.refs_3_ = bf16[80,2560]{1,0:T(8,128)(2,1)S(1)} collective-permute-done((bf16[80,2560]{1,0:T(8,128)(2,1)S(1)}, bf16[80,2560]{1,0:T(8,128)(2,1)S(1)}, u32[]{:S(2)}, u32[]{:S(2)}) %collective-permute-start.34) | collective-permute-done | bytes 409632 | tf_op jit(solution)/shard_map/ppermute | solution.py:27
  396.8 6.5 %all-to-all-start.3 = ((bf16[16,160,256]{2,1,0:T(8,128)(2,1)}), bf16[16,160,256]{2,1,0:T(8,128)(2,1)}, u32[]{:S(2)}, u32[]{:S(2)}) async-start(bf16[16,160,256]{2,1,0:T(8,128)(2,1)} %shard_map.203), calls=%async_computation.3 | async-start | bytes 2621440 | tf_op jit(solution)/shard_map/all_to_all | solution.py:31
  413.9 10.0 %all-to-all-done.3.refs_0_ = bf16[16,160,256]{2,1,0:T(8,128)(2,1)} async-done(((bf16[16,160,256]{2,1,0:T(8,128)(2,1)}), bf16[16,160,256]{2,1,0:T(8,128)(2,1)}, u32[]{:S(2)}, u32[]{:S(2)}) %all-to-all-start.3) | async-done | bytes 1310752 | tf_op jit(solution)/shard_map/all_to_all | solution.py:31
  438.6 5.7 shard_map.207
  444.3 8.2 %shard_map.213 = bf16[2560,704]{1,0:T(8,128)(2,1)} custom-call(bf16[640,2560]{1,0:T(8,128)(2,1)S(1)} %copy-done.20, bf16[640,384]{1,0:T(8,128)(2,1)S(1)} %pad_maximum_fusion.3.refs_0_.g_ref, bf16[640,2560]{1,0:T(8,128)(2,1)} %copy-done.3, bf16[640,320]{1,0:T(8,128)(2,1)S(1)} %bitcast.278), custom_call_target="tpu_custom_call" | custom-call | tf_op jit(solution)/shard_map/pallas_call | solution.py:136
  465.2 7.9 %collective-permute-done.48 = bf16[4,80,704]{2,1,0:T(8,128)(2,1)S(1)} collective-permute-done((bf16[4,80,704]{2,1,0:T(8,128)(2,1)}, bf16[4,80,704]{2,1,0:T(8,128)(2,1)S(1)}, u32[]{:S(2)}, u32[]{:S(2)}) %collective-permute-start.48) | collective-permute-done | bytes 450592 | tf_op jit(solution)/shard_map/ppermute | solution.py:27
  473.1 10.6 %collective-permute-start.56 = (bf16[4,80,704]{2,1,0:T(8,128)(2,1)}, bf16[4,80,704]{2,1,0:T(8,128)(2,1)}, u32[]{:S(2)}, u32[]{:S(2)}) collective-permute-start(bf16[4,80,704]{2,1,0:T(8,128)(2,1)} %get-tuple-element.66), channel_id=1, source_target_pairs={{0,4},{2,6},{4,0},{6,2},{1,5},{3,7},{5,1},{7,3},{8,12},{10,14},{12... | collective-permute-start | bytes 1351688 | tf_op jit(solution)/shard_map/ppermute | solution.py:27
  494.7 12.5 %collective-permute-done.55 = bf16[4,80,704]{2,1,0:T(8,128)(2,1)} collective-permute-done((bf16[4,80,704]{2,1,0:T(8,128)(2,1)}, bf16[4,80,704]{2,1,0:T(8,128)(2,1)}, u32[]{:S(2)}, u32[]{:S(2)}) %collective-permute-start.55) | collective-permute-done | bytes 450592 | tf_op jit(solution)/shard_map/ppermute | solution.py:27
  518.8 6.1 %collective-permute-done.45 = bf16[80,2560]{1,0:T(8,128)(2,1)S(1)} collective-permute-done((bf16[80,2560]{1,0:T(8,128)(2,1)S(1)}, bf16[80,2560]{1,0:T(8,128)(2,1)S(1)}, u32[]{:S(2)}, u32[]{:S(2)}) %collective-permute-start.45) | collective-permute-done | bytes 409632 | tf_op jit(solution)/shard_map/ppermute | solution.py:27
  530.0 9.1 %collective-permute-done.44 = bf16[80,2560]{1,0:T(8,128)(2,1)S(1)} collective-permute-done((bf16[80,2560]{1,0:T(8,128)(2,1)S(1)}, bf16[80,2560]{1,0:T(8,128)(2,1)S(1)}, u32[]{:S(2)}, u32[]{:S(2)}) %collective-permute-start.44) | collective-permute-done | bytes 409632 | tf_op jit(solution)/shard_map/ppermute | solution.py:27
  543.5 5.4 collective-permute-done.42
  548.9 8.7 %collective-permute-start.47 = (bf16[80,2560]{1,0:T(8,128)(2,1)S(1)}, bf16[80,2560]{1,0:T(8,128)(2,1)S(1)}, u32[]{:S(2)}, u32[]{:S(2)}) collective-permute-start(bf16[80,2560]{1,0:T(8,128)(2,1)S(1)} %shard_map.211.mine_ref), channel_id=1, source_target_pairs={{0,1},{1,0},{2,3},{3,2},{4,5},{5,4},{6,7},{7,6},{8,9},{9,8},{10,11... | collective-permute-start | bytes 1228808 | tf_op jit(solution)/shard_map/ppermute | solution.py:27
  570.1 6.4 %collective-permute-done.63.b1 = bf16[40,3072]{1,0:T(8,128)(2,1)S(1)} collective-permute-done((bf16[40,3072]{1,0:T(8,128)(2,1)S(1)}, bf16[40,3072]{1,0:T(8,128)(2,1)S(1)}, u32[]{:S(2)}, u32[]{:S(2)}) %collective-permute-start.63) | collective-permute-done | bytes 245792 | tf_op jit(solution)/shard_map/ppermute | solution.py:27
  (448 shorter events, 241.3 us)
Async XLA Ops:
  7.2 186.0 %all-gather.3.cloned.1.call-start = ((), (), s32[]{:S(2)}) async-start(), calls=%async_computation.5 | async-start | bytes 6656000 | tf_op jit(solution)/shard_map/all_gather | solution.py:489
  14.5 58.0 %all-to-all-start = ((bf16[64,48,384]{2,1,0:T(8,128)(2,1)}), bf16[64,48,384]{2,1,0:T(8,128)(2,1)S(1)}, u32[]{:S(2)}, u32[]{:S(2)}) async-start(bf16[64,48,384]{2,1,0:T(8,128)(2,1)} %bitcast.292), calls=%async_computation | async-start | bytes 4718592 | tf_op jit(solution)/shard_map/all_to_all | solution.py:31
  25.1 212.2 %all-gather.5.cloned.1.call-start = ((), (), s32[]{:S(2)}) async-start(), calls=%async_computation.6 | async-start | bytes 16711680 | tf_op jit(solution)/shard_map/all_gather | solution.py:508
  25.2 37.9 %collective-permute-start.2 = (bf16[80,2560]{1,0:T(8,128)(2,1)S(1)}, bf16[80,2560]{1,0:T(8,128)(2,1)}, u32[]{:S(2)}, u32[]{:S(2)}) collective-permute-start(bf16[80,2560]{1,0:T(8,128)(2,1)S(1)} %copy.106.refs_0_), channel_id=1, source_target_pairs={{0,32},{32,64},{64,96},{96,0},{1,33},{33,65},{65,97},{97,1},{2,34}... | collective-permute-start | bytes 1228808 | tf_op jit(solution)/shard_map/ppermute | solution.py:27
  26.4 46.0 %collective-permute-start.1 = (bf16[80,2560]{1,0:T(8,128)(2,1)S(1)}, bf16[80,2560]{1,0:T(8,128)(2,1)}, u32[]{:S(2)}, u32[]{:S(2)}) collective-permute-start(bf16[80,2560]{1,0:T(8,128)(2,1)S(1)} %copy.106.refs_0_), channel_id=1, source_target_pairs={{0,64},{32,96},{64,0},{96,32},{1,65},{33,97},{65,1},{97,33},{2,66}... | collective-permute-start | bytes 1228808 | tf_op jit(solution)/shard_map/ppermute | solution.py:27
  28.8 43.6 %collective-permute-start = (bf16[80,2560]{1,0:T(8,128)(2,1)S(1)}, bf16[80,2560]{1,0:T(8,128)(2,1)}, u32[]{:S(2)}, u32[]{:S(2)}) collective-permute-start(bf16[80,2560]{1,0:T(8,128)(2,1)S(1)} %copy.106.refs_0_), channel_id=1, source_target_pairs={{0,96},{32,0},{64,32},{96,64},{1,97},{33,1},{65,33},{97,65},{2,98}... | collective-permute-start | bytes 1228808 | tf_op jit(solution)/shard_map/ppermute | solution.py:27
  32.1 45.4 %collective-permute-start.17 = (bf16[40,3072]{1,0:T(8,128)(2,1)}, bf16[40,3072]{1,0:T(8,128)(2,1)S(1)}, u32[]{:S(2)}, u32[]{:S(2)}) collective-permute-start(bf16[40,3072]{1,0:T(8,128)(2,1)} %get-tuple-element.88), channel_id=1, source_target_pairs={{0,96},{32,0},{64,32},{96,64},{1,97},{33,1},{65,33},{97,65},{2,98}... | collective-permute-start | bytes 737288 | tf_op jit(solution)/shard_map/ppermute | solution.py:27
  32.1 47.4 %collective-permute-start.16 = (bf16[40,3072]{1,0:T(8,128)(2,1)}, bf16[40,3072]{1,0:T(8,128)(2,1)S(1)}, u32[]{:S(2)}, u32[]{:S(2)}) collective-permute-start(bf16[40,3072]{1,0:T(8,128)(2,1)} %get-tuple-element.89), channel_id=1, source_target_pairs={{0,64},{32,96},{64,0},{96,32},{1,65},{33,97},{65,1},{97,33},{2,66}... | collective-permute-start | bytes 737288 | tf_op jit(solution)/shard_map/ppermute | solution.py:27
  63.1 24.7 %collective-permute-start.15 = (bf16[40,3072]{1,0:T(8,128)(2,1)}, bf16[40,3072]{1,0:T(8,128)(2,1)}, u32[]{:S(2)}, u32[]{:S(2)}) collective-permute-start(bf16[40,3072]{1,0:T(8,128)(2,1)} %get-tuple-element.90), channel_id=1, source_target_pairs={{0,32},{32,64},{64,96},{96,0},{1,33},{33,65},{65,97},{97,1},{2,34}... | collective-permute-start | bytes 737288 | tf_op jit(solution)/shard_map/ppermute | solution.py:27
  124.2 26.4 %all-to-all-start.2 = ((bf16[16,160,256]{2,1,0:T(8,128)(2,1)}), bf16[16,160,256]{2,1,0:T(8,128)(2,1)}, u32[]{:S(2)}, u32[]{:S(2)}) async-start(bf16[16,160,256]{2,1,0:T(8,128)(2,1)} %broadcast_in_dim.110), calls=%async_computation.2 | async-start | bytes 2621440 | tf_op jit(solution)/shard_map/all_to_all | solution.py:31
  130.9 427.9 %reduce-scatter.2.cloned.1.call-start = ((), (), s32[]{:S(2)}) async-start(), calls=%async_computation.7 | async-start | bytes 16711680 | tf_op jit(solution)/shard_map/reduce_scatter | solution.py:560
  150.7 32.5 %collective-permute-start.5 = (bf16[2560,256]{1,0:T(8,128)(2,1)}, bf16[2560,256]{1,0:T(8,128)(2,1)}, u32[]{:S(2)}, u32[]{:S(2)}) collective-permute-start(bf16[2560,256]{1,0:T(8,128)(2,1)} %bitcast.16), channel_id=1, source_target_pairs={{0,1},{1,0},{2,3},{3,2},{4,5},{5,4},{6,7},{7,6},{8,9},{9,8},{10,11... | collective-permute-start | bytes 3932168 | tf_op jit(solution)/shard_map/ppermute | solution.py:27
  204.5 21.2 %collective-permute-start.12 = (bf16[80,2560]{1,0:T(8,128)(2,1)S(1)}, bf16[80,2560]{1,0:T(8,128)(2,1)S(1)}, u32[]{:S(2)}, u32[]{:S(2)}) collective-permute-start(bf16[80,2560]{1,0:T(8,128)(2,1)S(1)} %shard_map.191.refs_0_), channel_id=1, source_target_pairs={{0,64},{32,96},{64,0},{96,32},{1,65},{33,97},{65,1},{97,33},{2,66}... | collective-permute-start | bytes 1228808 | tf_op jit(solution)/shard_map/ppermute | solution.py:27
  368.7 26.4 %collective-permute-start.31 = (bf16[2560,256]{1,0:T(8,128)(2,1)}, bf16[2560,256]{1,0:T(8,128)(2,1)S(1)}, u32[]{:S(2)}, u32[]{:S(2)}) collective-permute-start(bf16[2560,256]{1,0:T(8,128)(2,1)} %get-tuple-element.133), channel_id=1, source_target_pairs={{0,1},{1,0},{2,3},{3,2},{4,5},{5,4},{6,7},{7,6},{8,9},{9,8},{10,11... | collective-permute-start | bytes 3932168 | tf_op jit(solution)/shard_map/ppermute | solution.py:27
  390.6 21.1 %collective-permute-start.35 = (bf16[320,2560]{1,0:T(8,128)(2,1)S(1)}, bf16[320,2560]{1,0:T(8,128)(2,1)}, u32[]{:S(2)}, u32[]{:S(2)}) collective-permute-start(bf16[320,2560]{1,0:T(8,128)(2,1)S(1)} %bitcast.271), channel_id=1, source_target_pairs={{0,1},{1,0},{2,3},{3,2},{4,5},{5,4},{6,7},{7,6},{8,9},{9,8},{10,11... | collective-permute-start | bytes 4915208 | tf_op jit(solution)/shard_map/ppermute | solution.py:27
  396.8 27.1 %all-to-all-start.3 = ((bf16[16,160,256]{2,1,0:T(8,128)(2,1)}), bf16[16,160,256]{2,1,0:T(8,128)(2,1)}, u32[]{:S(2)}, u32[]{:S(2)}) async-start(bf16[16,160,256]{2,1,0:T(8,128)(2,1)} %shard_map.203), calls=%async_computation.3 | async-start | bytes 2621440 | tf_op jit(solution)/shard_map/all_to_all | solution.py:31
  408.1 27.1 %collective-permute-start.28 = (bf16[160,320]{1,0:T(8,128)(2,1)}, bf16[160,320]{1,0:T(8,128)(2,1)S(1)}, u32[]{:S(2)}, u32[]{:S(2)}) collective-permute-start(bf16[160,320]{1,0:T(8,128)(2,1)} %bitcast.257), channel_id=1, source_target_pairs={{0,32},{32,64},{64,96},{96,0},{1,33},{33,65},{65,97},{97,1},{2,34}... | collective-permute-start | bytes 307208 | tf_op jit(solution)/shard_map/ppermute | solution.py:27
  408.2 27.5 %collective-permute-start.29 = (bf16[160,320]{1,0:T(8,128)(2,1)}, bf16[160,320]{1,0:T(8,128)(2,1)}, u32[]{:S(2)}, u32[]{:S(2)}) collective-permute-start(bf16[160,320]{1,0:T(8,128)(2,1)} %bitcast.256), channel_id=1, source_target_pairs={{0,64},{32,96},{64,0},{96,32},{1,65},{33,97},{65,1},{97,33},{2,66}... | collective-permute-start | bytes 307208 | tf_op jit(solution)/shard_map/ppermute | solution.py:27
  411.7 24.0 %collective-permute-start.30 = (bf16[160,320]{1,0:T(8,128)(2,1)}, bf16[160,320]{1,0:T(8,128)(2,1)}, u32[]{:S(2)}, u32[]{:S(2)}) collective-permute-start(bf16[160,320]{1,0:T(8,128)(2,1)} %bitcast.255), channel_id=1, source_target_pairs={{0,96},{32,0},{64,32},{96,64},{1,97},{33,1},{65,33},{97,65},{2,98}... | collective-permute-start | bytes 307208 | tf_op jit(solution)/shard_map/ppermute | solution.py:27
  452.5 58.4 %collective-permute-start.39 = (bf16[320,2560]{1,0:T(8,128)(2,1)}, bf16[320,2560]{1,0:T(8,128)(2,1)}, u32[]{:S(2)}, u32[]{:S(2)}) collective-permute-start(bf16[320,2560]{1,0:T(8,128)(2,1)} %get-tuple-element.38), channel_id=1, source_target_pairs={{0,1},{1,0},{2,3},{3,2},{4,5},{5,4},{6,7},{7,6},{8,9},{9,8},{10,11... | collective-permute-start | bytes 4915208 | tf_op jit(solution)/shard_map/ppermute | solution.py:27
  459.3 24.4 %collective-permute-start.50 = (bf16[4,80,704]{2,1,0:T(8,128)(2,1)}, bf16[4,80,704]{2,1,0:T(8,128)(2,1)S(1)}, u32[]{:S(2)}, u32[]{:S(2)}) collective-permute-start(bf16[4,80,704]{2,1,0:T(8,128)(2,1)} %get-tuple-element.63), channel_id=1, source_target_pairs={{0,16},{8,24},{16,0},{24,8},{1,17},{9,25},{17,1},{25,9},{2,18},{10... | collective-permute-start | bytes 1351688 | tf_op jit(solution)/shard_map/ppermute | solution.py:27
  463.3 22.2 %collective-permute-start.49 = (bf16[4,80,704]{2,1,0:T(8,128)(2,1)S(1)}, bf16[4,80,704]{2,1,0:T(8,128)(2,1)}, u32[]{:S(2)}, u32[]{:S(2)}) collective-permute-start(bf16[4,80,704]{2,1,0:T(8,128)(2,1)S(1)} %get-tuple-element.64), channel_id=1, source_target_pairs={{0,24},{8,0},{16,8},{24,16},{1,25},{9,1},{17,9},{25,17},{2,26},{10... | collective-permute-start | bytes 1351688 | tf_op jit(solution)/shard_map/ppermute | solution.py:27
  464.8 23.0 %collective-permute-start.54 = (bf16[4,80,704]{2,1,0:T(8,128)(2,1)}, bf16[4,80,704]{2,1,0:T(8,128)(2,1)}, u32[]{:S(2)}, u32[]{:S(2)}) collective-permute-start(bf16[4,80,704]{2,1,0:T(8,128)(2,1)} %get-tuple-element.65), channel_id=1, source_target_pairs={{0,2},{2,4},{4,6},{6,0},{1,3},{3,5},{5,7},{7,1},{8,10},{10,12},{12... | collective-permute-start | bytes 1351688 | tf_op jit(solution)/shard_map/ppermute | solution.py:27
  473.1 21.6 %collective-permute-start.56 = (bf16[4,80,704]{2,1,0:T(8,128)(2,1)}, bf16[4,80,704]{2,1,0:T(8,128)(2,1)}, u32[]{:S(2)}, u32[]{:S(2)}) collective-permute-start(bf16[4,80,704]{2,1,0:T(8,128)(2,1)} %get-tuple-element.66), channel_id=1, source_target_pairs={{0,4},{2,6},{4,0},{6,2},{1,5},{3,7},{5,1},{7,3},{8,12},{10,14},{12... | collective-permute-start | bytes 1351688 | tf_op jit(solution)/shard_map/ppermute | solution.py:27
  483.7 23.5 %collective-permute-start.55 = (bf16[4,80,704]{2,1,0:T(8,128)(2,1)}, bf16[4,80,704]{2,1,0:T(8,128)(2,1)}, u32[]{:S(2)}, u32[]{:S(2)}) collective-permute-start(bf16[4,80,704]{2,1,0:T(8,128)(2,1)} %get-tuple-element.67), channel_id=1, source_target_pairs={{0,6},{2,0},{4,2},{6,4},{1,7},{3,1},{5,3},{7,5},{8,14},{10,8},{12,... | collective-permute-start | bytes 1351688 | tf_op jit(solution)/shard_map/ppermute | solution.py:27
  487.0 28.4 %collective-permute-start.51 = (bf16[80,704]{1,0:T(8,128)(2,1)S(1)}, bf16[80,704]{1,0:T(8,128)(2,1)S(1)}, u32[]{:S(2)}, u32[]{:S(2)}) collective-permute-start(bf16[80,704]{1,0:T(8,128)(2,1)S(1)} %get-tuple-element.92), channel_id=1, source_target_pairs={{0,2},{2,4},{4,6},{6,0},{1,3},{3,5},{5,7},{7,1},{8,10},{10,12},{12... | collective-permute-start | bytes 337928 | tf_op jit(solution)/shard_map/ppermute | solution.py:27
  487.9 30.0 %collective-permute-start.53 = (bf16[80,704]{1,0:T(8,128)(2,1)S(1)}, bf16[80,704]{1,0:T(8,128)(2,1)S(1)}, u32[]{:S(2)}, u32[]{:S(2)}) collective-permute-start(bf16[80,704]{1,0:T(8,128)(2,1)S(1)} %get-tuple-element.93), channel_id=1, source_target_pairs={{0,4},{2,6},{4,0},{6,2},{1,5},{3,7},{5,1},{7,3},{8,12},{10,14},{12... | collective-permute-start | bytes 337928 | tf_op jit(solution)/shard_map/ppermute | solution.py:27
  494.7 23.2 %collective-permute-start.52 = (bf16[80,704]{1,0:T(8,128)(2,1)S(1)}, bf16[80,704]{1,0:T(8,128)(2,1)S(1)}, u32[]{:S(2)}, u32[]{:S(2)}) collective-permute-start(bf16[80,704]{1,0:T(8,128)(2,1)S(1)} %get-tuple-element.94), channel_id=1, source_target_pairs={{0,6},{2,0},{4,2},{6,4},{1,7},{3,1},{5,3},{7,5},{8,14},{10,8},{12,... | collective-permute-start | bytes 337928 | tf_op jit(solution)/shard_map/ppermute | solution.py:27
  508.8 51.3 %collective-permute-start.57 = (bf16[80,704]{1,0:T(8,128)(2,1)S(1)}, bf16[80,704]{1,0:T(8,128)(2,1)S(1)}, u32[]{:S(2)}, u32[]{:S(2)}) collective-permute-start(bf16[80,704]{1,0:T(8,128)(2,1)S(1)} %get-tuple-element.95), channel_id=1, source_target_pairs={{0,8},{8,16},{16,24},{24,0},{1,9},{9,17},{17,25},{25,1},{2,10},{10... | collective-permute-start | bytes 337928 | tf_op jit(solution)/shard_map/ppermute | solution.py:27
  510.9 50.2 %collective-permute-start.59 = (bf16[80,704]{1,0:T(8,128)(2,1)S(1)}, bf16[80,704]{1,0:T(8,128)(2,1)S(1)}, u32[]{:S(2)}, u32[]{:S(2)}) collective-permute-start(bf16[80,704]{1,0:T(8,128)(2,1)S(1)} %get-tuple-element.96), channel_id=1, source_target_pairs={{0,16},{8,24},{16,0},{24,8},{1,17},{9,25},{17,1},{25,9},{2,18},{10... | collective-permute-start | bytes 337928 | tf_op jit(solution)/shard_map/ppermute | solution.py:27
  517.9 21.2 %collective-permute-start.44 = (bf16[80,2560]{1,0:T(8,128)(2,1)S(1)}, bf16[80,2560]{1,0:T(8,128)(2,1)S(1)}, u32[]{:S(2)}, u32[]{:S(2)}) collective-permute-start(bf16[80,2560]{1,0:T(8,128)(2,1)S(1)} %get-tuple-element.73.refs_1_), channel_id=1, source_target_pairs={{0,32},{32,64},{64,96},{96,0},{1,33},{33,65},{65,97},{97,1},{2,34}... | collective-permute-start | bytes 1228808 | tf_op jit(solution)/shard_map/ppermute | solution.py:27
  526.3 22.6 %collective-permute-start.42 = (bf16[80,2560]{1,0:T(8,128)(2,1)S(1)}, bf16[80,2560]{1,0:T(8,128)(2,1)S(1)}, u32[]{:S(2)}, u32[]{:S(2)}) collective-permute-start(bf16[80,2560]{1,0:T(8,128)(2,1)S(1)} %get-tuple-element.69), channel_id=1, source_target_pairs={{0,64},{32,96},{64,0},{96,32},{1,65},{33,97},{65,1},{97,33},{2,66}... | collective-permute-start | bytes 1228808 | tf_op jit(solution)/shard_map/ppermute | solution.py:27
  (119 other events, 1350.9 us)
Sparse Core Ops, SparseCore 0:
  10.9 114.4 all-gather.2
  127.6 109.6 all-gather.4
  333.6 116.2 reduce-scatter.1

commit v5 on v4

--- a/solution.py
+++ b/solution.py
@@ -15,6 +15,7 @@
 Y, X, Z, T = "shard", "context_0", "context_1", "tensor"
 VMEM = pltpu.CompilerParams(vmem_limit_bytes=48 * 2**20)
 ANYWHERE = pl.BlockSpec(memory_space=pl.ANY)
+FREE = pl.CostEstimate(flops=0, bytes_accessed=0, transcendentals=0)
 
 EPSILON = 1e-06
 NEGATIVE_FILL = -1e30
@@ -43,6 +44,7 @@
         out_specs=ANYWHERE,
         input_output_aliases={0: 0},
         compiler_params=VMEM,
+        cost_estimate=FREE,
     )(x, *others)
 
 
@@ -70,6 +72,7 @@
         in_specs=[whole] * 4 + [ANYWHERE] * len(first),
         out_specs=whole,
         compiler_params=VMEM,
+        cost_estimate=FREE,
     )(*blocks, *first)
 
 
@@ -99,63 +102,63 @@
         + [ANYWHERE] * len(first),
         out_specs=(pl.BlockSpec((320, rows), lambda i: (0, i)),) * 2,
         compiler_params=VMEM,
+        cost_estimate=FREE,
     )(*lefts, *[weight] * count, *first)
 
 
-def scatter_parts(lefts, weight, at, width, *first):
-    far, near = row_products(lefts, weight, at, width, *first)
+def core_sum(far, near):
     return (near.astype(F32) + shift(far, T, 1).astype(F32)).astype(BF).reshape(4, 80, -1)
 
 
-def scatter_blocks(low):
-    me = lax.axis_index(Y)
-    return [lax.dynamic_index_in_dim(low, (me + r) % 4, 0, keepdims=False) for r in range(4)]
-
-
-def scatter_sum(blocks):
-    return scatter_total(blocks[0], [shift(blocks[r], Y, r) for r in (1, 3, 2)])
-
-
-def scatter_total(own, got):
-    total = own.astype(F32)
-    for block in got:
-        total = total + block.astype(F32)
-    return total
-
-
-def outer_kernel(x_ref, g_ref, y_ref, h_ref, out_ref):
-    split = g_ref.shape[1]
-    out_ref[:, :split] = dot(x_ref[...], g_ref[...], 0, 0).astype(BF)
-    out_ref[:, split:] = dot(y_ref[...], h_ref[...], 0, 0).astype(BF)
-
-
-def outer(x, g, y, h):
-    rows, n, cols = 512, x.shape[1], g.shape[1] + h.shape[1]
-    left = pl.BlockSpec((640, rows), lambda i: (0, i))
-    right = [pl.BlockSpec((640, a.shape[1]), lambda i: (0, 0)) for a in (g, h)]
-    return pl.pallas_call(
-        outer_kernel,
-        grid=(n // rows,),
-        out_shape=jax.ShapeDtypeStruct((n, cols), BF),
-        in_specs=[left, right[0], left, right[1]],
-        out_specs=pl.BlockSpec((rows, cols), lambda i: (i, 0)),
-        compiler_params=VMEM,
-    )(x, g, y, h)
-
-
-def summed_over(parts, axis, dim):
+def own_and_received(parts, axis, dim):
     me = lax.axis_index(axis)
     own, *rest = [
         lax.dynamic_index_in_dim(parts, (me + r) % 4, dim, keepdims=False) for r in range(4)
     ]
-    return scatter_total(own, [shift(rest[r - 1], axis, r) for r in (1, 3, 2)]).astype(BF)
-
-
-def scatter_context(parts):
-    grid = parts.reshape(4, 4, 160, -1)
-    one = summed_over(grid[:, :, :80], X, 0)
-    two = summed_over(grid[:, :, 80:], Z, 1)
-    return jnp.concatenate([summed_over(one, Z, 0), summed_over(two, X, 0)])
+    return [own] + [shift(rest[r - 1], axis, r) for r in (1, 3, 2)]
+
+
+def sums_kernel(kinds, *refs):
+    for i, out in enumerate(refs[4 * len(kinds) :]):
+        total = refs[4 * i][...].astype(F32)
+        for ref in refs[4 * i + 1 : 4 * i + 4]:
+            total = total + ref[...].astype(F32)
+        out[...] = total.astype(kinds[i])
+
+
+def sums(groups, kinds):
+    return pl.pallas_call(
+        functools.partial(sums_kernel, kinds),
+        out_shape=tuple(jax.ShapeDtypeStruct(g[0].shape, k) for g, k in zip(groups, kinds)),
+        compiler_params=VMEM,
+        cost_estimate=FREE,
+    )(*[block for group in groups for block in group])
+
+
+def outer_kernel(x_ref, g_ref, y_ref, h_ref, one_ref, two_ref):
+    split = g_ref.shape[1]
+    for left, right, columns in (
+        (x_ref, g_ref, slice(0, split)),
+        (y_ref, h_ref, slice(split, split + h_ref.shape[1])),
+    ):
+        part = dot(left[...], right[...], 0, 0).astype(BF).reshape(4, 160, right.shape[1])
+        one_ref[0, :, :, columns] = part[:, :80]
+        two_ref[0, :, :, columns] = part[:, 80:]
+
+
+def outer(x, g, y, h):
+    rows, cols = 640, g.shape[1] + h.shape[1]
+    left = pl.BlockSpec((640, rows), lambda i: (0, i))
+    right = [pl.BlockSpec((640, a.shape[1]), lambda i: (0, 0)) for a in (g, h)]
+    return pl.pallas_call(
+        outer_kernel,
+        grid=(4,),
+        out_shape=(jax.ShapeDtypeStruct((4, 4, 80, cols), BF),) * 2,
+        in_specs=[left, right[0], left, right[1]],
+        out_specs=(pl.BlockSpec((1, 4, 80, cols), lambda i: (i, 0, 0, 0)),) * 2,
+        compiler_params=VMEM,
+        cost_estimate=FREE,
+    )(x, g, y, h)
 
 
 def to_owners(sums):
@@ -173,14 +176,14 @@
     return blocks.reshape(4, 2, 80, cols).swapaxes(0, 1).reshape(640, cols)
 
 
-def columns_out(x):
+def columns_out(x, *first):
     me = lax.axis_index(Y)
     blocks = quarters(x)
     got = []
     for r in range(4):
         block = lax.dynamic_index_in_dim(blocks, (me + r) % 4, 0, keepdims=False)
         got.append(shift(block, Y, r) if r else block)
-    return by_half(place(got, Y, sign=-1))
+    return by_half(place(got, Y, *first, sign=-1))
 
 
 def quarters(x):
@@ -207,6 +210,7 @@
         out_shape=jax.ShapeDtypeStruct((4, 48, 384), BF),
         in_specs=[whole, whole, whole, ANYWHERE],
         compiler_params=VMEM,
+        cost_estimate=FREE,
     )(w_query, keyval_half, gains, first)
 
 
@@ -223,6 +227,7 @@
         pack_mlp_kernel,
         out_shape=jax.ShapeDtypeStruct((4, 40, 3072), BF),
         compiler_params=VMEM,
+        cost_estimate=FREE,
     )(w_gate, w_up, w_down)
 
 
@@ -260,6 +265,7 @@
         + [ANYWHERE] * len(first),
         out_specs=pl.BlockSpec((rows, 1024), lambda j, i: (i, j)),
         compiler_params=VMEM,
+        cost_estimate=FREE,
     )(normed, grads, gate, up, hidden, *first)
 
 
@@ -292,6 +298,7 @@
         + [pl.BlockSpec((2560, cols), lambda j, k=k: (0, k * steps + j)) for k in range(3)],
         out_specs=(out, out, out),
         compiler_params=VMEM,
+        cost_estimate=FREE,
     )(x, y, w_mlp, w_mlp, w_mlp)
 
 
@@ -375,62 +382,53 @@
             pl.BlockSpec((1, 80, 384), lambda i: (i % 4, i // 4, 0)),
         ),
         compiler_params=VMEM,
+        cost_estimate=FREE,
     )(own, other, gain, weight)
 
 
-def owned_kernel(b0, b1, b2, b3, query_ref, keyval_ref, *rest):
-    query_out, keyval_out, output_out, gain_out, held = rest[-5:]
+def owners_kernel(*refs):
+    home, mlp = refs[:4], refs[4:8]
+    query_ref, keyval_ref, gate_ref, up_ref, block_mine, block_other, rows_mine, rows_other = refs[8:16]
+    query_out, keyval_out, output_out, gate_out, up_out, down_out, gain_out, block_out, rows_out = refs[16:25]
+    held, held_mlp = refs[25:]
     me = lax.axis_index(Y)
-    for r, block in enumerate((b0, b1, b2, b3)):
-        held[lax.rem(me + 4 - r, 4)] = block[...]
+    for r in range(4):
+        held[lax.rem(me + 4 - r, 4)] = home[r][...]
+        held_mlp[lax.rem(me + 4 - r, 4)] = mlp[r][...]
     for j in range(4):
+        columns = slice(960 * j, 960 * j + 960)
+        gate_out[:, columns] = held_mlp[j, :, :960].astype(F32)
+        up_out[:, columns] = held_mlp[j, :, 1024:1984].astype(F32)
+        down_out[:, columns] = held_mlp[j, :, 2048:3008].astype(F32)
         total = held[j].astype(F32)
         query_out[:, 320 * j : 320 * j + 320] = total[:, :320]
         keyval_out[:, 64 * j : 64 * j + 64] = total[:, 320:384]
         output_out[:, 320 * j : 320 * j + 320] = total[:, 384:]
-    gain = jnp.zeros((40, 1), F32)
-    for weight, grad in ((query_ref, query_out), (keyval_ref, keyval_out)):
-        gain += jnp.sum(weight[...].astype(F32) * grad[...], axis=1, keepdims=True)
-    gain_out[...] = jnp.broadcast_to(gain, (40, 128))
-
-
-def owned(blocks, w_query, keyval_half, *first):
-    whole = pl.BlockSpec(memory_space=pltpu.VMEM)
-    return pl.pallas_call(
-        owned_kernel,
-        in_specs=[whole] * 6 + [ANYWHERE] * len(first),
-        out_shape=(
-            jax.ShapeDtypeStruct((40, 1280), F32),
-            jax.ShapeDtypeStruct((40, 256), F32),
-            jax.ShapeDtypeStruct((40, 1280), F32),
-            jax.ShapeDtypeStruct((40, 128), F32),
-        ),
-        scratch_shapes=[pltpu.VMEM((4, 40, 704), BF)],
-        compiler_params=VMEM,
-    )(*blocks, w_query, keyval_half, *first)
-
-
-def owned_mlp_kernel(b0, b1, b2, b3, gate_ref, up_ref, gate_out, up_out, down_out, gain_out, held):
-    me = lax.axis_index(Y)
-    for r, block in enumerate((b0, b1, b2, b3)):
-        held[lax.rem(me + 4 - r, 4)] = block[...]
-    for j in range(4):
-        columns = slice(960 * j, 960 * j + 960)
-        gate_out[:, columns] = held[j, :, :960].astype(F32)
-        up_out[:, columns] = held[j, :, 1024:1984].astype(F32)
-        down_out[:, columns] = held[j, :, 2048:3008].astype(F32)
-    products = gate_ref[...].astype(F32) * gate_out[...] + up_ref[...].astype(F32) * up_out[...]
-    gain_out[...] = jnp.broadcast_to(jnp.sum(products, axis=1, keepdims=True), (40, 128))
-
-
-def owned_mlp(blocks, w_gate, w_up):
-    wide = jax.ShapeDtypeStruct((40, 3840), F32)
-    return pl.pallas_call(
-        owned_mlp_kernel,
-        out_shape=(wide, wide, wide, jax.ShapeDtypeStruct((40, 128), F32)),
-        scratch_shapes=[pltpu.VMEM((4, 40, 3072), BF)],
-        compiler_params=VMEM,
-    )(*blocks, w_gate, w_up)
+
+    def products(weight, grad):
+        return jnp.sum(weight[...].astype(F32) * grad[...], axis=1, keepdims=True)
+
+    one = products(query_ref, query_out) + products(keyval_ref, keyval_out)
+    two = products(gate_ref, gate_out) + products(up_ref, up_out)
+    gain_out[:, :128] = jnp.broadcast_to(one, (40, 128))
+    gain_out[:, 128:] = jnp.broadcast_to(two, (40, 128))
+    at = 80 * lax.axis_index(T)
+    for mine, other, out in ((block_mine, block_other, block_out), (rows_mine, rows_other, rows_out)):
+        out[pl.ds(pl.multiple_of(at, 16), 80), :] = mine[...]
+        out[pl.ds(pl.multiple_of(80 - at, 16), 80), :] = other[...]
+
+
+def owners(home, mlp, w_query, keyval_half, w_gate, w_up, block, rows):
+    wide, narrow = (jax.ShapeDtypeStruct((40, n), F32) for n in (3840, 1280))
+    small = jax.ShapeDtypeStruct((40, 256), F32)
+    tokens = jax.ShapeDtypeStruct((160, 2560), BF)
+    return pl.pallas_call(
+        owners_kernel,
+        out_shape=(narrow, small, narrow, wide, wide, wide, small, tokens, tokens),
+        scratch_shapes=[pltpu.VMEM((4, 40, 704), BF), pltpu.VMEM((4, 40, 3072), BF)],
+        compiler_params=VMEM,
+        cost_estimate=FREE,
+    )(*home, *mlp, w_query, keyval_half, w_gate, w_up, *block, *rows)
 
 
 def token_order_kernel(x_ref, out_ref):
@@ -442,22 +440,8 @@
 
 def from_piece_order(x):
     return pl.pallas_call(
-        token_order_kernel, out_shape=jax.ShapeDtypeStruct(x.shape, BF), compiler_params=VMEM
+        token_order_kernel, out_shape=jax.ShapeDtypeStruct(x.shape, BF), compiler_params=VMEM, cost_estimate=FREE
     )(x)
-
-
-def halves_kernel(mine_ref, other_ref, out_ref):
-    at = 80 * lax.axis_index(T)
-    out_ref[pl.ds(pl.multiple_of(at, 16), 80), :] = mine_ref[...]
-    out_ref[pl.ds(pl.multiple_of(80 - at, 16), 80), :] = other_ref[...]
-
-
-def halves_home(mine):
-    return pl.pallas_call(
-        halves_kernel,
-        out_shape=jax.ShapeDtypeStruct((160, mine.shape[1]), BF),
-        compiler_params=VMEM,
-    )(mine, shift(mine, T, 1))
 
 
 def shards(
@@ -486,7 +470,8 @@
     live_turned = turned >= padding
     live_mine = live_turned[:80, None]
 
-    w_out = lax.all_gather(w_output, PIECES, axis=0, tiled=True)
+    out_rows = place(ring_blocks(w_output, Y), Y).reshape(160, 1280)
+    w_out = lax.all_gather(out_rows, CONTEXT, axis=0, tiled=True)
 
     x_low = to_piece_order(lax.dynamic_slice_in_dim(tokens[0], t * 80, 80, 0))
     cot_mine = to_piece_order(lax.dynamic_slice_in_dim(cotangent[0], t * 80, 80, 0))
@@ -508,7 +493,6 @@
     w_mlp = lax.all_gather(mlp_block, CONTEXT, axis=0, tiled=True)
 
     normed, projected = project(x_own, x_other, gain_one, w_qkv)
-    grad_own, grad_other = gather_rows(after(grad_mine, projected))
     home = exchange(projected, Y)
     keyval_turned = joined(home[:, :, 320:])
     keyval_own = jnp.where(
@@ -518,6 +502,7 @@
     keys_own = rotate(keyval_own[:, None].astype(F32), cosine_nat, sine_nat)[:, 0].astype(BF)
     kv_own = jnp.where(t == 0, keys_own, keyval_own)
     kv_mine = exchange(jnp.broadcast_to(kv_own[None], (16, 160, 256)), CONTEXT).reshape(2560, 256)
+    grad_own, grad_other = gather_rows(after(grad_mine, kv_own), kv_mine)
     grad_group = jnp.concatenate([grad_own, grad_other])
     kv_other = shift(kv_mine, T, 1)
     keys = jnp.where(t == 0, kv_mine, kv_other)
@@ -547,18 +532,15 @@
     normed_two_mine = (hidden_mine * inverse_two * gain_two).astype(BF)
     normed_two = jnp.concatenate(gather_rows(after(normed_two_mine, grad_group)))
     hidden, grad_gate, grad_up = feed_forward(normed_two, grad_group, w_mlp)
-    normed_two_low = scatter_parts((grad_gate, grad_up), w_mlp, 0, 1024)
-
-    normed_two_blocks = scatter_blocks(normed_two_low)
-    got = [shift(normed_two_blocks[r], Y, r) for r in (1, 3, 2)]
-    trip = small_trip(normed_two_low, *normed_two_blocks[1:])
-    mlp_low = scatter_parts((hidden,), w_mlp, 2, 1024, trip)
-    attended_group = columns_out(attended)
+    normed_two_low = core_sum(*row_products((grad_gate, grad_up), w_mlp, 0, 1024))
+    got = own_and_received(normed_two_low, Y, 0)
+
+    mlp_rows = row_products((hidden,), w_mlp, 2, 1024, normed_two_low)
     mlp_part = mlp_grads(
-        normed_two, grad_group, grad_gate, grad_up, hidden, *got[:2], mlp_low, attended_group
+        normed_two, grad_group, grad_gate, grad_up, hidden, *got, *mlp_rows
     )
     mlp_sum = lax.psum_scatter(mlp_part, CONTEXT, scatter_dimension=0, tiled=True)
-    grad_normed_two = scatter_total(after(normed_two_blocks[0], mlp_part), got)
+    grad_normed_two = sum(block.astype(F32) for block in got)
 
     grad_h_mine = grad_mine.astype(F32) + norm_back(
         grad_normed_two, hidden_mine, inverse_two, gain_two
@@ -566,8 +548,6 @@
     branch_mine = grad_h_mine.astype(BF)
     branch_low = jnp.concatenate([branch_mine, shift(branch_mine, T, 1)])
     grad_attended = dot(branch_low, w_out, 1, 0).astype(BF).reshape(160, 5, head_dim)
-    branch_own, branch_other = gather_rows(branch_mine)
-    branch_group = jnp.concatenate([branch_own, branch_other])
 
     grad_prob = jnp.einsum("qhd,kd->hqk", grad_attended, values, preferred_element_type=F32)
     spread = jnp.sum(prob * grad_prob, axis=-1, keepdims=True)
@@ -582,34 +562,54 @@
     )
     kv_part = (keep + shift(give, T, 1).astype(F32)).astype(BF).reshape(16, 160, 256)
     kv_part = after(kv_part, grad_query_pre)
-    kv_home = after(exchange(kv_part, CONTEXT), branch_group)
+    kv_home = exchange(kv_part, CONTEXT)
+    branch_group = jnp.concatenate(gather_rows(branch_mine, kv_home))
+    attended_group = columns_out(attended, kv_home)
     kv_sum = jnp.sum(kv_home.astype(F32), axis=0)
-    grad_query_group = columns_out(grad_query_pre)
+    grad_query_group = columns_out(grad_query_pre, kv_home)
 
     keys_back = rotate(kv_sum[:, None], cosine_nat, -sine_nat)[:, 0]
     kv_back = jnp.where(t == 0, keys_back, kv_sum).astype(BF)
     kv_back = jnp.where(t == 0, kv_back, jnp.concatenate([kv_back[80:], kv_back[:80]]))
     grad_kv_group = columns_out(kv_back)
     grad_qkv = jnp.concatenate([grad_query_group, grad_kv_group], axis=1)
-    normed_low = scatter_parts((grad_qkv,), w_qkv, 0, 384)
-    normed_blocks = scatter_blocks(normed_low)
-    part = outer(normed, grad_qkv, branch_group, attended_group)
-    home = to_owners(scatter_context(part))
-
-    mlp_mine = scatter_sum(scatter_blocks(after(mlp_low, *normed_blocks[1:])))
-    block_mine = jnp.where(live_mine, hidden_mine + mlp_mine, 0.0)
-
-    grad_normed = scatter_sum(normed_blocks)
+    normed_low = core_sum(*row_products((grad_qkv,), w_qkv, 0, 384))
+    first_half, last_half = outer(normed, grad_qkv, branch_group, attended_group)
+    one, two, grad_normed = sums(
+        (
+            own_and_received(first_half, X, 0),
+            own_and_received(last_half, Z, 1),
+            own_and_received(normed_low, Y, 0),
+        ),
+        (BF, BF, F32),
+    )
+    mlp_low = core_sum(*mlp_rows)
+    one, two, mlp_mine = sums(
+        (
+            own_and_received(one, Z, 0),
+            own_and_received(two, X, 0),
+            own_and_received(after(mlp_low, one), Y, 0),
+        ),
+        (BF, BF, F32),
+    )
+    home = to_owners(jnp.concatenate([one, two]))
+    block_mine = from_piece_order(jnp.where(live_mine, hidden_mine + mlp_mine, 0.0))
     inverse_one = inverse_root(x_mine)
-    tokens_mine = grad_h_mine + norm_back(grad_normed, x_mine, inverse_one, gain_one)
-    gate_grad, up_grad, down_grad, two_part = owned_mlp(to_owners(mlp_sum), w_gate, w_up)
-    block_out = halves_home(from_piece_order(block_mine))
-    tokens_grad = halves_home(from_piece_order(tokens_mine))
-
-    query_grad, kv_half, output_grad, one_part = owned(
-        home, w_query, keyval_half, two_part, block_out, tokens_grad
-    )
-    mine = jnp.concatenate([kv_half, one_part, two_part], axis=1)
+    tokens_mine = from_piece_order(
+        grad_h_mine + norm_back(grad_normed, x_mine, inverse_one, gain_one)
+    )
+    query_grad, kv_half, output_grad, gate_grad, up_grad, down_grad, gain_part, block_out, tokens_grad = owners(
+        home,
+        to_owners(mlp_sum),
+        w_query,
+        keyval_half,
+        w_gate,
+        w_up,
+        (block_mine, shift(block_mine, T, 1)),
+        (tokens_mine, shift(tokens_mine, T, 1)),
+    )
+
+    mine = jnp.concatenate([kv_half, gain_part], axis=1)
     other = shift(mine, T, 1)
     kv_other = other[:, :256]
     keyval_grad = jnp.where(

time: 601 us -> 561 us (0.933)
  the two profiles are of different devices: /device:TPU:35 before, /device:TPU:1 now
where the time goes in v5:
time: 561 us; the launch traced here: 550 us
  waiting for transfers between devices  185 us (33%)
  starting transfers between devices  139 us (25%)
  Pallas kernels  93.1 us (17%)
  local copies, waits for them, and re-layouts  50 us (9%)
  other arithmetic  33.9 us (6%)
  matrix products  31.9 us (6%)
  between operations  16.5 us (3%)
    ppermute x69, waiting for transfers between devices, shift(): return lax.ppermute(x, axis, [(i, (i + by) % n) for i in range(n)])  148 us
    ppermute x69, starting transfers between devices, shift(): return lax.ppermute(x, axis, [(i, (i + by) % n) for i in range(n)])  112 us
    all_to_all x4, waiting for transfers between devices, exchange(): return lax.all_to_all(blocks, axis, 0, 0, tiled=True)  37 us
    all_to_all x4, starting transfers between devices, exchange(): return lax.all_to_all(blocks, axis, 0, 0, tiled=True)  27.3 us
    pallas_call x3, Pallas kernels, row_products(): pl.pallas_call(functools.partial(rows_kernel, count), grid=(n // rows,),...  27.1 us
    pallas_call x1, Pallas kernels, mlp_grads(): pl.pallas_call(mlp_grad_kernel, grid=(3, 2560 // rows), out_shape=jax.Sha...  20.8 us
    unnamed x151, local copies, waits for them, and re-layouts  16.4 us
    pallas_call x1, Pallas kernels, feed_forward(): pl.pallas_call(feed_forward_kernel, grid=(steps,), out_shape=(part, part,...  16 us
  transfers between devices with their start and end apart: 76, of which 33 were waited for; matrix products, arithmetic and copies ran while one was open for 18% of the time, Pallas kernels for 8%

profile of v5, /device:TPU:1, one launch (start us, length us, event | category | flops | bytes accessed | tf_op | source)
XLA Modules:
  0.0 550.0 jit_solution(5094338665573202704)
XLA Ops:
  26.8 9.5 %all-to-all-start = ((bf16[64,48,384]{2,1,0:T(8,128)(2,1)}), bf16[64,48,384]{2,1,0:T(8,128)(2,1)S(1)}, u32[]{:S(2)}, u32[]{:S(2)}) async-start(bf16[64,48,384]{2,1,0:T(8,128)(2,1)} %bitcast.279), calls=%async_computation | async-start | bytes 4718592 | tf_op jit(solution)/shard_map/all_to_all | solution.py:32
  45.1 27.8 %collective-permute-done.2.refs_3_ = bf16[80,2560]{1,0:T(8,128)(2,1)} collective-permute-done((bf16[80,2560]{1,0:T(8,128)(2,1)S(1)}, bf16[80,2560]{1,0:T(8,128)(2,1)}, u32[]{:S(2)}, u32[]{:S(2)}) %collective-permute-start.2) | collective-permute-done | bytes 409632 | tf_op jit(solution)/shard_map/ppermute | solution.py:28
  72.9 8.8 %collective-permute-done.1.refs_2_ = bf16[80,2560]{1,0:T(8,128)(2,1)} collective-permute-done((bf16[80,2560]{1,0:T(8,128)(2,1)S(1)}, bf16[80,2560]{1,0:T(8,128)(2,1)}, u32[]{:S(2)}, u32[]{:S(2)}) %collective-permute-start.1) | collective-permute-done | bytes 409632 | tf_op jit(solution)/shard_map/ppermute | solution.py:28
  86.9 6.3 %collective-permute-done.18.refs_1_ = bf16[40,3072]{1,0:T(8,128)(2,1)} collective-permute-done((bf16[40,3072]{1,0:T(8,128)(2,1)}, bf16[40,3072]{1,0:T(8,128)(2,1)}, u32[]{:S(2)}, u32[]{:S(2)}) %collective-permute-start.18) | collective-permute-done | bytes 245792 | tf_op jit(solution)/shard_map/ppermute | solution.py:28
  100.5 8.1 %shard_map.188 = (bf16[640,2560]{1,0:T(8,128)(2,1)}, bf16[4,160,384]{2,1,0:T(8,128)(2,1)}) custom-call(bf16[320,2560]{1,0:T(8,128)(2,1)S(1)} %bitcast.262, bf16[320,2560]{1,0:T(8,128)(2,1)} %collective-permute-done.4.other_ref, f32[1,2560]{1,0:T(1,128)S(1)} %reshape.623.gain_ref, bf16[2560,384]{1,0:T(8,128)(2,1)S(1)} %bitcast.255), custom_call_target="tpu_custom_call" | custom-call | tf_op jit(solution)/shard_map/pallas_call | solution.py:367
  113.4 7.4 %all-to-all-done.1 = bf16[4,160,384]{2,1,0:T(8,128)(2,1)S(1)} async-done(((bf16[4,160,384]{2,1,0:T(8,128)(2,1)}), bf16[4,160,384]{2,1,0:T(8,128)(2,1)S(1)}, u32[]{:S(2)}, u32[]{:S(2)}) %all-to-all-start.1) | async-done | bytes 491552 | tf_op jit(solution)/shard_map/all_to_all | solution.py:32
  123.7 10.6 %all-to-all-start.2 = ((bf16[16,160,256]{2,1,0:T(8,128)(2,1)}), bf16[16,160,256]{2,1,0:T(8,128)(2,1)}, u32[]{:S(2)}, u32[]{:S(2)}) async-start(bf16[16,160,256]{2,1,0:T(8,128)(2,1)} %broadcast_in_dim.109), calls=%async_computation.2 | async-start | bytes 2621440 | tf_op jit(solution)/shard_map/all_to_all | solution.py:32
  135.6 17.0 %all-to-all-done.2 = bf16[16,160,256]{2,1,0:T(8,128)(2,1)} async-done(((bf16[16,160,256]{2,1,0:T(8,128)(2,1)}), bf16[16,160,256]{2,1,0:T(8,128)(2,1)}, u32[]{:S(2)}, u32[]{:S(2)}) %all-to-all-start.2) | async-done | bytes 1310752 | tf_op jit(solution)/shard_map/all_to_all | solution.py:32
  152.6 4.0 collective-permute-start.5
  171.1 9.3 %collective-permute-done.11.refs_2_ = bf16[80,2560]{1,0:T(8,128)(2,1)S(1)} collective-permute-done((bf16[80,2560]{1,0:T(8,128)(2,1)S(1)}, bf16[80,2560]{1,0:T(8,128)(2,1)S(1)}, u32[]{:S(2)}, u32[]{:S(2)}) %collective-permute-start.11) | collective-permute-done | bytes 409632 | tf_op jit(solution)/shard_map/ppermute | solution.py:28
  188.2 4.5 fusion.28
  193.4 5.2 fusion.82
  209.6 7.3 %collective-permute-done.16.refs_3_ = bf16[80,2560]{1,0:T(8,128)(2,1)S(1)} collective-permute-done((bf16[80,2560]{1,0:T(8,128)(2,1)S(1)}, bf16[80,2560]{1,0:T(8,128)(2,1)S(1)}, u32[]{:S(2)}, u32[]{:S(2)}) %collective-permute-start.16) | collective-permute-done | bytes 409632 | tf_op jit(solution)/shard_map/ppermute | solution.py:28
  216.9 9.2 %collective-permute-done.15.refs_2_ = bf16[80,2560]{1,0:T(8,128)(2,1)S(1)} collective-permute-done((bf16[80,2560]{1,0:T(8,128)(2,1)S(1)}, bf16[80,2560]{1,0:T(8,128)(2,1)S(1)}, u32[]{:S(2)}, u32[]{:S(2)}) %collective-permute-start.15) | collective-permute-done | bytes 409632 | tf_op jit(solution)/shard_map/ppermute | solution.py:28
  232.5 16.0 %shard_map.196 = (bf16[640,1024]{1,0:T(8,128)(2,1)S(1)}, bf16[640,1024]{1,0:T(8,128)(2,1)S(1)}, bf16[640,1024]{1,0:T(8,128)(2,1)S(1)}) custom-call(bf16[640,2560]{1,0:T(8,128)(2,1)} %pad_maximum_fusion.1.x_ref, bf16[640,2560]{1,0:T(8,128)(2,1)} %copy-done.2, bf16[2560,3072]{1,0:T(8,128)(2,1)} %all-gather.5.cloned.1.call-done.gate_ref.up_ref.down_ref.refs_2_.refs_3_.refs_1_, ...), custom_call_target="tpu_custom_call" | custom-call | tf_op jit(solution)/shard_map/pallas_call | solution.py:293
  248.5 11.8 %shard_map.197 = (bf16[320,2560]{1,0:T(8,128)(2,1)S(1)}, bf16[320,2560]{1,0:T(8,128)(2,1)S(1)}) custom-call(bf16[640,1024]{1,0:T(8,128)(2,1)S(1)} %get-tuple-element.40.refs_0_.gate_ref, bf16[640,1024]{1,0:T(8,128)(2,1)S(1)} %get-tuple-element.41.refs_1_.up_ref, ...), custom_call_target="tpu_custom_call" | custom-call | tf_op jit(solution)/shard_map/pallas_call | solution.py:96
  269.2 9.7 %shard_map.206 = (bf16[320,2560]{1,0:T(8,128)(2,1)}, bf16[320,2560]{1,0:T(8,128)(2,1)S(1)}) custom-call(bf16[640,1024]{1,0:T(8,128)(2,1)S(1)} %get-tuple-element.50.refs_0_.hidden_ref, bf16[2560,3072]{1,0:T(8,128)(2,1)} %all-gather.5.cloned.1.call-done.gate_ref.up_ref.down_ref.refs_2_.refs_3_.refs_1_, bf16[4,80,2560]{2,1,0:T(8,128)(2,1)S(1)} %bitcast.258), custom_call_target="tpu_custom_call" | custom-call | tf_op jit(solution)/shard_map/pallas_call | solution.py:96
  278.9 7.1 %collective-permute-done.24.rest_3_ = bf16[80,2560]{1,0:T(8,128)(2,1)S(1)} collective-permute-done((bf16[80,2560]{1,0:T(8,128)(2,1)S(1)}, bf16[80,2560]{1,0:T(8,128)(2,1)S(1)}, u32[]{:S(2)}, u32[]{:S(2)}) %collective-permute-start.24) | collective-permute-done | bytes 409632 | tf_op jit(solution)/shard_map/ppermute | solution.py:28
  286.4 20.8 %shard_map.209 = bf16[2560,3072]{1,0:T(8,128)(2,1)} custom-call(bf16[640,2560]{1,0:T(8,128)(2,1)} %pad_maximum_fusion.1.x_ref, bf16[640,2560]{1,0:T(8,128)(2,1)} %copy-done.2, bf16[640,1024]{1,0:T(8,128)(2,1)S(1)} %get-tuple-element.40.refs_0_.gate_ref, bf16[640,1024]{1,0:T(8,128)(2,1)S(1)} %get-tuple-element.41.refs_1_.up_ref, ...), custom_call_target="tpu_custom_call" | custom-call | tf_op jit(solution)/shard_map/pallas_call | solution.py:254
  312.5 4.5 convolution_convert_fusion
  317.1 7.1 %fusion = (f32[5,160]{1,0:T(8,128)S(1)}, f32[2560,160,5]{0,1,2:T(8,128)S(1)}) fusion(f32[5,160]{1,0:T(8,128)S(1)} %broadcast_select_fusion.7, f32[5,160]{1,0:T(8,128)S(1)} %broadcast_select_fusion.8, f32[2560,160,5]{0,1,2:T(8,128)} %copy-done.32, pred[160,2560]{1,0:T(8,128)(4,1)S(1)} %copy-done.41, bf16[20,5,8,256]{3,2,1,0:T(8,128)(2,1)S(1)} %bitcast.315, ...), kind=kOutput, calls=%fused_computation.2 | convolution fusion | flops 1059470592 | bytes 19834240 | tf_op jit(solution)/shard_map/qhd,kd->hqk/dot_general | solution.py:552
  356.9 12.5 %all-to-all-done.3.refs_4_ = bf16[16,160,256]{2,1,0:T(8,128)(2,1)S(1)} async-done(((bf16[16,160,256]{2,1,0:T(8,128)(2,1)}), bf16[16,160,256]{2,1,0:T(8,128)(2,1)S(1)}, u32[]{:S(2)}, u32[]{:S(2)}) %all-to-all-start.3) | async-done | bytes 1310752 | tf_op jit(solution)/shard_map/all_to_all | solution.py:32
  387.7 5.7 %shard_map.204 = (bf16[320,2560]{1,0:T(8,128)(2,1)}, bf16[320,2560]{1,0:T(8,128)(2,1)S(1)}) custom-call(bf16[640,384]{1,0:T(8,128)(2,1)S(1)} %pad_maximum_fusion.3.g_ref.refs_0_, bf16[2560,384]{1,0:T(8,128)(2,1)S(1)} %bitcast.256), custom_call_target="tpu_custom_call" | custom-call | tf_op jit(solution)/shard_map/pallas_call | solution.py:96
  412.4 6.4 %shard_map.203 = (bf16[4,4,80,704]{3,2,1,0:T(8,128)(2,1)S(1)}, bf16[4,4,80,704]{3,2,1,0:T(8,128)(2,1)S(1)}) custom-call(bf16[640,2560]{1,0:T(8,128)(2,1)} %get-tuple-element.38.x_ref, bf16[640,384]{1,0:T(8,128)(2,1)S(1)} %copy-done.13, bf16[640,2560]{1,0:T(8,128)(2,1)} %pad_maximum_fusion.2.y_ref, bf16[640,320]{1,0:T(8,128)(2,1)S(1)} %bitcast.269), custom_call_target="tpu_custom_call" | custom-call | tf_op jit(solution)/shard_map/pallas_call | solution.py:153
  431.8 5.9 %collective-permute-start.41 = (bf16[4,80,704]{2,1,0:T(8,128)(2,1)S(1)}, bf16[4,80,704]{2,1,0:T(8,128)(2,1)S(1)}, u32[]{:S(2)}, u32[]{:S(2)}) collective-permute-start(bf16[4,80,704]{2,1,0:T(8,128)(2,1)S(1)} %copy-done.53), channel_id=1, source_target_pairs={{0,24},{8,0},{16,8},{24,16},{1,25},{9,1},{17,9},{25,17},{2,26},{10... | collective-permute-start | bytes 1351688 | tf_op jit(solution)/shard_map/ppermute | solution.py:28
  437.8 4.2 collective-permute-start.40
  441.9 4.1 collective-permute-done.48.refs_10_
  446.0 5.0 collective-permute-start.45
  454.4 6.9 %collective-permute-done.45.refs_7_ = bf16[4,80,704]{2,1,0:T(8,128)(2,1)S(1)} collective-permute-done((bf16[4,80,704]{2,1,0:T(8,128)(2,1)S(1)}, bf16[4,80,704]{2,1,0:T(8,128)(2,1)S(1)}, u32[]{:S(2)}, u32[]{:S(2)}) %collective-permute-start.45) | collective-permute-done | bytes 450592 | tf_op jit(solution)/shard_map/ppermute | solution.py:28
  461.3 11.5 %collective-permute-done.44.refs_6_ = bf16[4,80,704]{2,1,0:T(8,128)(2,1)S(1)} collective-permute-done((bf16[4,80,704]{2,1,0:T(8,128)(2,1)S(1)}, bf16[4,80,704]{2,1,0:T(8,128)(2,1)S(1)}, u32[]{:S(2)}, u32[]{:S(2)}) %collective-permute-start.44) | collective-permute-done | bytes 450592 | tf_op jit(solution)/shard_map/ppermute | solution.py:28
  495.5 11.0 %collective-permute-done.58.refs_10_ = bf16[80,2560]{1,0:T(8,128)(2,1)S(1)} collective-permute-done((bf16[80,2560]{1,0:T(8,128)(2,1)S(1)}, bf16[80,2560]{1,0:T(8,128)(2,1)S(1)}, u32[]{:S(2)}, u32[]{:S(2)}) %collective-permute-start.58) | collective-permute-done | bytes 409632 | tf_op jit(solution)/shard_map/ppermute | solution.py:28
  516.9 8.4 %collective-permute-done.62.refs_3_ = bf16[40,704]{1,0:T(8,128)(2,1)S(1)} collective-permute-done((bf16[40,704]{1,0:T(8,128)(2,1)S(1)}, bf16[40,704]{1,0:T(8,128)(2,1)S(1)}, u32[]{:S(2)}, u32[]{:S(2)}) %collective-permute-start.62) | collective-permute-done | bytes 56352 | tf_op jit(solution)/shard_map/ppermute | solution.py:28
  (429 shorter events, 239.9 us)
Async XLA Ops:
  7.2 186.2 %all-gather.3.cloned.1.call-start = ((), (), s32[]{:S(2)}) async-start(), calls=%async_computation.5 | async-start | bytes 6963200 | tf_op jit(solution)/shard_map/all_gather | solution.py:474
  26.8 55.0 %all-to-all-start = ((bf16[64,48,384]{2,1,0:T(8,128)(2,1)}), bf16[64,48,384]{2,1,0:T(8,128)(2,1)S(1)}, u32[]{:S(2)}, u32[]{:S(2)}) async-start(bf16[64,48,384]{2,1,0:T(8,128)(2,1)} %bitcast.279), calls=%async_computation | async-start | bytes 4718592 | tf_op jit(solution)/shard_map/all_to_all | solution.py:32
  36.2 196.3 %all-gather.5.cloned.1.call-start = ((), (), s32[]{:S(2)}) async-start(), calls=%async_computation.6 | async-start | bytes 16711680 | tf_op jit(solution)/shard_map/all_gather | solution.py:493
  36.3 36.6 %collective-permute-start.2 = (bf16[80,2560]{1,0:T(8,128)(2,1)S(1)}, bf16[80,2560]{1,0:T(8,128)(2,1)}, u32[]{:S(2)}, u32[]{:S(2)}) collective-permute-start(bf16[80,2560]{1,0:T(8,128)(2,1)S(1)} %copy.91.refs_0_), channel_id=1, source_target_pairs={{0,32},{32,64},{64,96},{96,0},{1,33},{33,65},{65,97},{97,1},{2,34}... | collective-permute-start | bytes 1228808 | tf_op jit(solution)/shard_map/ppermute | solution.py:28
  37.4 44.4 %collective-permute-start.1 = (bf16[80,2560]{1,0:T(8,128)(2,1)S(1)}, bf16[80,2560]{1,0:T(8,128)(2,1)}, u32[]{:S(2)}, u32[]{:S(2)}) collective-permute-start(bf16[80,2560]{1,0:T(8,128)(2,1)S(1)} %copy.91.refs_0_), channel_id=1, source_target_pairs={{0,64},{32,96},{64,0},{96,32},{1,65},{33,97},{65,1},{97,33},{2,66}... | collective-permute-start | bytes 1228808 | tf_op jit(solution)/shard_map/ppermute | solution.py:28
  39.8 42.0 %collective-permute-start = (bf16[80,2560]{1,0:T(8,128)(2,1)S(1)}, bf16[80,2560]{1,0:T(8,128)(2,1)}, u32[]{:S(2)}, u32[]{:S(2)}) collective-permute-start(bf16[80,2560]{1,0:T(8,128)(2,1)S(1)} %copy.91.refs_0_), channel_id=1, source_target_pairs={{0,96},{32,0},{64,32},{96,64},{1,97},{33,1},{65,33},{97,65},{2,98}... | collective-permute-start | bytes 1228808 | tf_op jit(solution)/shard_map/ppermute | solution.py:28
  43.0 42.9 %collective-permute-start.20 = (bf16[40,3072]{1,0:T(8,128)(2,1)}, bf16[40,3072]{1,0:T(8,128)(2,1)S(1)}, u32[]{:S(2)}, u32[]{:S(2)}) collective-permute-start(bf16[40,3072]{1,0:T(8,128)(2,1)} %get-tuple-element.109), channel_id=1, source_target_pairs={{0,96},{32,0},{64,32},{96,64},{1,97},{33,1},{65,33},{97,65},{2,98}... | collective-permute-start | bytes 737288 | tf_op jit(solution)/shard_map/ppermute | solution.py:28
  43.0 43.9 %collective-permute-start.19 = (bf16[40,3072]{1,0:T(8,128)(2,1)}, bf16[40,3072]{1,0:T(8,128)(2,1)S(1)}, u32[]{:S(2)}, u32[]{:S(2)}) collective-permute-start(bf16[40,3072]{1,0:T(8,128)(2,1)} %get-tuple-element.110), channel_id=1, source_target_pairs={{0,64},{32,96},{64,0},{96,32},{1,65},{33,97},{65,1},{97,33},{2,66}... | collective-permute-start | bytes 737288 | tf_op jit(solution)/shard_map/ppermute | solution.py:28
  123.7 28.9 %all-to-all-start.2 = ((bf16[16,160,256]{2,1,0:T(8,128)(2,1)}), bf16[16,160,256]{2,1,0:T(8,128)(2,1)}, u32[]{:S(2)}, u32[]{:S(2)}) async-start(bf16[16,160,256]{2,1,0:T(8,128)(2,1)} %broadcast_in_dim.109), calls=%async_computation.2 | async-start | bytes 2621440 | tf_op jit(solution)/shard_map/all_to_all | solution.py:32
  134.3 375.1 %reduce-scatter.2.cloned.1.call-start = ((), (), s32[]{:S(2)}) async-start(), calls=%async_computation.7 | async-start | bytes 16711680 | tf_op jit(solution)/shard_map/reduce_scatter | solution.py:542
  152.6 30.5 %collective-permute-start.5 = (bf16[2560,256]{1,0:T(8,128)(2,1)}, bf16[2560,256]{1,0:T(8,128)(2,1)}, u32[]{:S(2)}, u32[]{:S(2)}) collective-permute-start(bf16[2560,256]{1,0:T(8,128)(2,1)} %bitcast.16.refs_4_), channel_id=1, source_target_pairs={{0,1},{1,0},{2,3},{3,2},{4,5},{5,4},{6,7},{7,6},{8,9},{9,8},{10,11... | collective-permute-start | bytes 3932168 | tf_op jit(solution)/shard_map/ppermute | solution.py:28
  159.5 20.8 %collective-permute-start.11 = (bf16[80,2560]{1,0:T(8,128)(2,1)S(1)}, bf16[80,2560]{1,0:T(8,128)(2,1)S(1)}, u32[]{:S(2)}, u32[]{:S(2)}) collective-permute-start(bf16[80,2560]{1,0:T(8,128)(2,1)S(1)} %shard_map.190.refs_0_), channel_id=1, source_target_pairs={{0,64},{32,96},{64,0},{96,32},{1,65},{33,97},{65,1},{97,33},{2,66}... | collective-permute-start | bytes 1228808 | tf_op jit(solution)/shard_map/ppermute | solution.py:28
  205.7 20.4 %collective-permute-start.15 = (bf16[80,2560]{1,0:T(8,128)(2,1)S(1)}, bf16[80,2560]{1,0:T(8,128)(2,1)S(1)}, u32[]{:S(2)}, u32[]{:S(2)}) collective-permute-start(bf16[80,2560]{1,0:T(8,128)(2,1)S(1)} %shard_map.192.refs_0_), channel_id=1, source_target_pairs={{0,64},{32,96},{64,0},{96,32},{1,65},{33,97},{65,1},{97,33},{2,66}... | collective-permute-start | bytes 1228808 | tf_op jit(solution)/shard_map/ppermute | solution.py:28
  337.2 32.2 %all-to-all-start.3 = ((bf16[16,160,256]{2,1,0:T(8,128)(2,1)}), bf16[16,160,256]{2,1,0:T(8,128)(2,1)S(1)}, u32[]{:S(2)}, u32[]{:S(2)}) async-start(bf16[16,160,256]{2,1,0:T(8,128)(2,1)} %shard_map.198), calls=%async_computation.3 | async-start | bytes 2621440 | tf_op jit(solution)/shard_map/all_to_all | solution.py:32
  341.0 28.7 %collective-permute-start.35 = (bf16[80,2560]{1,0:T(8,128)(2,1)S(1)}, bf16[80,2560]{1,0:T(8,128)(2,1)S(1)}, u32[]{:S(2)}, u32[]{:S(2)}) collective-permute-start(bf16[80,2560]{1,0:T(8,128)(2,1)S(1)} %get-tuple-element.72.refs_0_), channel_id=1, source_target_pairs={{0,32},{32,64},{64,96},{96,0},{1,33},{33,65},{65,97},{97,1},{2,34}... | collective-permute-start | bytes 1228808 | tf_op jit(solution)/shard_map/ppermute | solution.py:28
  342.1 29.9 %collective-permute-start.34 = (bf16[80,2560]{1,0:T(8,128)(2,1)S(1)}, bf16[80,2560]{1,0:T(8,128)(2,1)S(1)}, u32[]{:S(2)}, u32[]{:S(2)}) collective-permute-start(bf16[80,2560]{1,0:T(8,128)(2,1)S(1)} %get-tuple-element.72.refs_0_), channel_id=1, source_target_pairs={{0,64},{32,96},{64,0},{96,32},{1,65},{33,97},{65,1},{97,33},{2,66}... | collective-permute-start | bytes 1228808 | tf_op jit(solution)/shard_map/ppermute | solution.py:28
  344.3 27.7 %collective-permute-start.33 = (bf16[80,2560]{1,0:T(8,128)(2,1)S(1)}, bf16[80,2560]{1,0:T(8,128)(2,1)S(1)}, u32[]{:S(2)}, u32[]{:S(2)}) collective-permute-start(bf16[80,2560]{1,0:T(8,128)(2,1)S(1)} %get-tuple-element.72.refs_0_), channel_id=1, source_target_pairs={{0,96},{32,0},{64,32},{96,64},{1,97},{33,1},{65,33},{97,65},{2,98}... | collective-permute-start | bytes 1228808 | tf_op jit(solution)/shard_map/ppermute | solution.py:28
  355.8 22.0 %collective-permute-start.26 = (bf16[160,320]{1,0:T(8,128)(2,1)}, bf16[160,320]{1,0:T(8,128)(2,1)S(1)}, u32[]{:S(2)}, u32[]{:S(2)}) collective-permute-start(bf16[160,320]{1,0:T(8,128)(2,1)} %bitcast.252), channel_id=1, source_target_pairs={{0,32},{32,64},{64,96},{96,0},{1,33},{33,65},{65,97},{97,1},{2,34}... | collective-permute-start | bytes 307208 | tf_op jit(solution)/shard_map/ppermute | solution.py:28
  356.1 23.4 %collective-permute-start.27 = (bf16[160,320]{1,0:T(8,128)(2,1)}, bf16[160,320]{1,0:T(8,128)(2,1)S(1)}, u32[]{:S(2)}, u32[]{:S(2)}) collective-permute-start(bf16[160,320]{1,0:T(8,128)(2,1)} %bitcast.251), channel_id=1, source_target_pairs={{0,64},{32,96},{64,0},{96,32},{1,65},{33,97},{65,1},{97,33},{2,66}... | collective-permute-start | bytes 307208 | tf_op jit(solution)/shard_map/ppermute | solution.py:28
  373.3 35.1 %collective-permute-start.36 = (bf16[320,2560]{1,0:T(8,128)(2,1)}, bf16[320,2560]{1,0:T(8,128)(2,1)}, u32[]{:S(2)}, u32[]{:S(2)}) collective-permute-start(bf16[320,2560]{1,0:T(8,128)(2,1)} %bitcast.59), channel_id=1, source_target_pairs={{0,1},{1,0},{2,3},{3,2},{4,5},{5,4},{6,7},{7,6},{8,9},{9,8},{10,11... | collective-permute-start | bytes 4915208 | tf_op jit(solution)/shard_map/ppermute | solution.py:28
  394.6 27.4 %collective-permute-start.46 = (bf16[320,2560]{1,0:T(8,128)(2,1)}, bf16[320,2560]{1,0:T(8,128)(2,1)}, u32[]{:S(2)}, u32[]{:S(2)}) collective-permute-start(bf16[320,2560]{1,0:T(8,128)(2,1)} %get-tuple-element.47), channel_id=1, source_target_pairs={{0,1},{1,0},{2,3},{3,2},{4,5},{5,4},{6,7},{7,6},{8,9},{9,8},{10,11... | collective-permute-start | bytes 4915208 | tf_op jit(solution)/shard_map/ppermute | solution.py:28
  405.2 26.7 %collective-permute-start.56 = (bf16[320,2560]{1,0:T(8,128)(2,1)}, bf16[320,2560]{1,0:T(8,128)(2,1)}, u32[]{:S(2)}, u32[]{:S(2)}) collective-permute-start(bf16[320,2560]{1,0:T(8,128)(2,1)} %get-tuple-element.52.rest_4_), channel_id=1, source_target_pairs={{0,1},{1,0},{2,3},{3,2},{4,5},{5,4},{6,7},{7,6},{8,9},{9,8},{10,11... | collective-permute-start | bytes 4915208 | tf_op jit(solution)/shard_map/ppermute | solution.py:28
  420.0 31.6 %collective-permute-start.42 = (bf16[4,80,704]{2,1,0:T(8,128)(2,1)}, bf16[4,80,704]{2,1,0:T(8,128)(2,1)S(1)}, u32[]{:S(2)}, u32[]{:S(2)}) collective-permute-start(bf16[4,80,704]{2,1,0:T(8,128)(2,1)} %get-tuple-element.84), channel_id=1, source_target_pairs={{0,16},{8,24},{16,0},{24,8},{1,17},{9,25},{17,1},{25,9},{2,18},{10... | collective-permute-start | bytes 1351688 | tf_op jit(solution)/shard_map/ppermute | solution.py:28
  429.0 22.0 %collective-permute-start.47 = (bf16[80,2560]{1,0:T(8,128)(2,1)}, bf16[80,2560]{1,0:T(8,128)(2,1)}, u32[]{:S(2)}, u32[]{:S(2)}) collective-permute-start(bf16[80,2560]{1,0:T(8,128)(2,1)} %get-tuple-element.94), channel_id=1, source_target_pairs={{0,32},{32,64},{64,96},{96,0},{1,33},{33,65},{65,97},{97,1},{2,34}... | collective-permute-start | bytes 1228808 | tf_op jit(solution)/shard_map/ppermute | solution.py:28
  431.8 22.6 %collective-permute-start.41 = (bf16[4,80,704]{2,1,0:T(8,128)(2,1)S(1)}, bf16[4,80,704]{2,1,0:T(8,128)(2,1)S(1)}, u32[]{:S(2)}, u32[]{:S(2)}) collective-permute-start(bf16[4,80,704]{2,1,0:T(8,128)(2,1)S(1)} %copy-done.53), channel_id=1, source_target_pairs={{0,24},{8,0},{16,8},{24,16},{1,25},{9,1},{17,9},{25,17},{2,26},{10... | collective-permute-start | bytes 1351688 | tf_op jit(solution)/shard_map/ppermute | solution.py:28
  451.0 21.8 %collective-permute-start.44 = (bf16[4,80,704]{2,1,0:T(8,128)(2,1)S(1)}, bf16[4,80,704]{2,1,0:T(8,128)(2,1)S(1)}, u32[]{:S(2)}, u32[]{:S(2)}) collective-permute-start(bf16[4,80,704]{2,1,0:T(8,128)(2,1)S(1)} %get-tuple-element.81), channel_id=1, source_target_pairs={{0,6},{2,0},{4,2},{6,4},{1,7},{3,1},{5,3},{7,5},{8,14},{10,8},{12,... | collective-permute-start | bytes 1351688 | tf_op jit(solution)/shard_map/ppermute | solution.py:28
  451.6 21.6 %collective-permute-start.43 = (bf16[4,80,704]{2,1,0:T(8,128)(2,1)S(1)}, bf16[4,80,704]{2,1,0:T(8,128)(2,1)S(1)}, u32[]{:S(2)}, u32[]{:S(2)}) collective-permute-start(bf16[4,80,704]{2,1,0:T(8,128)(2,1)S(1)} %get-tuple-element.82), channel_id=1, source_target_pairs={{0,2},{2,4},{4,6},{6,0},{1,3},{3,5},{5,7},{7,1},{8,10},{10,12},{12... | collective-permute-start | bytes 1351688 | tf_op jit(solution)/shard_map/ppermute | solution.py:28
  490.8 23.4 %collective-permute-start.67 = (bf16[80,2560]{1,0:T(8,128)(2,1)S(1)}, bf16[80,2560]{1,0:T(8,128)(2,1)S(1)}, u32[]{:S(2)}, u32[]{:S(2)}) collective-permute-start(bf16[80,2560]{1,0:T(8,128)(2,1)S(1)} %shard_map.211.refs_14_), channel_id=1, source_target_pairs={{0,1},{1,0},{2,3},{3,2},{4,5},{5,4},{6,7},{7,6},{8,9},{9,8},{10,11... | collective-permute-start | bytes 1228808 | tf_op jit(solution)/shard_map/ppermute | solution.py:28
  507.8 27.1 %collective-permute-start.66 = (bf16[80,2560]{1,0:T(8,128)(2,1)S(1)}, bf16[80,2560]{1,0:T(8,128)(2,1)S(1)}, u32[]{:S(2)}, u32[]{:S(2)}) collective-permute-start(bf16[80,2560]{1,0:T(8,128)(2,1)S(1)} %shard_map.210.refs_12_), channel_id=1, source_target_pairs={{0,1},{1,0},{2,3},{3,2},{4,5},{5,4},{6,7},{7,6},{8,9},{9,8},{10,11... | collective-permute-start | bytes 1228808 | tf_op jit(solution)/shard_map/ppermute | solution.py:28
  510.9 24.0 %collective-permute-start.65 = (bf16[40,3072]{1,0:T(8,128)(2,1)S(1)}, bf16[40,3072]{1,0:T(8,128)(2,1)S(1)}, u32[]{:S(2)}, u32[]{:S(2)}) collective-permute-start(bf16[40,3072]{1,0:T(8,128)(2,1)S(1)} %get-tuple-element.103), channel_id=1, source_target_pairs={{0,96},{32,0},{64,32},{96,64},{1,97},{33,1},{65,33},{97,65},{2,98}... | collective-permute-start | bytes 737288 | tf_op jit(solution)/shard_map/ppermute | solution.py:28
  513.3 21.6 %collective-permute-start.64 = (bf16[40,3072]{1,0:T(8,128)(2,1)S(1)}, bf16[40,3072]{1,0:T(8,128)(2,1)S(1)}, u32[]{:S(2)}, u32[]{:S(2)}) collective-permute-start(bf16[40,3072]{1,0:T(8,128)(2,1)S(1)} %get-tuple-element.104), channel_id=1, source_target_pairs={{0,64},{32,96},{64,0},{96,32},{1,65},{33,97},{65,1},{97,33},{2,66}... | collective-permute-start | bytes 737288 | tf_op jit(solution)/shard_map/ppermute | solution.py:28
  514.1 20.8 %collective-permute-start.63 = (bf16[40,3072]{1,0:T(8,128)(2,1)S(1)}, bf16[40,3072]{1,0:T(8,128)(2,1)S(1)}, u32[]{:S(2)}, u32[]{:S(2)}) collective-permute-start(bf16[40,3072]{1,0:T(8,128)(2,1)S(1)} %get-tuple-element.105), channel_id=1, source_target_pairs={{0,32},{32,64},{64,96},{96,0},{1,33},{33,65},{65,97},{97,1},{2,34}... | collective-permute-start | bytes 737288 | tf_op jit(solution)/shard_map/ppermute | solution.py:28
  (114 other events, 1542.6 us)
Sparse Core Ops, SparseCore 0:
  18.6 87.9 all-gather.2
  108.8 117.4 all-gather.4
  307.3 117.6 reduce-scatter.1
